TPU v7x, 32 devices: a whole 2x2x4 slice. The times are simulated.
32 devices in a mesh: replica: 4 (over x, core), shard: 8 (over z, y).
Axes of the slice: x: 2, y: 2, z: 4, core: 2. Of those that a mesh axis runs over, the one named last changes fastest.
Arguments:
- tokens: bfloat16 [32, 128, 1536], P(('replica', 'shard')), may hold values from -6 to 6
- segments: int32 [32, 128], P(('replica', 'shard')), may hold values from 0 to 3, never falling along the last dimension, each value on 1 to 64 neighbouring positions
- gain_attn: bfloat16 [1536], P('shard'), may hold values from 0.25 to 1.75
- w_qkv: bfloat16 [1536, 2048], P('shard'), may hold values from -0.15625 to 0.15625
- b_qkv: bfloat16 [2048], P('shard'), may hold values from -3 to 3
- w_out: bfloat16 [1536, 1536], P('shard'), may hold values from -0.625 to 0.625
- gain_ffn: bfloat16 [1536], P('shard'), may hold values from 0.25 to 1.75
- w_gate: bfloat16 [1536, 8960], P('shard'), may hold values from -0.15625 to 0.15625
- w_up: bfloat16 [1536, 8960], P('shard'), may hold values from -0.15625 to 0.15625
- w_down: bfloat16 [8960, 1536], P('shard'), may hold values from -0.0625 to 0.0625
- cotangent: bfloat16 [32, 128, 1536], P(('replica', 'shard')), may hold values from -6 to 6
Outputs:
- out: bfloat16 [32, 128, 1536], P(('replica', 'shard'))
- grad_tokens: bfloat16 [32, 128, 1536], P(('replica', 'shard'))
- grad_gain_attn: float32 [1536], P('shard')
- grad_w_qkv: float32 [1536, 2048], P('shard')
- grad_b_qkv: float32 [2048], P('shard')
- grad_w_out: float32 [1536, 1536], P('shard')
- grad_gain_ffn: float32 [1536], P('shard')
- grad_w_gate: float32 [1536, 8960], P('shard')
- grad_w_up: float32 [1536, 8960], P('shard')
- grad_w_down: float32 [8960, 1536], P('shard')
Inputs may be any that keep to these rules, and one draw needn't show every extreme that they name: `segments`: along each sequence the document numbers never fall; a document has 1 to 64 tokens, and one of each sequence has exactly 64.
All inputs are finite; a program needn't handle non-finite values.
Results may differ from a plain program's by a relative error of at most 0.018.
Values may be sent and summed in bfloat16 or wider, within the bound.
A program may use at most 448 MiB of HBM per device.

v0:
```python
import math

import jax
import jax.numpy as jnp
from jax import lax
from jax.sharding import PartitionSpec as P

QUERY_HEADS = 12
KEY_VALUE_HEADS = 2
HEAD_DIMENSION = 128


eps_norm = 1e-06
rope_base = 1000000.0


def tables(segment_ids, head_size):
    token_length = segment_ids.shape[-1]
    row_index = jnp.arange(token_length, dtype=jnp.int32)
    earlier = jnp.sum(
        (segment_ids[..., None, :] < segment_ids[..., :, None]).astype(jnp.int32),
        axis=-1,
        dtype=jnp.int32,
    )
    positions = (row_index - earlier).astype(jnp.float32)
    frequencies = jnp.exp(
        jnp.arange(head_size // 2, dtype=jnp.float32) * (-2.0 * math.log(rope_base) / head_size)
    )
    angles = positions[..., None] * frequencies
    cosine = jnp.concatenate([jnp.cos(angles), jnp.cos(angles)], axis=-1)
    sine_vals = jnp.concatenate([jnp.sin(angles), jnp.sin(angles)], axis=-1)
    allowed = (
        (segment_ids[..., None, :] == segment_ids[..., :, None])
        & (row_index[None, :] <= row_index[:, None])
    ).astype(jnp.int32)
    return (cosine, sine_vals, allowed)


def apply_rotation(values, cosine, sine_vals):
    halfway = values.shape[-1] // 2
    turned = jnp.concatenate([-values[..., halfway:], values[..., :halfway]], axis=-1)
    return values * cosine + turned * sine_vals


def rotate_back(values, cosine, sine_vals):
    halfway = values.shape[-1] // 2
    shifted = values * sine_vals
    return values * cosine + jnp.concatenate(
        [shifted[..., halfway:], -shifted[..., :halfway]], axis=-1
    )


def norm_forward(hidden, gain_vec):
    rstd_rows = lax.rsqrt(jnp.mean(hidden * hidden, axis=-1, keepdims=True) + eps_norm)
    unit_rows = hidden * rstd_rows
    return (unit_rows * gain_vec, unit_rows, rstd_rows)


def norm_backward(grad_in, gain_vec, unit_rows, rstd_rows):
    inner_grad = grad_in * gain_vec
    return rstd_rows * (
        inner_grad - unit_rows * jnp.mean(inner_grad * unit_rows, axis=-1, keepdims=True)
    )


def column_term(left_side, right_side):
    return jnp.einsum("lf,ld->fd", left_side, right_side, preferred_element_type=jnp.float32)


def shards(
    tokens, segments, gain_attn, w_qkv, b_qkv, w_out, gain_ffn, w_gate, w_up, w_down, cotangent
):
    heads_per_group = QUERY_HEADS // KEY_VALUE_HEADS
    head_dimension = QUERY_HEADS * HEAD_DIMENSION
    key_value_limit = head_dimension + KEY_VALUE_HEADS * HEAD_DIMENSION
    logit_scale = HEAD_DIMENSION ** (-0.5)
    token_length = tokens.shape[1]
    attn_set = (
        lax.all_gather(gain_attn, "shard", axis=0, tiled=True),
        lax.all_gather(w_qkv, "shard", axis=0, tiled=True),
        lax.all_gather(b_qkv, "shard", axis=0, tiled=True),
        lax.all_gather(w_out, "shard", axis=0, tiled=True),
        lax.all_gather(gain_ffn, "shard", axis=0, tiled=True),
    )
    full_gain_attn, full_qkv, full_bias, full_out, full_gain_ffn = attn_set
    full_gate, full_up, full_down = (
        lax.all_gather(w_gate, "shard", axis=0, tiled=True),
        lax.all_gather(w_up, "shard", axis=0, tiled=True),
        lax.all_gather(w_down, "shard", axis=0, tiled=True),
    )
    gain_first = full_gain_attn.astype(jnp.float32)
    gain_second = full_gain_ffn.astype(jnp.float32)
    cosine, sine_vals, allowed = tables(segments[0], HEAD_DIMENSION)
    cosine_per_head = cosine[:, None, :]
    sine_per_head = sine_vals[:, None, :]
    inputs = tokens[0].astype(jnp.float32)
    normed_first, unit_first, rstd_first = norm_forward(inputs, gain_first)
    acts_first = normed_first.astype(jnp.bfloat16)
    joined_projection = jnp.dot(
        acts_first, full_qkv, preferred_element_type=jnp.float32
    ) + full_bias.astype(jnp.float32)
    query_rows = apply_rotation(
        joined_projection[:, :head_dimension].reshape(token_length, QUERY_HEADS, HEAD_DIMENSION),
        cosine_per_head,
        sine_per_head,
    )
    query_reduced = (
        (query_rows * logit_scale)
        .astype(jnp.bfloat16)
        .reshape(token_length, KEY_VALUE_HEADS, heads_per_group, HEAD_DIMENSION)
    )
    k_low = apply_rotation(
        joined_projection[:, head_dimension:key_value_limit].reshape(
            token_length, KEY_VALUE_HEADS, HEAD_DIMENSION
        ),
        cosine_per_head,
        sine_per_head,
    ).astype(jnp.bfloat16)
    value_reduced = (
        joined_projection[:, key_value_limit:]
        .reshape(token_length, KEY_VALUE_HEADS, HEAD_DIMENSION)
        .astype(jnp.bfloat16)
    )
    scores = jnp.einsum("ikrd,jkd->krij", query_reduced, k_low, preferred_element_type=jnp.float32)
    scores = jnp.where(allowed != 0, scores, -1e30)
    largest = jnp.max(scores, axis=-1, keepdims=True)
    exponents = jnp.exp(scores - largest)
    soft_probs = exponents / jnp.sum(exponents, axis=-1, keepdims=True)
    soft_low = soft_probs.astype(jnp.bfloat16)
    attended = jnp.einsum(
        "krij,jkd->ikrd", soft_low, value_reduced, preferred_element_type=jnp.float32
    )
    attended = attended.reshape(token_length, head_dimension).astype(jnp.bfloat16)
    hidden_mid = inputs + jnp.dot(attended, full_out, preferred_element_type=jnp.float32)
    normed_second, unit_second, rstd_second = norm_forward(hidden_mid, gain_second)
    acts_second = normed_second.astype(jnp.bfloat16)
    gate_vals = jnp.dot(acts_second, full_gate, preferred_element_type=jnp.float32)
    up_vals = jnp.dot(acts_second, full_up, preferred_element_type=jnp.float32)
    sigmoid_gate = jax.nn.sigmoid(gate_vals)
    active = gate_vals * sigmoid_gate
    mixed_hidden = (active * up_vals).astype(jnp.bfloat16)
    result = (
        hidden_mid + jnp.dot(mixed_hidden, full_down, preferred_element_type=jnp.float32)
    ).astype(jnp.bfloat16)
    full_qkv, full_out = (
        lax.all_gather(w_qkv, "shard", axis=0, tiled=True),
        lax.all_gather(w_out, "shard", axis=0, tiled=True),
    )
    full_gate, full_up, full_down = (
        lax.all_gather(w_gate, "shard", axis=0, tiled=True),
        lax.all_gather(w_up, "shard", axis=0, tiled=True),
        lax.all_gather(w_down, "shard", axis=0, tiled=True),
    )
    grad_out = cotangent[0]
    d_mixed = jnp.einsum("ld,fd->lf", grad_out, full_down, preferred_element_type=jnp.float32)
    d_active = d_mixed * up_vals
    d_gate = (
        d_active * sigmoid_gate + d_active * gate_vals * sigmoid_gate * (1.0 - sigmoid_gate)
    ).astype(jnp.bfloat16)
    d_up = (d_mixed * active).astype(jnp.bfloat16)
    down_grad = lax.psum_scatter(
        column_term(mixed_hidden, grad_out).astype(jnp.bfloat16),
        "shard",
        scatter_dimension=0,
        tiled=True,
    )
    gate_grad = lax.psum_scatter(
        column_term(acts_second, d_gate).astype(jnp.bfloat16),
        "shard",
        scatter_dimension=0,
        tiled=True,
    )
    up_grad = lax.psum_scatter(
        column_term(acts_second, d_up).astype(jnp.bfloat16),
        "shard",
        scatter_dimension=0,
        tiled=True,
    )
    d_normed_second = jnp.einsum("lf,df->ld", d_gate, full_gate, preferred_element_type=jnp.float32)
    d_normed_second = d_normed_second + jnp.einsum(
        "lf,df->ld", d_up, full_up, preferred_element_type=jnp.float32
    )
    gain_second_grad = jnp.sum(d_normed_second * unit_second, axis=0)
    d_hidden_mid = grad_out.astype(jnp.float32) + norm_backward(
        d_normed_second, gain_second, unit_second, rstd_second
    )
    d_branch = d_hidden_mid.astype(jnp.bfloat16)
    out_grad_term = jnp.einsum("le,ld->ed", attended, d_branch, preferred_element_type=jnp.float32)
    attended_gradient = jnp.einsum(
        "ld,ed->le", d_branch, full_out, preferred_element_type=jnp.float32
    )
    attended_gradient = attended_gradient.astype(jnp.bfloat16).reshape(
        token_length, KEY_VALUE_HEADS, heads_per_group, HEAD_DIMENSION
    )
    d_probs = jnp.einsum(
        "ikrd,jkd->krij", attended_gradient, value_reduced, preferred_element_type=jnp.float32
    )
    value_gradient = jnp.einsum(
        "krij,ikrd->jkd", soft_low, attended_gradient, preferred_element_type=jnp.float32
    )
    d_scores = soft_probs * (d_probs - jnp.sum(soft_probs * d_probs, axis=-1, keepdims=True))
    d_scores_low = d_scores.astype(jnp.bfloat16)
    d_queries = jnp.einsum(
        "krij,jkd->ikrd", d_scores_low, k_low, preferred_element_type=jnp.float32
    )
    d_queries = rotate_back(
        d_queries.reshape(token_length, QUERY_HEADS, HEAD_DIMENSION) * logit_scale,
        cosine_per_head,
        sine_per_head,
    )
    key_gradient = jnp.einsum(
        "krij,ikrd->jkd", d_scores_low, query_reduced, preferred_element_type=jnp.float32
    )
    key_gradient = rotate_back(key_gradient, cosine_per_head, sine_per_head)
    d_joined = jnp.concatenate(
        [
            d_queries.reshape(token_length, head_dimension),
            key_gradient.reshape(token_length, KEY_VALUE_HEADS * HEAD_DIMENSION),
            value_gradient.reshape(token_length, KEY_VALUE_HEADS * HEAD_DIMENSION),
        ],
        axis=1,
    ).astype(jnp.bfloat16)
    bias_grad_term = jnp.sum(d_joined.astype(jnp.float32), axis=0)
    qkv_grad_term = jnp.einsum(
        "ld,le->de", acts_first, d_joined, preferred_element_type=jnp.float32
    )
    d_normed_first = jnp.einsum("le,de->ld", d_joined, full_qkv, preferred_element_type=jnp.float32)
    gain_first_grad = jnp.sum(d_normed_first * unit_first, axis=0)
    d_inputs = d_hidden_mid + norm_backward(d_normed_first, gain_first, unit_first, rstd_first)
    owned = (
        lax.psum_scatter(
            gain_first_grad.astype(jnp.bfloat16), "shard", scatter_dimension=0, tiled=True
        ).astype(jnp.float32),
        lax.psum_scatter(
            qkv_grad_term.astype(jnp.bfloat16), "shard", scatter_dimension=0, tiled=True
        ).astype(jnp.float32),
        lax.psum_scatter(
            bias_grad_term.astype(jnp.bfloat16), "shard", scatter_dimension=0, tiled=True
        ).astype(jnp.float32),
        lax.psum_scatter(
            out_grad_term.astype(jnp.bfloat16), "shard", scatter_dimension=0, tiled=True
        ).astype(jnp.float32),
        lax.psum_scatter(
            gain_second_grad.astype(jnp.bfloat16), "shard", scatter_dimension=0, tiled=True
        ).astype(jnp.float32),
    )
    summed = (
        lax.psum(owned[0].astype(jnp.bfloat16), "replica").astype(jnp.float32),
        lax.psum(owned[1].astype(jnp.bfloat16), "replica").astype(jnp.float32),
        lax.psum(owned[2].astype(jnp.bfloat16), "replica").astype(jnp.float32),
        lax.psum(owned[3].astype(jnp.bfloat16), "replica").astype(jnp.float32),
        lax.psum(owned[4].astype(jnp.bfloat16), "replica").astype(jnp.float32),
        lax.psum(gate_grad, "replica").astype(jnp.float32),
        lax.psum(up_grad, "replica").astype(jnp.float32),
        lax.psum(down_grad, "replica").astype(jnp.float32),
    )
    return (
        result[None],
        d_inputs.astype(jnp.bfloat16)[None],
        summed[0],
        summed[1],
        summed[2],
        summed[3],
        summed[4],
        summed[5],
        summed[6],
        summed[7],
    )


def solution(mesh):
    placed = (
        P(("replica", "shard"), None, None),
        P(("replica", "shard"), None),
        P("shard"),
        P("shard", None),
        P("shard"),
        P("shard", None),
        P("shard"),
        P("shard", None),
        P("shard", None),
        P("shard", None),
        P(("replica", "shard"), None, None),
    )
    return jax.shard_map(
        shards,
        mesh=mesh,
        in_specs=placed,
        out_specs=(
            P(("replica", "shard"), None, None),
            P(("replica", "shard"), None, None),
            P("shard"),
            P("shard", None),
            P("shard"),
            P("shard", None),
            P("shard"),
            P("shard", None),
            P("shard", None),
            P("shard", None),
        ),
        check_vma=False,
    )
```

profile of v0, /device:TPU:0, one launch (start us, length us, event | category | flops | bytes accessed | tf_op | source)
XLA Modules:
  0.0 3599.3 jit_solution(6908769301761609728)
XLA Ops:
  7.2 0.7 all-gather.7.cloned.1.call-update
  8.0 0.7 all-gather.9.cloned.1.call-update
  8.8 0.7 all-gather.11.cloned.1.call-update
  9.5 0.5 all-gather.13.cloned.1.call-update
  10.1 0.5 all-gather.15.cloned.1.call-update
  10.7 22.7 all-gather
  33.4 0.6 fusion.48
  35.2 18.0 all-reduce.6
  53.6 0.7 broadcast_multiply_fusion.1
  54.5 58.2 %all-gather.7.cloned.1.call-done = bf16[1536,2048]{1,0:T(8,128)(2,1)} async-done(((bf16[192,2048]{1,0:T(8,128)(2,1)}), bf16[1536,2048]{1,0:T(8,128)(2,1)}) %all-gather.7.cloned.1.call-update) | async-done | bytes 6291472 | tf_op jit(solution)/shard_map/all_gather | solution.py:80
  112.7 3.8 convolution_add_fusion.3
  116.8 0.3 copy.55
  117.3 1.3 fusion.49
  118.6 0.6 convolution_convert_fusion.6
  119.2 73.7 %all-gather.9.cloned.1.call-done = bf16[1536,1536]{1,0:T(8,128)(2,1)} async-done(((bf16[192,1536]{1,0:T(8,128)(2,1)}), bf16[1536,1536]{1,0:T(8,128)(2,1)}) %all-gather.9.cloned.1.call-update) | async-done | bytes 4718608 | tf_op jit(solution)/shard_map/all_gather | solution.py:82
  193.0 3.2 multiply_reduce_fusion.3
  196.4 520.9 %all-gather.11.cloned.1.call-done = bf16[1536,8960]{1,0:T(8,128)(2,1)} async-done(((bf16[192,8960]{1,0:T(8,128)(2,1)}), bf16[1536,8960]{1,0:T(8,128)(2,1)}) %all-gather.11.cloned.1.call-update) | async-done | bytes 27525136 | tf_op jit(solution)/shard_map/all_gather | solution.py:87
  717.4 15.2 fusion.50
  732.5 510.9 %all-gather.13.cloned.1.call-done = bf16[1536,8960]{1,0:T(8,128)(2,1)} async-done(((bf16[192,8960]{1,0:T(8,128)(2,1)}), bf16[1536,8960]{1,0:T(8,128)(2,1)}) %all-gather.13.cloned.1.call-update) | async-done | bytes 27525136 | tf_op jit(solution)/shard_map/all_gather | solution.py:88
  1243.4 15.2 fusion.51
  1258.6 510.9 %all-gather.15.cloned.1.call-done = bf16[8960,1536]{1,0:T(8,128)(2,1)} async-done(((bf16[1120,1536]{1,0:T(8,128)(2,1)}), bf16[8960,1536]{1,0:T(8,128)(2,1)}) %all-gather.15.cloned.1.call-update) | async-done | bytes 27525136 | tf_op jit(solution)/shard_map/all_gather | solution.py:89
  1769.5 17.8 multiply_convert_fusion
  1787.3 14.9 fusion.52
  1802.2 16.1 multiply_reduce_fusion
  1818.3 0.7 broadcast_multiply_fusion.4
  1819.0 1.5 multiply_add_fusion
  1820.5 0.9 copy-done.2
  1821.4 4.6 convolution_convert_fusion.4
  1826.0 0.3 reduce-scatter.6.cloned.1.call-start
  1826.2 5.0 convolution_convert_fusion.5
  1831.2 1.9 copy.61
  1833.1 1.6 multiply_reduce_fusion.1
  1834.8 1.3 multiply_convert_fusion.2
  1836.6 0.8 fusion.24
  1837.4 0.3 broadcast_multiply_fusion
  1837.8 2.4 fusion.11
  1840.1 5.6 convolution_convert_fusion.3
  1845.8 14.1 convolution_convert_fusion.2
  1860.0 0.3 reduce-scatter.12.cloned.1.call-start
  1860.3 1.3 copy-done
  1861.6 14.2 convolution_convert_fusion.1
  1875.9 1.6 copy-done.1
  1877.5 13.9 convolution_convert_fusion
  1891.4 30.0 reduce-scatter.8.cloned.1.call-done
  1921.4 122.0 %reduce-scatter.6.cloned.1.call-done = bf16[192,2048]{1,0:T(8,128)(2,1)} async-done(((bf16[1536,2048]{1,0:T(8,128)(2,1)}), bf16[192,2048]{1,0:T(8,128)(2,1)}) %reduce-scatter.6.cloned.1.call-update) | async-done | bytes 786448 | tf_op jit(solution)/shard_map/reduce_scatter | solution.py:234
  2043.4 440.8 %reduce-scatter.10.cloned.1.call-done = bf16[192,8960]{1,0:T(8,128)(2,1)} async-done(((bf16[1536,8960]{1,0:T(8,128)(2,1)}), bf16[192,8960]{1,0:T(8,128)(2,1)}) %reduce-scatter.10.cloned.1.call-update) | async-done | bytes 3440656 | tf_op jit(solution)/shard_map/reduce_scatter | solution.py:167
  2484.1 441.3 %reduce-scatter.12.cloned.1.call-done = bf16[192,8960]{1,0:T(8,128)(2,1)} async-done(((bf16[1536,8960]{1,0:T(8,128)(2,1)}), bf16[192,8960]{1,0:T(8,128)(2,1)}) %reduce-scatter.12.cloned.1.call-update) | async-done | bytes 3440656 | tf_op jit(solution)/shard_map/reduce_scatter | solution.py:173
  2925.4 440.6 %reduce-scatter.14.cloned.1.call-done = bf16[1120,1536]{1,0:T(8,128)(2,1)} async-done(((bf16[8960,1536]{1,0:T(8,128)(2,1)}), bf16[1120,1536]{1,0:T(8,128)(2,1)}) %reduce-scatter.14.cloned.1.call-update) | async-done | bytes 3440656 | tf_op jit(solution)/shard_map/reduce_scatter | solution.py:161
  3367.3 1.3 fusion.44
  3368.6 6.7 fusion.18
  3375.3 35.1 all-reduce.5
  3410.6 6.8 all-reduce.7
  3417.5 0.6 convert_element_type.169
  3418.0 0.6 convert_element_type.172
  3418.6 0.6 convert_element_type.176
  3419.2 0.7 broadcast_multiply_fusion.3
  3419.8 2.5 fusion.25
  3422.3 12.4 fusion.3
  3434.7 142.1 %all-reduce.11.cloned.1.call-done = (bf16[192,2048]{1,0:T(8,128)(2,1)}, bf16[192,1536]{1,0:T(8,128)(2,1)}, bf16[192,8960]{1,0:T(8,128)(2,1)}, bf16[192,8960]{1,0:T(8,128)(2,1)}, bf16[1120,1536]{1,0:T(8,128)(2,1)}) async-done(((bf16[192,2048]{1,0:T(8,128)(2,1)}, bf16[192,1536]{1,0:T(8,128)(2,1)}, bf16[192,8960]{1,0:T(8,128)(2,1)}, bf16[192,8960]{1,0:T(8,128)(2,1)}, bf16[1120,1536]{1,0:T(8,128)(2,1)}), ...) | async-done | bytes 11698192 | tf_op jit(solution)/shard_map/psum | solution.py:249
  3576.7 2.6 convert_element_type.171
  3579.3 2.2 convert_element_type.174
  3581.5 3.4 convert_element_type.178
  3585.0 3.4 convert_element_type.180
  3588.4 3.8 convert_element_type.182
  (105 shorter events, 2.9 us)
Async XLA Ops:
  7.2 105.5 %all-gather.7.cloned.1.call-start = ((), (), s32[]{:S(2)}) async-start(), calls=%async_computation.5 | async-start | bytes 7077888 | tf_op jit(solution)/shard_map/all_gather | solution.py:80
  7.9 185.1 %all-gather.9.cloned.1.call-start = ((), (), s32[]{:S(2)}) async-start(), calls=%async_computation.6 | async-start | bytes 5308416 | tf_op jit(solution)/shard_map/all_gather | solution.py:82
  8.7 2.0 copy-start.26
  8.7 24.7 copy-start.25
  8.7 26.0 copy-start.27
  8.7 26.2 copy-start.28
  8.7 44.5 %copy-start.24 = (s32[1,128]{1,0:T(1,128)S(1)}, s32[1,128]{1,0:T(1,128)}, u32[]{:S(2)}) copy-start(s32[1,128]{1,0:T(1,128)} %param.12) | copy-start | bytes 1540
  8.7 45.5 %copy-start.3 = (bf16[1,128,1536]{2,1,0:T(8,128)(2,1)S(1)}, bf16[1,128,1536]{2,1,0:T(8,128)(2,1)}, u32[]{:S(2)}) copy-start(bf16[1,128,1536]{2,1,0:T(8,128)(2,1)} %param.11) | copy-start | bytes 1179652
  8.7 708.6 %all-gather.11.cloned.1.call-start = ((), (), s32[]{:S(2)}) async-start(), calls=%async_computation.7 | async-start | bytes 30965760 | tf_op jit(solution)/shard_map/all_gather | solution.py:87
  9.5 1234.0 %all-gather.13.cloned.1.call-start = ((), (), s32[]{:S(2)}) async-start(), calls=%async_computation.8 | async-start | bytes 30965760 | tf_op jit(solution)/shard_map/all_gather | solution.py:88
  10.0 1759.5 %all-gather.15.cloned.1.call-start = ((), (), s32[]{:S(2)}) async-start(), calls=%async_computation.9 | async-start | bytes 30965760 | tf_op jit(solution)/shard_map/all_gather | solution.py:89
  10.6 1910.8 %reduce-scatter.8.cloned.1.call-start = ((), (), s32[]{:S(2)}) async-start(), calls=%async_computation.11 | async-start | bytes 5308416 | tf_op jit(solution)/shard_map/reduce_scatter | solution.py:240
  54.2 62.9 %copy-start.11 = (f32[128,128]{0,1:T(8,128)}, f32[128,128]{0,1:T(8,128)S(1)}, u32[]{:S(2)}) copy-start(f32[128,128]{0,1:T(8,128)S(1)} %get-tuple-element.56) | copy-start | bytes 196612
  54.4 62.2 %copy-start.22 = (f32[128]{0:T(128)}, f32[128]{0:T(128)S(1)}, u32[]{:S(2)}) copy-start(f32[128]{0:T(128)S(1)} %add_rsqrt_fusion.1) | copy-start | bytes 1540
  54.5 64.1 %copy-start.19 = (pred[128,128]{0,1:T(8,128)(4,1)}, pred[128,128]{0,1:T(8,128)(4,1)S(1)}, u32[]{:S(2)}) copy-start(pred[128,128]{0,1:T(8,128)(4,1)S(1)} %convert_compare_fusion) | copy-start | bytes 49156
  116.7 2.6 copy-start.17
  117.1 79.1 %copy-start.14 = (bf16[128,2,128,1]{0,2,3,1:T(8,128)(2,1)}, bf16[128,2,128,1]{0,2,3,1:T(8,128)(2,1)S(1)}, u32[]{:S(2)}) copy-start(bf16[128,2,128,1]{0,2,3,1:T(8,128)(2,1)S(1)} %fusion.38) | copy-start | bytes 196612
  117.3 78.9 %copy-start.9 = (bf16[128,2,6,128]{0,3,2,1:T(8,128)(2,1)}, bf16[128,2,6,128]{0,3,2,1:T(8,128)(2,1)S(1)}, u32[]{:S(2)}) copy-start(bf16[128,2,6,128]{0,3,2,1:T(8,128)(2,1)S(1)} %fusion.22) | copy-start | bytes 1179652
  118.6 77.6 %copy-start.20 = (f32[2,6,128]{2,1,0:T(8,128)}, f32[2,6,128]{2,1,0:T(8,128)S(1)}, u32[]{:S(2)}) copy-start(f32[2,6,128]{2,1,0:T(8,128)S(1)} %get-tuple-element.46) | copy-start | bytes 18436
  119.2 77.0 %copy-start.8 = (bf16[2,128,6,128]{3,1,2,0:T(8,128)(2,1)}, bf16[2,128,6,128]{3,1,2,0:T(8,128)(2,1)S(1)}, u32[]{:S(2)}) copy-start(bf16[2,128,6,128]{3,1,2,0:T(8,128)(2,1)S(1)} %convolution_convert_fusion.6) | copy-start | bytes 1179652
  196.3 536.3 %copy-start.23 = (f32[128]{0:T(128)}, f32[128]{0:T(128)S(1)}, u32[]{:S(2)}) copy-start(f32[128]{0:T(128)S(1)} %add_rsqrt_fusion) | copy-start | bytes 1540
  196.4 1047.0 %copy-start.4 = (bf16[128,1536]{1,0:T(8,128)(2,1)}, bf16[128,1536]{1,0:T(8,128)(2,1)S(1)}, u32[]{:S(2)}) copy-start(bf16[128,1536]{1,0:T(8,128)(2,1)S(1)} %multiply_convert_fusion.3) | copy-start | bytes 1179652
  1820.5 0.9 copy-start.2
  1825.9 7.2 copy-start.21
  1826.0 217.4 %reduce-scatter.6.cloned.1.call-start = ((), (), s32[]{:S(2)}) async-start(), calls=%async_computation.10 | async-start | bytes 7077888 | tf_op jit(solution)/shard_map/reduce_scatter | solution.py:234
  1833.1 3.0 copy-start.15
  1833.1 3.2 copy-start.16
  1834.7 1.8 copy-start.13
  1834.7 2.7 copy-start.10
  1836.1 1.6 copy-start.12
  1845.8 638.3 %reduce-scatter.10.cloned.1.call-start = ((), (), s32[]{:S(2)}) async-start(), calls=%async_computation.12 | async-start | bytes 30965760 | tf_op jit(solution)/shard_map/reduce_scatter | solution.py:167
  1859.9 1.7 copy-start
  1860.0 1065.4 %reduce-scatter.12.cloned.1.call-start = ((), (), s32[]{:S(2)}) async-start(), calls=%async_computation.13 | async-start | bytes 30965760 | tf_op jit(solution)/shard_map/reduce_scatter | solution.py:173
  1875.8 1.6 copy-start.1
  1875.9 1490.1 %reduce-scatter.14.cloned.1.call-start = ((), (), s32[]{:S(2)}) async-start(), calls=%async_computation.14 | async-start | bytes 30965760 | tf_op jit(solution)/shard_map/reduce_scatter | solution.py:161
  1891.4 1685.3 %all-reduce.11.cloned.1.call-start = ((), (), s32[]{:S(2)}) async-start(), calls=%async_computation.15 | async-start | bytes 23396352 | tf_op jit(solution)/shard_map/psum | solution.py:249
  3366.0 9.2 copy-start.18
  3576.7 4.8 copy-start.7
  3581.5 3.4 copy-start.6
  3585.0 3.4 copy-start.5
Sparse Core Ops, SparseCore 0:
  10.2 102.4 all-gather.6
  114.9 78.0 all-gather.8
  194.5 522.8 all-gather.10
  718.8 524.6 all-gather.12
  1244.8 524.6 all-gather.14
  1826.1 95.2 reduce-scatter.7
  1925.6 117.7 reduce-scatter.5
  2047.2 436.8 reduce-scatter.9
  2488.5 436.8 reduce-scatter.11
  2929.1 436.8 reduce-scatter.13
  3369.3 207.3 all-reduce.10
where the time goes:
time: 3610 us; the launch traced here: 3600 us
  waiting for transfers between devices  3290 us (91%)
  matrix products  169 us (5%)
  blocking collectives  82.7 us (2%)
    all_gather x1, waiting for transfers between devices, shards(): lax.all_gather(w_gate, 'shard', axis=0, tiled=True)  521 us
    all_gather x1, waiting for transfers between devices, shards(): lax.all_gather(w_up, 'shard', axis=0, tiled=True)  511 us
    all_gather x1, waiting for transfers between devices, shards(): lax.all_gather(w_down, 'shard', axis=0, tiled=True)  511 us
    reduce_scatter x1, waiting for transfers between devices, shards(): lax.psum_scatter(column_term(acts_second, d_up).astype(jnp.bfloat16), 'sh...  441 us
    reduce_scatter x1, waiting for transfers between devices, shards(): lax.psum_scatter(column_term(acts_second, d_gate).astype(jnp.bfloat16), '...  441 us
    reduce_scatter x1, waiting for transfers between devices, shards(): lax.psum_scatter(column_term(mixed_hidden, grad_out).astype(jnp.bfloat16)...  441 us
    psum x1, waiting for transfers between devices, shards(): lax.psum(owned[1].astype(jnp.bfloat16), 'replica').astype(jnp.float32)  142 us
    reduce_scatter x1, waiting for transfers between devices, shards(): lax.psum_scatter(qkv_grad_term.astype(jnp.bfloat16), 'shard', scatter_dim...  122 us
  transfers between devices with their start and end apart: 11, of which 11 were waited for; matrix products, arithmetic and copies ran while one was open for 4% of the time, Pallas kernels for 0%

commit v1 on v0

--- a/solution.py
+++ b/solution.py
@@ -67,6 +67,24 @@
     return jnp.einsum("lf,ld->fd", left_side, right_side, preferred_element_type=jnp.float32)
 
 
+def to_columns(rows):
+    ranks = lax.axis_size("shard")
+    depth, width = rows.shape
+    split = rows.reshape(depth, ranks, width // ranks).transpose(1, 0, 2)
+    return lax.all_to_all(split, "shard", 0, 0, tiled=True).reshape(ranks * depth, width // ranks)
+
+
+def to_rows(columns):
+    ranks, copies = lax.axis_size("shard"), lax.axis_size("replica")
+    depth, width = columns.shape
+    depth = depth // ranks
+    parts = columns.reshape(ranks, copies, depth // copies, width)
+    part = lax.psum_scatter(parts, "replica", scatter_dimension=1, tiled=False)
+    part = lax.all_to_all(part, "shard", 0, 0, tiled=True)
+    part = part.transpose(1, 0, 2).reshape(depth // copies, ranks * width)
+    return lax.all_gather(part, "replica", axis=0, tiled=True)
+
+
 def shards(
     tokens, segments, gain_attn, w_qkv, b_qkv, w_out, gain_ffn, w_gate, w_up, w_down, cotangent
 ):
@@ -75,19 +93,16 @@
     key_value_limit = head_dimension + KEY_VALUE_HEADS * HEAD_DIMENSION
     logit_scale = HEAD_DIMENSION ** (-0.5)
     token_length = tokens.shape[1]
-    attn_set = (
+    full_gain_attn, full_qkv, full_bias, full_out, full_gain_ffn = (
         lax.all_gather(gain_attn, "shard", axis=0, tiled=True),
         lax.all_gather(w_qkv, "shard", axis=0, tiled=True),
         lax.all_gather(b_qkv, "shard", axis=0, tiled=True),
         lax.all_gather(w_out, "shard", axis=0, tiled=True),
         lax.all_gather(gain_ffn, "shard", axis=0, tiled=True),
     )
-    full_gain_attn, full_qkv, full_bias, full_out, full_gain_ffn = attn_set
-    full_gate, full_up, full_down = (
-        lax.all_gather(w_gate, "shard", axis=0, tiled=True),
-        lax.all_gather(w_up, "shard", axis=0, tiled=True),
-        lax.all_gather(w_down, "shard", axis=0, tiled=True),
-    )
+    gate_columns = to_columns(w_gate)
+    up_columns = to_columns(w_up)
+    all_cot = lax.all_gather(cotangent[0], "shard", axis=0, tiled=True)
     gain_first = full_gain_attn.astype(jnp.float32)
     gain_second = full_gain_ffn.astype(jnp.float32)
     cosine, sine_vals, allowed = tables(segments[0], HEAD_DIMENSION)
@@ -134,52 +149,36 @@
     hidden_mid = inputs + jnp.dot(attended, full_out, preferred_element_type=jnp.float32)
     normed_second, unit_second, rstd_second = norm_forward(hidden_mid, gain_second)
     acts_second = normed_second.astype(jnp.bfloat16)
-    gate_vals = jnp.dot(acts_second, full_gate, preferred_element_type=jnp.float32)
-    up_vals = jnp.dot(acts_second, full_up, preferred_element_type=jnp.float32)
+    all_acts = lax.all_gather(acts_second, "shard", axis=0, tiled=True)
+    gate_vals = jnp.dot(all_acts, gate_columns, preferred_element_type=jnp.float32)
+    up_vals = jnp.dot(all_acts, up_columns, preferred_element_type=jnp.float32)
     sigmoid_gate = jax.nn.sigmoid(gate_vals)
     active = gate_vals * sigmoid_gate
     mixed_hidden = (active * up_vals).astype(jnp.bfloat16)
-    result = (
-        hidden_mid + jnp.dot(mixed_hidden, full_down, preferred_element_type=jnp.float32)
-    ).astype(jnp.bfloat16)
-    full_qkv, full_out = (
-        lax.all_gather(w_qkv, "shard", axis=0, tiled=True),
-        lax.all_gather(w_out, "shard", axis=0, tiled=True),
-    )
-    full_gate, full_up, full_down = (
-        lax.all_gather(w_gate, "shard", axis=0, tiled=True),
-        lax.all_gather(w_up, "shard", axis=0, tiled=True),
-        lax.all_gather(w_down, "shard", axis=0, tiled=True),
-    )
-    grad_out = cotangent[0]
-    d_mixed = jnp.einsum("ld,fd->lf", grad_out, full_down, preferred_element_type=jnp.float32)
+    d_mixed = jnp.einsum("ld,fd->lf", all_cot, w_down, preferred_element_type=jnp.float32)
     d_active = d_mixed * up_vals
     d_gate = (
         d_active * sigmoid_gate + d_active * gate_vals * sigmoid_gate * (1.0 - sigmoid_gate)
     ).astype(jnp.bfloat16)
     d_up = (d_mixed * active).astype(jnp.bfloat16)
-    down_grad = lax.psum_scatter(
-        column_term(mixed_hidden, grad_out).astype(jnp.bfloat16),
-        "shard",
-        scatter_dimension=0,
-        tiled=True,
-    )
-    gate_grad = lax.psum_scatter(
-        column_term(acts_second, d_gate).astype(jnp.bfloat16),
-        "shard",
-        scatter_dimension=0,
-        tiled=True,
-    )
-    up_grad = lax.psum_scatter(
-        column_term(acts_second, d_up).astype(jnp.bfloat16),
-        "shard",
-        scatter_dimension=0,
-        tiled=True,
-    )
-    d_normed_second = jnp.einsum("lf,df->ld", d_gate, full_gate, preferred_element_type=jnp.float32)
-    d_normed_second = d_normed_second + jnp.einsum(
-        "lf,df->ld", d_up, full_up, preferred_element_type=jnp.float32
-    )
+    d_normed_part = jnp.einsum("lf,df->ld", d_gate, gate_columns, preferred_element_type=jnp.float32)
+    d_normed_part = d_normed_part + jnp.einsum(
+        "lf,df->ld", d_up, up_columns, preferred_element_type=jnp.float32
+    )
+    d_normed_second = lax.psum_scatter(
+        d_normed_part.astype(jnp.bfloat16), "shard", scatter_dimension=0, tiled=True
+    ).astype(jnp.float32)
+    down_part = jnp.dot(mixed_hidden, w_down, preferred_element_type=jnp.float32)
+    result = (
+        hidden_mid
+        + lax.psum_scatter(
+            down_part.astype(jnp.bfloat16), "shard", scatter_dimension=0, tiled=True
+        ).astype(jnp.float32)
+    ).astype(jnp.bfloat16)
+    grad_out = cotangent[0]
+    down_grad = column_term(mixed_hidden, all_cot).astype(jnp.bfloat16)
+    gate_grad = to_rows(column_term(all_acts, d_gate).astype(jnp.bfloat16))
+    up_grad = to_rows(column_term(all_acts, d_up).astype(jnp.bfloat16))
     gain_second_grad = jnp.sum(d_normed_second * unit_second, axis=0)
     d_hidden_mid = grad_out.astype(jnp.float32) + norm_backward(
         d_normed_second, gain_second, unit_second, rstd_second
@@ -250,8 +249,8 @@
         lax.psum(owned[2].astype(jnp.bfloat16), "replica").astype(jnp.float32),
         lax.psum(owned[3].astype(jnp.bfloat16), "replica").astype(jnp.float32),
         lax.psum(owned[4].astype(jnp.bfloat16), "replica").astype(jnp.float32),
-        lax.psum(gate_grad, "replica").astype(jnp.float32),
-        lax.psum(up_grad, "replica").astype(jnp.float32),
+        gate_grad.astype(jnp.float32),
+        up_grad.astype(jnp.float32),
         lax.psum(down_grad, "replica").astype(jnp.float32),
     )
     return (

time: 3610 us -> 1200 us (0.33)
  waiting for transfers between devices: 3290 us -> 693 us
  blocking collectives: 82.7 us -> 267 us
  matrix products: 169 us -> 107 us
  local copies, waits for them, and re-layouts: 7.57 us -> 58.6 us
    all_gather x3 -> x4, waiting for transfers between devices: 1540 us -> 142 us  [the longest x1 99.8 us: shards(): all_acts = lax.all_gather(acts_second, 'shard', axis=0, tiled=True)]
    reduce_scatter x3 -> x2, waiting for transfers between devices: 1320 us -> 142 us  [the longest x1 76.6 us: shards(): lax.psum_scatter(down_part.astype(jnp.bfloat16), 'shard', scatter_dimensi...]
    unnamed x2, blocking collectives: 53.2 us -> 145 us
    psum x1, waiting for transfers between devices: 142 us -> 213 us  [shards(): lax.psum(owned[1].astype(jnp.bfloat16), 'replica').astype(jnp.float32)]
    all_gather x1, waiting for transfers between devices: 58.2 us -> 0.02 us  [shards(): lax.all_gather(w_qkv, 'shard', axis=0, tiled=True)]
    all_to_all x0 -> x2, blocking collectives: none -> 53.5 us  [to_rows(): part = lax.all_to_all(part, 'shard', 0, 0, tiled=True)]
    all_gather x1, waiting for transfers between devices: 73.7 us -> 27.3 us  [shards(): lax.all_gather(w_out, 'shard', axis=0, tiled=True)]
    dot_general x6, matrix products: 91.5 us -> 50.9 us  [the longest x1 10.1 us: shards(): jnp.einsum('ld,fd->lf', all_cot, w_down, preferred_element_type=jnp.float32)]
  transfers between devices with their start and end apart: 11 -> 13, of which waited for: 11 -> 8; matrix products, arithmetic and copies ran while one was open for 4% -> 13% of each run, Pallas kernels for 0% -> 0%
where the time goes in v1:
time: 1200 us; the launch traced here: 1190 us
  waiting for transfers between devices  693 us (58%)
  blocking collectives  267 us (22%)
  matrix products  107 us (9%)
  local copies, waits for them, and re-layouts  58.6 us (5%)
  other arithmetic  36 us (3%)
  between operations  16.5 us (1%)
  starting transfers between devices  13.5 us (1%)
    psum x1, waiting for transfers between devices, shards(): lax.psum(owned[1].astype(jnp.bfloat16), 'replica').astype(jnp.float32)  213 us
    unnamed x2, blocking collectives  145 us
    reduce_scatter x1, waiting for transfers between devices, shards(): lax.psum_scatter(qkv_grad_term.astype(jnp.bfloat16), 'shard', scatter_dim...  122 us
    all_gather x1, waiting for transfers between devices, shards(): all_acts = lax.all_gather(acts_second, 'shard', axis=0, tiled=True)  99.8 us
    reduce_scatter x1, waiting for transfers between devices, shards(): lax.psum_scatter(down_part.astype(jnp.bfloat16), 'shard', scatter_dimensi...  76.6 us
    reduce_scatter x1, waiting for transfers between devices, shards(): lax.psum_scatter(d_normed_part.astype(jnp.bfloat16), 'shard', scatter_dim...  65.3 us
    all_gather x1, blocking collectives, shards(): lax.all_gather(b_qkv, 'shard', axis=0, tiled=True)  63.1 us
    all_to_all x2, blocking collectives, to_rows(): part = lax.all_to_all(part, 'shard', 0, 0, tiled=True)  53.5 us
  transfers between devices with their start and end apart: 13, of which 8 were waited for; matrix products, arithmetic and copies ran while one was open for 13% of the time, Pallas kernels for 0%

profile of v1, /device:TPU:0, one launch (start us, length us, event | category | flops | bytes accessed | tf_op | source)
XLA Modules:
  0.0 1192.5 jit_solution(7288558131185316525)
XLA Ops:
  8.7 8.7 reshape.130
  17.4 4.4 copy.132
  21.8 7.7 all-to-all-start
  31.3 110.1 %all-reduce.8 = (bf16[1536]{0:T(1024)(128)(2,1)S(1)}, bf16[1536]{0:T(1024)(128)(2,1)S(1)}) all-reduce(bf16[1536]{0:T(1024)(128)(2,1)S(1)} %dynamic-update-slice, bf16[1536]{0:T(1024)(128)(2,1)S(1)} %dynamic-update-slice.1), channel_id=1, replica_groups=mesh['replica'=4,'shard'=8] {'shard'}, use_global_device_ids=true, to_apply=%add | all-reduce | flops 3072 | bytes 12288
  141.4 63.1 %all-gather.1 = bf16[8,1,256]{2,1,0:T(2,128)(2,1)S(1)} all-gather(bf16[1,1,256]{2,1,0:T(2,128)(2,1)S(1)} %reshape.152), channel_id=1, replica_groups=mesh['replica'=4,'shard'=8] {'shard'}, dimensions={0}, use_global_device_ids=true | all-gather | bytes 4608 | tf_op jit(solution)/shard_map/all_gather | solution.py:99
  205.5 1.2 fusion.26
  206.8 4.0 convolution_add_fusion.1
  210.8 1.0 slice.49
  212.7 2.3 copy.82
  215.0 1.7 copy.122
  216.6 0.9 slice_negate_fusion.3
  217.5 2.1 slice_negate_fusion.1
  219.6 1.6 fusion.43
  221.2 1.5 slice.61
  222.7 1.5 convert_element_type.159
  224.2 2.3 fusion.29
  226.5 2.3 fusion.54
  228.8 2.4 convolution_convert_fusion.7
  231.2 27.3 %all-gather.11.cloned.1.call-done = bf16[1536,1536]{1,0:T(8,128)(2,1)} async-done(((bf16[192,1536]{1,0:T(8,128)(2,1)}), bf16[1536,1536]{1,0:T(8,128)(2,1)}) %all-gather.11.cloned.1.call-update) | async-done | bytes 4718608 | tf_op jit(solution)/shard_map/all_gather | solution.py:100
  258.6 3.4 multiply_reduce_fusion.1
  262.0 0.9 copy-done.2
  262.9 0.9 multiply_convert_fusion.3
  263.8 8.7 reshape.132
  272.5 4.4 copy.131
  276.9 4.5 all-to-all-start.1
  282.3 99.8 %all-gather.13.cloned.1.call-done = bf16[1024,1536]{1,0:T(8,128)(2,1)} async-done(((bf16[128,1536]{1,0:T(8,128)(2,1)}), bf16[1024,1536]{1,0:T(8,128)(2,1)}) %all-gather.13.cloned.1.call-update) | async-done | bytes 3145744 | tf_op jit(solution)/shard_map/all_gather | solution.py:152
  382.1 8.9 fusion.55
  390.9 8.9 fusion.56
  399.8 42.0 %all-gather.19.cloned.1.call-done = bf16[1,1024,1536]{2,1,0:T(8,128)(2,1)} async-done(((bf16[1,128,1536]{2,1,0:T(8,128)(2,1)}), bf16[1,1024,1536]{2,1,0:T(8,128)(2,1)}) %all-gather.19.cloned.1.call-update) | async-done | bytes 3145744 | tf_op jit(solution)/shard_map/all_gather | solution.py:105
  441.8 10.1 multiply_convert_fusion
  451.9 8.0 fusion.57
  459.9 7.7 add_convert_fusion
  467.7 7.4 convolution_convert_fusion.5
  475.6 65.3 %reduce-scatter.13.cloned.1.call-done = bf16[128,1536]{1,0:T(8,128)(2,1)} async-done(((bf16[1024,1536]{1,0:T(8,128)(2,1)}), bf16[128,1536]{1,0:T(8,128)(2,1)}) %reduce-scatter.13.cloned.1.call-update) | async-done | bytes 393232 | tf_op jit(solution)/shard_map/reduce_scatter | solution.py:168
  540.9 1.3 fusion.18
  542.2 76.6 %reduce-scatter.11.cloned.1.call-done = bf16[128,1536]{1,0:T(8,128)(2,1)} async-done(((bf16[1024,1536]{1,0:T(8,128)(2,1)}), bf16[128,1536]{1,0:T(8,128)(2,1)}) %reduce-scatter.11.cloned.1.call-update) | async-done | bytes 393232 | tf_op jit(solution)/shard_map/reduce_scatter | solution.py:174
  618.8 2.2 fusion.17
  621.0 3.6 convolution_convert_fusion.4
  624.6 4.0 convolution_convert_fusion.6
  631.4 1.6 fusion.12
  633.0 4.6 convolution_convert_fusion.3
  637.9 8.1 convolution_convert_fusion.1
  646.0 5.6 copy.96
  651.6 8.2 convolution_convert_fusion
  659.9 5.7 copy.98
  665.5 8.1 convolution_convert_fusion.2
  673.6 45.6 %reduce-scatter.17.cloned.1.call-done = bf16[192,1536]{1,0:T(8,128)(2,1)} async-done(((bf16[1536,1536]{1,0:T(8,128)(2,1)}), bf16[192,1536]{1,0:T(8,128)(2,1)}) %reduce-scatter.17.cloned.1.call-update) | async-done | bytes 589840 | tf_op jit(solution)/shard_map/reduce_scatter | solution.py:239
  719.3 121.9 %reduce-scatter.15.cloned.1.call-done = bf16[192,2048]{1,0:T(8,128)(2,1)} async-done(((bf16[1536,2048]{1,0:T(8,128)(2,1)}), bf16[192,2048]{1,0:T(8,128)(2,1)}) %reduce-scatter.15.cloned.1.call-update) | async-done | bytes 786448 | tf_op jit(solution)/shard_map/reduce_scatter | solution.py:233
  842.4 212.9 %all-reduce.13.cloned.1.call-done = (bf16[192,2048]{1,0:T(8,128)(2,1)}, bf16[192,1536]{1,0:T(8,128)(2,1)}, bf16[8,4,48,1120]{3,2,1,0:T(8,128)(2,1)}, bf16[8,4,48,1120]{3,2,1,0:T(8,128)(2,1)}, bf16[1120,1536]{1,0:T(8,128)(2,1)}) async-done(((bf16[192,2048]{1,0:T(8,128)(2,1)}, bf16[192,1536]{1,0:T(8,128)(2,1)}, bf16[8,4,48,1120]{3,2,1,0:T(8,128)(2,1)}, bf16[8,4,48,1120]{3,2,1,0:T(8,128)(2,1)}, ...) | async-done | bytes 11698192 | tf_op jit(solution)/shard_map/psum | solution.py:248
  1055.3 1.9 dynamic-slice_bitcast_fusion.1
  1057.2 28.1 %all_to_all.20 = bf16[8,48,1120]{2,1,0:T(8,128)(2,1)S(1)} all-to-all(bf16[8,48,1120]{2,1,0:T(8,128)(2,1)S(1)} %dynamic-slice_bitcast_fusion.1), channel_id=1, replica_groups=mesh['replica'=4,'shard'=8] {'shard'}, dimensions={0} | all-to-all | bytes 1720320 | tf_op jit(solution)/shard_map/all_to_all | solution.py:83
  1085.4 1.7 reshape.140
  1087.1 1.9 dynamic-slice_bitcast_fusion
  1089.0 25.5 %all_to_all.21 = bf16[8,48,1120]{2,1,0:T(8,128)(2,1)S(1)} all-to-all(bf16[8,48,1120]{2,1,0:T(8,128)(2,1)S(1)} %dynamic-slice_bitcast_fusion), channel_id=1, replica_groups=mesh['replica'=4,'shard'=8] {'shard'}, dimensions={0} | all-to-all | bytes 1720320 | tf_op jit(solution)/shard_map/all_to_all | solution.py:83
  1114.7 1.7 reshape.142
  1117.9 5.1 fusion.25
  1123.0 35.0 %all-reduce.7 = (bf16[1536]{0:T(1024)(128)(2,1)S(1)}, bf16[2048]{0:T(1024)(128)(2,1)S(1)}, bf16[1536]{0:T(1024)(128)(2,1)S(1)}) all-reduce(bf16[1536]{0:T(1024)(128)(2,1)S(1)} %get-tuple-element.12, bf16[2048]{0:T(1024)(128)(2,1)S(1)} %fusion.49, ...), channel_id=5, replica_groups=mesh['replica'=4,'shard'=8] {'shard'}, use_global_device_ids=true, to_apply=%region_11.12.clone | all-reduce | flops 5120 | bytes 20480
  1158.2 5.6 all-reduce.9
  1165.5 1.0 fusion.33
  1166.6 5.9 convert_element_type.198
  1172.5 1.3 convert_element_type.187
  1173.8 1.1 convert_element_type.190
  1175.0 5.5 convert_element_type.194
  1180.5 5.3 convert_element_type.196
  (119 shorter events, 12.7 us)
Async XLA Ops:
  7.2 434.6 %copy-start = (bf16[1120,1536]{1,0:T(8,128)(2,1)S(1)}, bf16[1120,1536]{1,0:T(8,128)(2,1)}, u32[]{:S(2)}) copy-start(bf16[1120,1536]{1,0:T(8,128)(2,1)} %param.20) | copy-start | bytes 10321924
  7.2 199.6 %all-gather.9.cloned.1.call-start = ((), (), s32[]{:S(2)}) async-start(), calls=%async_computation.8 | async-start | bytes 7077888 | tf_op jit(solution)/shard_map/all_gather | solution.py:98
  7.9 250.7 %all-gather.11.cloned.1.call-start = ((), (), s32[]{:S(2)}) async-start(), calls=%async_computation.9 | async-start | bytes 5308416 | tf_op jit(solution)/shard_map/all_gather | solution.py:100
  21.8 7.8 copy-start.19
  21.8 9.0 copy-start.20
  21.8 9.3 copy-start.21
  21.8 119.6 %copy-start.22 = (bf16[256]{0:T(256)(128)(2,1)S(1)}, bf16[256]{0:T(256)(128)(2,1)}, u32[]{:S(2)}) copy-start(bf16[256]{0:T(256)(128)(2,1)} %param.15) | copy-start | bytes 1540
  21.8 182.7 %copy-start.18 = (s32[1,128]{1,0:T(1,128)S(1)}, s32[1,128]{1,0:T(1,128)}, u32[]{:S(2)}) copy-start(s32[1,128]{1,0:T(1,128)} %param.12) | copy-start | bytes 1540
  21.8 255.1 %all-to-all-start = ((bf16[8,192,1120]{2,1,0:T(8,128)(2,1)}), bf16[8,192,1120]{2,1,0:T(8,128)(2,1)}, u32[]{:S(2)}, u32[]{:S(2)}) async-start(bf16[8,192,1120]{2,1,0:T(8,128)(2,1)} %bitcast.158), calls=%async_computation | async-start | bytes 7077888 | tf_op jit(solution)/shard_map/all_to_all | solution.py:74
  29.5 352.6 %all-gather.13.cloned.1.call-start = ((), (), s32[]{:S(2)}) async-start(), calls=%async_computation.10 | async-start | bytes 3538944 | tf_op jit(solution)/shard_map/all_gather | solution.py:152
  210.8 1.2 copy-start.5
  262.0 0.9 copy-start.2
  276.9 114.0 %all-to-all-start.1 = ((bf16[8,192,1120]{2,1,0:T(8,128)(2,1)}), bf16[8,192,1120]{2,1,0:T(8,128)(2,1)}, u32[]{:S(2)}, u32[]{:S(2)}) async-start(bf16[8,192,1120]{2,1,0:T(8,128)(2,1)} %bitcast.159), calls=%async_computation.1 | async-start | bytes 7077888 | tf_op jit(solution)/shard_map/all_to_all | solution.py:74
  281.4 160.4 %all-gather.19.cloned.1.call-start = ((), (), s32[]{:S(2)}) async-start(), calls=%async_computation.17 | async-start | bytes 3538944 | tf_op jit(solution)/shard_map/all_gather | solution.py:105
  282.0 258.9 %reduce-scatter.13.cloned.1.call-start = ((), (), s32[]{:S(2)}) async-start(), calls=%async_computation.12 | async-start | bytes 3538944 | tf_op jit(solution)/shard_map/reduce_scatter | solution.py:168
  451.9 8.0 copy-start.24
  451.9 8.0 copy-start.25
  467.6 151.2 %reduce-scatter.11.cloned.1.call-start = ((), (), s32[]{:S(2)}) async-start(), calls=%async_computation.11 | async-start | bytes 3538944 | tf_op jit(solution)/shard_map/reduce_scatter | solution.py:174
  475.1 65.8 %copy-start.3 = (f32[128,1536]{1,0:T(8,128)S(1)}, f32[128,1536]{1,0:T(8,128)}, u32[]{:S(2)}) copy-start(f32[128,1536]{1,0:T(8,128)} %copy-done.2) | copy-start | bytes 2359300
  475.1 143.7 %copy-start.8 = (bf16[1,128,1536]{2,1,0:T(8,128)(2,1)S(1)}, bf16[1,128,1536]{2,1,0:T(8,128)(2,1)}, u32[]{:S(2)}) copy-start(bf16[1,128,1536]{2,1,0:T(8,128)(2,1)} %param.21) | copy-start | bytes 1179652
  475.1 145.9 %copy-start.6 = (bf16[2,128,6,128]{3,1,2,0:T(8,128)(2,1)S(1)}, bf16[2,128,6,128]{3,1,2,0:T(8,128)(2,1)}, u32[]{:S(2)}) copy-start(bf16[2,128,6,128]{3,1,2,0:T(8,128)(2,1)} %convolution_convert_fusion.7) | copy-start | bytes 1179652
  475.1 244.1 %reduce-scatter.17.cloned.1.call-start = ((), (), s32[]{:S(2)}) async-start(), calls=%async_computation.14 | async-start | bytes 5308416 | tf_op jit(solution)/shard_map/reduce_scatter | solution.py:239
  624.5 4.4 copy-start.10
  624.6 4.4 copy-start.17
  624.6 216.6 %reduce-scatter.15.cloned.1.call-start = ((), (), s32[]{:S(2)}) async-start(), calls=%async_computation.13 | async-start | bytes 7077888 | tf_op jit(solution)/shard_map/reduce_scatter | solution.py:233
  628.7 1.1 copy-start.15
  628.7 1.4 copy-start.16
  628.9 0.8 copy-start.13
  629.7 0.8 copy-start.14
  630.1 1.0 copy-start.7
  630.2 1.2 copy-start.9
  630.5 2.5 copy-start.4
  637.7 417.6 %all-reduce.13.cloned.1.call-start = ((), (), s32[]{:S(2)}) async-start(), calls=%async_computation.18 | async-start | bytes 23789568 | tf_op jit(solution)/shard_map/psum | solution.py:248
  841.2 0.7 copy-start.23
  841.2 333.8 %all-gather.15.cloned.1.call-start = ((), (), s32[]{:S(2)}) async-start(), calls=%async_computation.15 | async-start | bytes 4300800 | tf_op jit(solution)/shard_map/all_gather | solution.py:85
  1087.1 93.4 %all-gather.17.cloned.1.call-start = ((), (), s32[]{:S(2)}) async-start(), calls=%async_computation.16 | async-start | bytes 4300800 | tf_op jit(solution)/shard_map/all_gather | solution.py:85
  1166.6 5.9 copy-start.11
  1166.6 7.3 copy-start.12
  1175.0 10.8 copy-start.1
Sparse Core Ops, SparseCore 0:
  10.2 167.7 all-gather.8
  180.2 78.3 all-gather.10
  263.9 118.0 all-gather.12
  384.1 57.6 all-gather.18
  467.8 73.1 reduce-scatter.12
  544.9 73.8 reduce-scatter.10
  624.7 94.5 reduce-scatter.16
  723.4 117.7 reduce-scatter.14
  844.8 210.4 all-reduce.12
  1087.2 27.9 all-gather.14
  1116.9 30.1 all-gather.16

commit v2 on v1

--- a/solution.py
+++ b/solution.py
@@ -3,7 +3,12 @@
 import jax
 import jax.numpy as jnp
 from jax import lax
+from jax.experimental import pallas as pl
+from jax.experimental.pallas import tpu as pltpu
 from jax.sharding import PartitionSpec as P
+
+MESH = pl.DeviceIdType.MESH
+BF, F32 = jnp.bfloat16, jnp.float32
 
 QUERY_HEADS = 12
 KEY_VALUE_HEADS = 2
@@ -65,6 +70,480 @@
 
 def column_term(left_side, right_side):
     return jnp.einsum("lf,ld->fd", left_side, right_side, preferred_element_type=jnp.float32)
+
+
+def topo():
+    r = lax.axis_index("replica"); s = lax.axis_index("shard")
+    x, c, z, y = r // 2, r % 2, s // 2, s % 2
+    return r, s, x, c, z, y
+
+def rcopy(src, dst, ssem, rsem, dev):
+    return pltpu.make_async_remote_copy(src_ref=src, dst_ref=dst, send_sem=ssem, recv_sem=rsem, device_id=dev, device_id_type=MESH)
+
+def greet(devs):
+    bar = pltpu.get_barrier_semaphore()
+    for d in devs:
+        pl.semaphore_signal(bar, inc=1, device_id=d, device_id_type=MESH)
+    pl.semaphore_wait(bar, len(devs))
+
+def k1_body(w_ref, g_ref, c_ref, small_ref, W, G, C, S,
+            own_rows, own_cols, own_cot, rw, rg, rc, rs, sw, swd, sg, sgd, sc, ss, loc):
+    r, s, x, c, z, y = topo()
+    cp, xp = (r + 1 - 2 * c, s), ((r + 2) % 4, s)
+    rcp, rxp = r + 1 - 2 * c, (r + 2) % 4
+    greet([cp, xp] + [(r, (s + k) % 8) for k in range(1, 8)])
+    def wq(t, q):
+        return W.at[pl.ds(pl.multiple_of(192 * t + 48 * q, 16), 48)]
+    def gq(t, q):
+        return G.at[pl.ds(pl.multiple_of(192 * t + 48 * q, 16), 48)]
+    def cb(t):
+        return C.at[pl.ds(pl.multiple_of(128 * t, 128), 128)]
+    own_w = w_ref.at[pl.ds(pl.multiple_of(48 * r, 16), 48)]
+    yp, up, dn = (r, s + 1 - 2 * y), (r, s + 2), (r, s - 2)
+    def plane(src_w, src_c, t, zz, go_up, go_dn):
+        def send(dev, d):
+            rcopy(src_w, wq(t, r), sw.at[zz, d], rw.at[t, r], dev).start()
+            rcopy(src_c, cb(t), sc.at[zz, d], rc.at[t], dev).start()
+        if go_up is not None:
+            pl.when(go_up)(lambda: send(up, 0))
+        if go_dn is not None:
+            pl.when(go_dn)(lambda: send(dn, 1))
+        send(yp, 2)
+    to_vmem = (
+        pltpu.make_async_copy(w_ref, own_rows, loc.at[0]),
+        pltpu.make_async_copy(g_ref.at[s], own_cols, loc.at[1]),
+        pltpu.make_async_copy(c_ref, own_cot, loc.at[2]),
+    )
+    own = pl.ds(pl.multiple_of(192 * s, 16), 192)
+    to_hbm = (
+        pltpu.make_async_copy(own_rows, W.at[own], loc.at[3]),
+        pltpu.make_async_copy(own_cols, G.at[own], loc.at[4]),
+        pltpu.make_async_copy(own_cot, cb(s), loc.at[5]),
+    )
+    for copy in to_vmem:
+        copy.start()
+    plane(own_w, c_ref, s, z, z < 3, z > 0)
+    for k in range(1, 8):
+        t = (s + k) % 8
+        rcopy(small_ref, S.at[s], ss.at[t], rs.at[s], (r, t)).start()
+        rcopy(g_ref.at[t, pl.ds(pl.multiple_of(48 * r, 16), 48)], gq(s, r), sg.at[t], rg.at[s, r], (r, t)).start()
+    S[s] = small_ref[...]
+    for near, far in zip(to_vmem, to_hbm):
+        near.wait()
+        far.start()
+    def wait_w(t, q):
+        rcopy(wq(t, q), wq(t, q), sw.at[0, 0], rw.at[t, q], cp).wait_recv()
+    def wait_g(t, q):
+        rcopy(gq(t, q), gq(t, q), sg.at[0], rg.at[t, q], cp).wait_recv()
+    def wait_c(t):
+        rcopy(cb(t), cb(t), sg.at[0], rc.at[t], cp).wait_recv()
+    def share(view, t, sems, rsems):
+        rcopy(view(t, r), view(t, r), sems.at[t, 0], rsems.at[t, r], xp).start()
+        rcopy(view(t, r), view(t, r), sems.at[t, 1], rsems.at[t, r], cp).start()
+    for k in (1, 2, 3):
+        def below():
+            t = s - 2 * k
+            wait_w(t, r); wait_c(t)
+            plane(wq(t, r), cb(t), t, z - k, z < 3, None)
+            share(wq, t, swd, rw)
+        def above():
+            t = s + 2 * k
+            wait_w(t, r); wait_c(t)
+            plane(wq(t, r), cb(t), t, z + k, None, z > 0)
+            share(wq, t, swd, rw)
+        pl.when(z >= k)(below)
+        pl.when(z + k <= 3)(above)
+    @pl.loop(0, 4)
+    def _(zz):
+        t = 2 * zz + 1 - y
+        wait_w(t, r)
+        share(wq, t, swd, rw)
+    @pl.loop(1, 8)
+    def _(k):
+        t = (s + k) % 8
+        wait_g(t, r)
+        share(gq, t, sgd, rg)
+    @pl.loop(1, 8)
+    def _(k):
+        t = (s + k) % 8
+        wait_w(t, rxp)
+        rcopy(wq(t, rxp), wq(t, rxp), swd.at[t, 2], rw.at[t, rxp], cp).start()
+    @pl.loop(1, 8)
+    def _(k):
+        t = (s + k) % 8
+        wait_g(t, rxp)
+        rcopy(gq(t, rxp), gq(t, rxp), sgd.at[t, 2], rg.at[t, rxp], cp).start()
+    @pl.loop(0, 4)
+    def _(zz):
+        wait_c(2 * zz + 1 - y)
+    @pl.loop(1, 8)
+    def _(k):
+        t = (s + k) % 8
+        rcopy(small_ref, S.at[t], ss.at[t], rs.at[t], cp).wait_recv()
+        rcopy(small_ref, S.at[t], ss.at[t], rs.at[t], cp).wait_send()
+        rcopy(gq(s, r), gq(s, r), sg.at[t], rg.at[s, r], cp).wait_send()
+        for q in (rcp, 3 - r):
+            wait_w(t, q)
+            wait_g(t, q)
+        for d in range(3):
+            rcopy(wq(t, r), wq(t, r), swd.at[t, d], rw.at[t, r], cp).wait_send()
+            rcopy(gq(t, r), gq(t, r), sgd.at[t, d], rg.at[t, r], cp).wait_send()
+    def sent(zz, d):
+        rcopy(own_w, own_w, sw.at[zz, d], rw.at[s, r], cp).wait_send()
+        rcopy(c_ref, c_ref, sc.at[zz, d], rc.at[s], cp).wait_send()
+    for zz in range(4):
+        sent(zz, 2)
+        pl.when((zz <= z) & (z < 3))(lambda: sent(zz, 0))
+        pl.when((zz >= z) & (z > 0))(lambda: sent(zz, 1))
+    for copy in to_hbm:
+        copy.wait()
+
+def k1(w, g, c, small):
+    A = pl.BlockSpec(memory_space=pl.ANY)
+    V = pl.BlockSpec(memory_space=pltpu.VMEM)
+    D = pltpu.SemaphoreType.DMA
+    return pl.pallas_call(
+        k1_body,
+        out_shape=(jax.ShapeDtypeStruct((1536, 3584), jnp.bfloat16), jax.ShapeDtypeStruct((1536, 2304), jnp.bfloat16),
+                   jax.ShapeDtypeStruct((1024, 1536), jnp.bfloat16), jax.ShapeDtypeStruct((8, 16, 128), jnp.bfloat16)),
+        in_specs=[A, A, A, V], out_specs=(A, A, A, V),
+        scratch_shapes=[pltpu.VMEM((192, 3584), BF), pltpu.VMEM((192, 2304), BF), pltpu.VMEM((128, 1536), BF), D((8, 4)), D((8, 4)), D((8,)), D((8,)), D((4, 3)), D((8, 3)), D((8,)), D((8, 3)), D((4, 3)), D((8,)), D((6,))],
+        compiler_params=pltpu.CompilerParams(collective_id=0, has_side_effects=True, vmem_limit_bytes=16 << 20), name="gather_weights",
+    )(w, g, c, small)
+
+
+def al(v, m): return pl.multiple_of(v, m)
+def dot(a, b): return lax.dot_general(a, b, (((1,), (0,)), ((), ())), preferred_element_type=F32)
+def dot_nt(a, b): return lax.dot_general(a, b, (((1,), (1,)), ((), ())), preferred_element_type=F32)
+
+def kb_body(n_ref, c_hbm, g_hbm, d_hbm, DS, OS, OG, OD,
+            vG, vD, vC, N, NT, MX, MT, H, PD, PO, YD, YO, ZD, ZO, GD, RCd, RXd, RC, RX,
+            rn, syn, szn, ryd, ryo, rzd, rzo, syd, szd, syo, szo,
+            scd, rcd, sxd, rxd, sfd, rfd, scg, rcg, sxg, rxg, sag, rag, sfg, loc):
+    r, s, x, c, z, y = topo()
+    cp, xp, yp = (r + 1 - 2 * c, s), ((r + 2) % 4, s), (r, s + 1 - 2 * y)
+    rcp, rxp, rdp = r + 1 - 2 * c, (r + 2) % 4, 3 - r
+    greet([cp, xp] + [(r, (s + k) % 8) for k in range(1, 8)])
+    def wr(ref, sem): rcopy(ref, ref, loc.at[0], sem, cp).wait_recv()
+    def ws(ref, sem): rcopy(ref, ref, sem, loc.at[0], cp).wait_send()
+    def line(k):
+        return (z + (1 - 2 * (z % 2)) * (k % 2) + (k // 2) * (2 - 4 * (z // 2)))
+    def nb(t): return N.at[pl.ds(al(128 * t, 128), 128)]
+    loads = [pltpu.make_async_copy(c_hbm, vC, loc.at[1]), pltpu.make_async_copy(g_hbm, vG, loc.at[2]),
+             pltpu.make_async_copy(d_hbm, vD, loc.at[3])]
+    l0 = pltpu.make_async_copy(n_ref, nb(s), loc.at[4])
+    l0.start()
+    rcopy(n_ref, nb(s), syn.at[z], rn.at[s], yp).start()
+    for k in (1, 2, 3):
+        zz = line(k)
+        rcopy(n_ref, nb(s), szn.at[zz], rn.at[s], (r, 2 * zz + y)).start()
+    for l in loads: l.start()
+    l0.wait()
+    for l in loads: l.wait()
+
+    def add_d(k):
+        zz = line(k)
+        t = 2 * zz + y
+        wr(YD.at[zz], ryd.at[zz])
+        PD[t] = (PD[t].astype(F32) + YD[zz].astype(F32)).astype(BF)
+    def send_d(k):
+        zz = line(k)
+        t = 2 * zz + y
+        rcopy(PD.at[t], ZD.at[z], szd.at[zz], rzd.at[z], (r, t)).start()
+
+    @pl.loop(0, 4)
+    def _(k):
+        zz = line(k)
+        @pl.when(k < 3)
+        def _():
+            zn = line(k + 1)
+            t = 2 * zn + y
+            wr(nb(t), rn.at[t])
+            rcopy(nb(t), nb(t), syn.at[zn], rn.at[t], yp).start()
+        to = 2 * zz + 1 - y
+        wr(nb(to), rn.at[to])
+        rows = pl.ds(al(256 * zz, 256), 256)
+        X = N[rows]
+        NT[:, rows] = X.T
+        Cp = vC[rows]
+        for j in range(3):
+            ga, ua = pl.ds(384 * j, 384), pl.ds(1152 + 384 * j, 384)
+            g = dot(X, vG[:, ga])
+            u = dot(X, vG[:, ua])
+            dm = dot_nt(Cp, vD[ga])
+            sg = jax.nn.sigmoid(g)
+            act = g * sg
+            du = dm * u
+            MX[:, ga] = (act * u).astype(BF)
+            H[rows, ga] = (du * sg + du * act * (1.0 - sg)).astype(BF)
+            H[rows, ua] = (dm * act).astype(BF)
+        for j in range(3):
+            co = pl.ds(512 * j, 512)
+            d = dot_nt(H[rows], vG[co]).astype(BF)
+            PD[2 * zz, :, co] = d[:128]
+            PD[2 * zz + 1, :, co] = d[128:]
+        rcopy(PD.at[to], YD.at[zz], syd.at[zz], ryd.at[zz], yp).start()
+        for j in range(3):
+            co = pl.ds(512 * j, 512)
+            o = dot(MX[...], vD[:, co]).astype(BF)
+            PO[2 * zz, :, co] = o[:128]
+            PO[2 * zz + 1, :, co] = o[128:]
+        MT[:, rows] = MX[...].T
+        @pl.when(k >= 1)
+        def _():
+            add_d(k - 1)
+        @pl.when(k >= 2)
+        def _():
+            send_d(k - 1)
+    for k in range(4):
+        zz = line(k)
+        to = 2 * zz + 1 - y
+        rcopy(PO.at[to], YO.at[zz], syo.at[zz], ryo.at[zz], yp).start()
+
+    def dch(i): return pl.ds(al(288 * i, 16), 288)
+    def qc(q): return pl.ds(al(384 * q, 128), 384)
+    def d1(i):
+        for j in range(3):
+            co = pl.ds(512 * j, 512)
+            GD[dch(i), co] = dot(MT[dch(i)], vC[:, co]).astype(BF)
+        for xx in range(2):
+            q = 2 * xx + 1 - c
+            rcopy(GD.at[dch(i), qc(q)], RCd.at[xx, dch(i)], scd.at[i, xx], rcd.at[i, xx], cp).start()
+    def d2(i):
+        for xx in range(2):
+            wr(RCd.at[xx, dch(i)], rcd.at[i, xx])
+            q = 2 * xx + c
+            GD[dch(i), qc(q)] = (GD[dch(i), qc(q)].astype(F32) + RCd[xx, dch(i)].astype(F32)).astype(BF)
+        rcopy(GD.at[dch(i), qc(rxp)], RXd.at[dch(i)], sxd.at[i], rxd.at[i], xp).start()
+    def d3(i):
+        wr(RXd.at[dch(i)], rxd.at[i])
+        GD[dch(i), qc(r)] = (GD[dch(i), qc(r)].astype(F32) + RXd[dch(i)].astype(F32)).astype(BF)
+        src, dst = GD.at[dch(i), qc(r)], OD.at[r, dch(i)]
+        pltpu.make_async_copy(src, dst, sfd.at[i, 3]).start()
+        rcopy(src, dst, sfd.at[i, 0], rfd.at[i, r], xp).start()
+        rcopy(src, dst, sfd.at[i, 1], rfd.at[i, r], cp).start()
+    def d4(i):
+        v = OD.at[rxp, dch(i)]
+        wr(v, rfd.at[i, rxp])
+        rcopy(v, v, sfd.at[i, 2], rfd.at[i, rxp], cp).start()
+    @pl.loop(0, 6)
+    def _(i):
+        pl.when(i < 4)(lambda: d1(i))
+        pl.when((i >= 1) & (i < 5))(lambda: d2(i - 1))
+        pl.when(i >= 2)(lambda: d3(i - 2))
+        @pl.when(i == 1)
+        def _():
+            add_d(3)
+            send_d(3)
+    def own(k): return (s + 1 + k) % 8
+    def gq(t, q): return pl.ds(al(192 * t + 48 * q, 16), 48)
+    def g1(k):
+        t = own(k)
+        rows = pl.ds(al(192 * t, 16), 192)
+        for j in range(3):
+            co = pl.ds(768 * j, 768)
+            vG[rows, co] = dot(NT[rows], H[:, co]).astype(BF)
+        for xx in range(2):
+            q = 2 * xx + 1 - c
+            rcopy(vG.at[gq(t, q)], RC.at[t, xx], scg.at[t, xx], rcg.at[t, xx], cp).start()
+    def g2(k):
+        t = own(k)
+        for xx in range(2):
+            wr(RC.at[t, xx], rcg.at[t, xx])
+            q = gq(t, 2 * xx + c)
+            vG[q] = (vG[q].astype(F32) + RC[t, xx].astype(F32)).astype(BF)
+        rcopy(vG.at[gq(t, rxp)], RX.at[t], sxg.at[t], rxg.at[t], xp).start()
+    def g3(k):
+        t = own(k)
+        wr(RX.at[t], rxg.at[t])
+        q = gq(t, r)
+        vG[q] = (vG[q].astype(F32) + RX[t].astype(F32)).astype(BF)
+        @pl.when(k < 7)
+        def _():
+            rcopy(vG.at[q], OG.at[r, s], sag.at[t], rag.at[s, r], (r, t)).start()
+        @pl.when(k == 7)
+        def _():
+            pltpu.make_async_copy(vG.at[q], OG.at[r, s], loc.at[5]).start()
+    def share(t):
+        v = OG.at[r, t]
+        rcopy(v, v, sfg.at[t, 0], rag.at[t, r], xp).start()
+        rcopy(v, v, sfg.at[t, 1], rag.at[t, r], cp).start()
+    def add_o(k):
+        zz = line(k)
+        t = 2 * zz + y
+        wr(YO.at[zz], ryo.at[zz])
+        PO[t] = (PO[t].astype(F32) + YO[zz].astype(F32)).astype(BF)
+    def send_o(k):
+        zz = line(k)
+        t = 2 * zz + y
+        rcopy(PO.at[t], ZO.at[z], szo.at[zz], rzo.at[z], (r, t)).start()
+    @pl.loop(0, 10)
+    def _(i):
+        pl.when(i < 8)(lambda: g1(i))
+        pl.when((i >= 1) & (i < 9))(lambda: g2(i - 1))
+        pl.when(i >= 2)(lambda: g3(i - 2))
+        pl.when(i < 4)(lambda: d4(i))
+        pl.when(i < 4)(lambda: add_o(i))
+        pl.when((i >= 1) & (i < 4))(lambda: send_o(i))
+    pltpu.make_async_copy(vG.at[gq(s, r)], OG.at[r, s], loc.at[5]).wait()
+    share(s)
+    @pl.loop(1, 8)
+    def _(k):
+        t = (s + 8 - k) % 8
+        wr(OG.at[r, t], rag.at[t, r])
+        share(t)
+    def total(P, Z, rz, out):
+        acc = P[s].astype(F32)
+        for k in (1, 2, 3):
+            zz = line(k)
+            wr(Z.at[zz], rz.at[zz])
+            acc = acc + Z[zz].astype(F32)
+        out[...] = acc
+    total(PD, ZD, rzd, DS)
+    total(PO, ZO, rzo, OS)
+    @pl.loop(0, 8)
+    def _(k):
+        t = (s + 8 - k) % 8
+        v = OG.at[rxp, t]
+        wr(v, rag.at[t, rxp])
+        rcopy(v, v, sfg.at[t, 2], rag.at[t, rxp], cp).start()
+    @pl.loop(0, 8)
+    def _(t):
+        for q in (rcp, rdp):
+            wr(OG.at[q, t], rag.at[t, q])
+        for d in range(3):
+            ws(OG.at[r, t], sfg.at[t, d])
+        for xx in range(2):
+            ws(RC.at[t, xx], scg.at[t, xx])
+        ws(RX.at[t], sxg.at[t])
+        @pl.when(t != s)
+        def _():
+            ws(OG.at[r, s], sag.at[t])
+    @pl.loop(0, 4)
+    def _(i):
+        for q in (rcp, rdp):
+            wr(OD.at[q, dch(i)], rfd.at[i, q])
+        for d in range(4):
+            ws(OD.at[r, dch(i)], sfd.at[i, d])
+        for xx in range(2):
+            ws(RCd.at[xx, dch(i)], scd.at[i, xx])
+        ws(RXd.at[dch(i)], sxd.at[i])
+        ws(nb(s), syn.at[i])
+        ws(YD.at[i], syd.at[i])
+        ws(YO.at[i], syo.at[i])
+        @pl.when(i != z)
+        def _():
+            ws(nb(s), szn.at[i])
+            ws(ZD.at[i], szd.at[i])
+            ws(ZO.at[i], szo.at[i])
+
+def kb(n2, C, G, Dn):
+    A = pl.BlockSpec(memory_space=pl.ANY)
+    V = pl.BlockSpec(memory_space=pltpu.VMEM)
+    D = pltpu.SemaphoreType.DMA
+    sh = lambda a, b=BF: jax.ShapeDtypeStruct(a, b)
+    vm = lambda *a: pltpu.VMEM(a, BF)
+    return pl.pallas_call(
+        kb_body,
+        out_shape=(sh((128, 1536), F32), sh((128, 1536), F32), sh((4, 8, 48, 2304)), sh((4, 1152, 384))),
+        in_specs=[A] * 4, out_specs=(V, V, A, A),
+        scratch_shapes=[vm(1536, 2304), vm(1152, 1536), vm(1024, 1536), vm(1024, 1536), vm(1536, 1024), vm(256, 1152), vm(1152, 1024),
+                        vm(1024, 2304), vm(8, 128, 1536), vm(8, 128, 1536)] + [vm(4, 128, 1536)] * 4 +
+                       [vm(1152, 1536), vm(2, 1152, 384), vm(1152, 384), vm(8, 2, 48, 2304), vm(8, 48, 2304)] +
+                       [D((8,)), D((4,)), D((4,))] + [D((4,))] * 8 +
+                       [D((4, 2)), D((4, 2)), D((4,)), D((4,)), D((4, 4)), D((4, 4)),
+                        D((8, 2)), D((8, 2)), D((8,)), D((8,)), D((8,)), D((8, 4)), D((8, 3)), D((6,))],
+        compiler_params=pltpu.CompilerParams(collective_id=1, has_side_effects=True, vmem_limit_bytes=63 << 20), name="feed_forward",
+    )(n2, C, G, Dn)
+
+
+def k4_body(w_ref, OW, V, RC, RX, Y, Z, scw, rcw, sxw, rxw, syw, ryw, szw, rzw, sfw, rfw, loc):
+    r, s, x, c, z, y = topo()
+    cp, xp, yp = (r + 1 - 2 * c, s), ((r + 2) % 4, s), (r, s + 1 - 2 * y)
+    rcp, rxp, rdp = r + 1 - 2 * c, (r + 2) % 4, 3 - r
+    def wr(ref, sem): rcopy(ref, ref, loc.at[0], sem, cp).wait_recv()
+    def ws(ref, sem): rcopy(ref, ref, sem, loc.at[0], cp).wait_send()
+    load = pltpu.make_async_copy(w_ref, V, loc.at[1])
+    load.start()
+    greet([cp, xp, yp] + [(r, (s + k) % 8) for k in (2, 4, 6)])
+    load.wait()
+    def line(k):
+        return (z + (1 - 2 * (z % 2)) * (k % 2) + (k // 2) * (2 - 4 * (z // 2)))
+    def own(k):
+        return 2 * line(3 - k % 4) + (1 - y + (k // 4) * (2 * y - 1))
+    def gq(t, q): return pl.ds(al(192 * t + 48 * q, 16), 48)
+    def p1(k):
+        t = own(k)
+        for xx in range(2):
+            rcopy(V.at[gq(t, 2 * xx + 1 - c)], RC.at[t, xx], scw.at[t, xx], rcw.at[t, xx], cp).start()
+    def p2(k):
+        t = own(k)
+        for xx in range(2):
+            wr(RC.at[t, xx], rcw.at[t, xx])
+            q = gq(t, 2 * xx + c)
+            V[q] = (V[q].astype(F32) + RC[t, xx].astype(F32)).astype(BF)
+        rcopy(V.at[gq(t, rxp)], RX.at[t], sxw.at[t], rxw.at[t], xp).start()
+    def p3(k):
+        t = own(k)
+        wr(RX.at[t], rxw.at[t])
+        q = gq(t, r)
+        V[q] = (V[q].astype(F32) + RX[t].astype(F32)).astype(BF)
+        @pl.when(k < 4)
+        def _():
+            rcopy(V.at[q], Y.at[t // 2], syw.at[t // 2], ryw.at[t // 2], yp).start()
+        @pl.when(k >= 4)
+        def _():
+            wr(Y.at[t // 2], ryw.at[t // 2])
+            V[q] = (V[q].astype(F32) + Y[t // 2].astype(F32)).astype(BF)
+        @pl.when((k >= 4) & (k < 7))
+        def _():
+            rcopy(V.at[q], Z.at[z], szw.at[t // 2], rzw.at[z], (r, t)).start()
+    @pl.loop(0, 8)
+    def _(k): p1(k)
+    @pl.loop(0, 9)
+    def _(i):
+        pl.when(i < 8)(lambda: p2(i))
+        pl.when(i >= 1)(lambda: p3(i - 1))
+    acc = V[gq(s, r)].astype(F32)
+    for k in (1, 2, 3):
+        zz = line(k)
+        wr(Z.at[zz], rzw.at[zz])
+        acc = acc + Z[zz].astype(F32)
+    OW[r] = acc.astype(BF)
+    rcopy(OW.at[r], OW.at[r], sfw.at[0], rfw.at[r], xp).start()
+    rcopy(OW.at[r], OW.at[r], sfw.at[1], rfw.at[r], cp).start()
+    wr(OW.at[rxp], rfw.at[rxp])
+    rcopy(OW.at[rxp], OW.at[rxp], sfw.at[2], rfw.at[rxp], cp).start()
+    wr(OW.at[rcp], rfw.at[rcp])
+    wr(OW.at[rdp], rfw.at[rdp])
+    for d in range(3):
+        ws(OW.at[r], sfw.at[d])
+    @pl.loop(0, 8)
+    def _(t):
+        for xx in range(2):
+            ws(RC.at[t, xx], scw.at[t, xx])
+        ws(RX.at[t], sxw.at[t])
+    @pl.loop(0, 4)
+    def _(i):
+        ws(Y.at[i], syw.at[i])
+        @pl.when(i != z)
+        def _():
+            ws(Z.at[i], szw.at[i])
+
+def k4(w):
+    A = pl.BlockSpec(memory_space=pl.ANY)
+    V = pl.BlockSpec(memory_space=pltpu.VMEM)
+    D = pltpu.SemaphoreType.DMA
+    vm = lambda *a: pltpu.VMEM(a, BF)
+    wide = w.shape[1]
+    return pl.pallas_call(
+        k4_body,
+        out_shape=jax.ShapeDtypeStruct((4, 48, wide), BF),
+        in_specs=[A], out_specs=V,
+        scratch_shapes=[vm(1536, wide), vm(8, 2, 48, wide), vm(8, 48, wide), vm(4, 48, wide), vm(4, 48, wide),
+                        D((8, 2)), D((8, 2)), D((8,)), D((8,)), D((4,)), D((4,)), D((4,)), D((4,)), D((3,)), D((4,)), D((2,))],
+        compiler_params=pltpu.CompilerParams(collective_id=2, has_side_effects=True, vmem_limit_bytes=50 << 20), name="attention_gradients",
+    )(w)
 
 
 def to_columns(rows):
@@ -267,6 +746,175 @@
     )
 
 
+def shards_eight(
+    tokens, segments, gain_attn, w_qkv, b_qkv, w_out, gain_ffn, w_gate, w_up, w_down, cotangent
+):
+    heads_per_group = QUERY_HEADS // KEY_VALUE_HEADS
+    head_dimension = QUERY_HEADS * HEAD_DIMENSION
+    key_value_limit = head_dimension + KEY_VALUE_HEADS * HEAD_DIMENSION
+    logit_scale = HEAD_DIMENSION ** (-0.5)
+    token_length = tokens.shape[1]
+    small = jnp.concatenate([gain_attn, b_qkv, gain_ffn]).reshape(5, 128)
+    columns = jnp.concatenate(
+        [
+            jnp.pad(w.reshape(192, 8, 1120).transpose(1, 0, 2), ((0, 0), (0, 0), (0, 32)))
+            for w in (w_gate, w_up)
+        ],
+        axis=2,
+    )
+    attn_full, gate_up, all_cot, smalls = k1(
+        jnp.concatenate([w_qkv, w_out], axis=1),
+        columns,
+        cotangent[0],
+        jnp.pad(small, ((0, 11), (0, 0))),
+    )
+    smalls = smalls[:, :5].reshape(8, 640)
+    full_gain_attn = smalls[:, :192].reshape(-1)
+    full_bias = smalls[:, 192:448].reshape(-1)
+    full_gain_ffn = smalls[:, 448:].reshape(-1)
+    full_qkv, full_out = attn_full[:, :2048], attn_full[:, 2048:]
+    gain_first = full_gain_attn.astype(jnp.float32)
+    gain_second = full_gain_ffn.astype(jnp.float32)
+    cosine, sine_vals, allowed = tables(segments[0], HEAD_DIMENSION)
+    cosine_per_head = cosine[:, None, :]
+    sine_per_head = sine_vals[:, None, :]
+    inputs = tokens[0].astype(jnp.float32)
+    normed_first, unit_first, rstd_first = norm_forward(inputs, gain_first)
+    acts_first = normed_first.astype(jnp.bfloat16)
+    joined_projection = jnp.dot(
+        acts_first, full_qkv, preferred_element_type=jnp.float32
+    ) + full_bias.astype(jnp.float32)
+    query_rows = apply_rotation(
+        joined_projection[:, :head_dimension].reshape(token_length, QUERY_HEADS, HEAD_DIMENSION),
+        cosine_per_head,
+        sine_per_head,
+    )
+    query_reduced = (
+        (query_rows * logit_scale)
+        .astype(jnp.bfloat16)
+        .reshape(token_length, KEY_VALUE_HEADS, heads_per_group, HEAD_DIMENSION)
+    )
+    k_low = apply_rotation(
+        joined_projection[:, head_dimension:key_value_limit].reshape(
+            token_length, KEY_VALUE_HEADS, HEAD_DIMENSION
+        ),
+        cosine_per_head,
+        sine_per_head,
+    ).astype(jnp.bfloat16)
+    value_reduced = (
+        joined_projection[:, key_value_limit:]
+        .reshape(token_length, KEY_VALUE_HEADS, HEAD_DIMENSION)
+        .astype(jnp.bfloat16)
+    )
+    scores = jnp.einsum("ikrd,jkd->krij", query_reduced, k_low, preferred_element_type=jnp.float32)
+    scores = jnp.where(allowed != 0, scores, -1e30)
+    largest = jnp.max(scores, axis=-1, keepdims=True)
+    exponents = jnp.exp(scores - largest)
+    soft_probs = exponents / jnp.sum(exponents, axis=-1, keepdims=True)
+    soft_low = soft_probs.astype(jnp.bfloat16)
+    attended = jnp.einsum(
+        "krij,jkd->ikrd", soft_low, value_reduced, preferred_element_type=jnp.float32
+    )
+    attended = attended.reshape(token_length, head_dimension).astype(jnp.bfloat16)
+    hidden_mid = inputs + jnp.dot(attended, full_out, preferred_element_type=jnp.float32)
+    normed_second, unit_second, rstd_second = norm_forward(hidden_mid, gain_second)
+    acts_second = normed_second.astype(jnp.bfloat16)
+    d_normed_second, down_sum, gate_up_rows, down_rows = kb(
+        acts_second, all_cot, gate_up, jnp.pad(w_down, ((0, 32), (0, 0)))
+    )
+    result = (hidden_mid + down_sum).astype(jnp.bfloat16)
+    grad_out = cotangent[0]
+    gate_up_rows = gate_up_rows.transpose(0, 2, 1, 3).reshape(192, 8, 2304)
+    gate_grad = gate_up_rows[:, :, :1120].reshape(192, 8960)
+    up_grad = gate_up_rows[:, :, 1152:2272].reshape(192, 8960)
+    down_grad = down_rows.transpose(1, 0, 2)[:1120].reshape(1120, 1536)
+    gain_second_grad = jnp.sum(d_normed_second * unit_second, axis=0)
+    d_hidden_mid = grad_out.astype(jnp.float32) + norm_backward(
+        d_normed_second, gain_second, unit_second, rstd_second
+    )
+    d_branch = d_hidden_mid.astype(jnp.bfloat16)
+    out_grad_term = jnp.einsum("le,ld->ed", attended, d_branch, preferred_element_type=jnp.float32)
+    attended_gradient = jnp.einsum(
+        "ld,ed->le", d_branch, full_out, preferred_element_type=jnp.float32
+    )
+    attended_gradient = attended_gradient.astype(jnp.bfloat16).reshape(
+        token_length, KEY_VALUE_HEADS, heads_per_group, HEAD_DIMENSION
+    )
+    d_probs = jnp.einsum(
+        "ikrd,jkd->krij", attended_gradient, value_reduced, preferred_element_type=jnp.float32
+    )
+    value_gradient = jnp.einsum(
+        "krij,ikrd->jkd", soft_low, attended_gradient, preferred_element_type=jnp.float32
+    )
+    d_scores = soft_probs * (d_probs - jnp.sum(soft_probs * d_probs, axis=-1, keepdims=True))
+    d_scores_low = d_scores.astype(jnp.bfloat16)
+    d_queries = jnp.einsum(
+        "krij,jkd->ikrd", d_scores_low, k_low, preferred_element_type=jnp.float32
+    )
+    d_queries = rotate_back(
+        d_queries.reshape(token_length, QUERY_HEADS, HEAD_DIMENSION) * logit_scale,
+        cosine_per_head,
+        sine_per_head,
+    )
+    key_gradient = jnp.einsum(
+        "krij,ikrd->jkd", d_scores_low, query_reduced, preferred_element_type=jnp.float32
+    )
+    key_gradient = rotate_back(key_gradient, cosine_per_head, sine_per_head)
+    d_joined = jnp.concatenate(
+        [
+            d_queries.reshape(token_length, head_dimension),
+            key_gradient.reshape(token_length, KEY_VALUE_HEADS * HEAD_DIMENSION),
+            value_gradient.reshape(token_length, KEY_VALUE_HEADS * HEAD_DIMENSION),
+        ],
+        axis=1,
+    ).astype(jnp.bfloat16)
+    bias_grad_term = jnp.sum(d_joined.astype(jnp.float32), axis=0)
+    qkv_grad_term = jnp.einsum(
+        "ld,le->de", acts_first, d_joined, preferred_element_type=jnp.float32
+    )
+    d_normed_first = jnp.einsum("le,de->ld", d_joined, full_qkv, preferred_element_type=jnp.float32)
+    gain_first_grad = jnp.sum(d_normed_first * unit_first, axis=0)
+    d_inputs = d_hidden_mid + norm_backward(d_normed_first, gain_first, unit_first, rstd_first)
+    small_terms = jnp.concatenate(
+        [
+            gain_first_grad.reshape(8, 192),
+            bias_grad_term.reshape(8, 256),
+            gain_second_grad.reshape(8, 192),
+        ],
+        axis=1,
+    )
+    small_terms = jnp.pad(small_terms.reshape(8, 5, 128), ((0, 0), (0, 187), (0, 0))).reshape(1536, 128)
+    owned = k4(
+        jnp.concatenate([t.astype(jnp.bfloat16) for t in (qkv_grad_term, out_grad_term, small_terms)], axis=1)
+    ).reshape(192, 3712)
+    small_rows = owned[:5, 3584:].reshape(640)
+    summed = tuple(
+        part.astype(jnp.float32)
+        for part in (
+            small_rows[:192],
+            owned[:, :2048],
+            small_rows[192:448],
+            owned[:, 2048:3584],
+            small_rows[448:],
+            gate_grad,
+            up_grad,
+            down_grad,
+        )
+    )
+    return (
+        result[None],
+        d_inputs.astype(jnp.bfloat16)[None],
+        summed[0],
+        summed[1],
+        summed[2],
+        summed[3],
+        summed[4],
+        summed[5],
+        summed[6],
+        summed[7],
+    )
+
+
 def solution(mesh):
     placed = (
         P(("replica", "shard"), None, None),
@@ -282,7 +930,7 @@
         P(("replica", "shard"), None, None),
     )
     return jax.shard_map(
-        shards,
+        shards_eight if (mesh.shape["replica"], mesh.shape["shard"]) == (4, 8) else shards,
         mesh=mesh,
         in_specs=placed,
         out_specs=(

time: 1200 us -> 606 us (0.51)
  waiting for transfers between devices: 693 us -> 0 us
  Pallas kernels: 0 us -> 464 us
  blocking collectives: 267 us -> 0 us
  matrix products: 107 us -> 24.7 us
  local copies, waits for them, and re-layouts: 58.6 us -> 80.3 us
  between operations: 16.5 us -> 1.26 us
  starting transfers between devices: 13.5 us -> 0 us
    pallas_call x0 -> x3, Pallas kernels: none -> 464 us  [the longest x1 200 us: kb(): pl.pallas_call(kb_body, out_shape=(sh((128, 1536), F32), sh((128, 1536),...]
    reduce_scatter x4 -> x0, waiting for transfers between devices: 309 us -> none  [the longest x1 122 us: shards(): lax.psum_scatter(qkv_grad_term.astype(jnp.bfloat16), 'shard', scatter_dim...]
    psum x1 -> x0, waiting for transfers between devices: 213 us -> none  [shards(): lax.psum(owned[1].astype(jnp.bfloat16), 'replica').astype(jnp.float32)]
    all_gather x6 -> x0, waiting for transfers between devices: 169 us -> none  [the longest x1 99.8 us: shards(): all_acts = lax.all_gather(acts_second, 'shard', axis=0, tiled=True)]
    unnamed x2 -> x0, blocking collectives: 145 us -> none
    dot_general x20 -> x11, matrix products: 105 us -> 23.4 us  [the longest x1 5.15 us: shards_eight(): jnp.einsum('le,de->ld', d_joined, full_qkv, preferred_element_type=jnp.fl...]
    all_gather x1 -> x0, blocking collectives: 63.1 us -> none  [shards(): lax.all_gather(b_qkv, 'shard', axis=0, tiled=True)]
    all_to_all x2 -> x0, blocking collectives: 53.5 us -> none  [to_rows(): part = lax.all_to_all(part, 'shard', 0, 0, tiled=True)]
  transfers between devices with their start and end apart: 13 -> 0, of which waited for: 8 -> 0; matrix products, arithmetic and copies ran while one was open for 13% -> 0% of each run, Pallas kernels for 0% -> 0%
where the time goes in v2:
time: 606 us; the launch traced here: 604 us
  Pallas kernels  464 us (77%)
  local copies, waits for them, and re-layouts  80.3 us (13%)
  other arithmetic  33.2 us (5%)
  matrix products  24.7 us (4%)
    pallas_call x1, Pallas kernels, kb(): pl.pallas_call(kb_body, out_shape=(sh((128, 1536), F32), sh((128, 1536),...  200 us
    pallas_call x1, Pallas kernels, k1(): pl.pallas_call(k1_body, out_shape=(jax.ShapeDtypeStruct((1536, 3584), jnp...  168 us
    pallas_call x1, Pallas kernels, k4(): pl.pallas_call(k4_body, out_shape=jax.ShapeDtypeStruct((4, 48, wide), BF)...  96.6 us
    convert_element_type x3, local copies, waits for them, and re-layouts, shards_eight(): part.astype(jnp.float32)  23.7 us
    unnamed x71, local copies, waits for them, and re-layouts  21.7 us
    reshape x2, local copies, waits for them, and re-layouts, shards_eight(): w.reshape(192, 8, 1120).transpose(1, 0, 2)  17.4 us
    convert_element_type x6, other arithmetic, shards_eight(): part.astype(jnp.float32)  16.2 us

profile of v2, /device:TPU:0, one launch (start us, length us, event | category | flops | bytes accessed | tf_op | source)
XLA Modules:
  0.0 603.6 jit_solution(12424233016581024525)
XLA Ops:
  0.6 0.8 convert_reduce_fusion
  1.5 1.2 fusion.36
  2.7 0.8 maximum_bitcast_fusion.1
  3.4 0.8 convert_compare_fusion
  4.3 0.2 multiply_cosine_fusion
  4.5 0.6 broadcast_multiply_fusion.1
  5.1 1.4 pad_maximum_fusion.1.w_ref
  6.5 8.7 %reshape.172 = bf16[192,8,1120]{2,1,0:T(8,128)(2,1)} reshape(bf16[192,8960]{1,0:T(8,128)(2,1)} %param.18) | data formatting | bytes 6881280 | tf_op jit(solution)/shard_map/reshape | solution.py:760
  15.2 8.7 %reshape.173 = bf16[192,8,1120]{2,1,0:T(8,128)(2,1)} reshape(bf16[192,8960]{1,0:T(8,128)(2,1)} %param.19) | data formatting | bytes 6881280 | tf_op jit(solution)/shard_map/reshape | solution.py:760
  23.9 4.3 copy_bitcast_fusion
  28.3 0.7 fusion.3.g_ref
  28.9 1.3 copy-done.7
  30.3 2.0 pad.23.d_hbm
  32.3 167.5 %gather_weights.1 = (bf16[1536,3584]{1,0:T(8,128)(2,1)S(1)}, bf16[1536,2304]{1,0:T(8,128)(2,1)S(1)}, bf16[1024,1536]{1,0:T(8,128)(2,1)S(1)}, bf16[8,16,128]{2,1,0:T(8,128)(2,1)S(1)}) custom-call(bf16[192,3584]{1,0:T(8,128)(2,1)S(1)} %pad_maximum_fusion.1.w_ref, bf16[8,192,2304]{2,1,0:T(8,128)(2,1)S(1)} %fusion.3.g_ref, bf16[128,1536]{1,0:T(8,128)(2,1)S(1)} %bitcast.125, ...), custom_call_target="tpu_custom_call" | custom-call | tf_op jit(solution)/shard_map/gather_weights/pallas_call | solution.py:205
  199.8 2.9 copy-done
  202.7 1.7 copy-done.1
  204.4 4.2 copy-done.3
  208.6 0.1 convert_bitcast_fusion
  208.9 0.6 copy-done.19
  209.5 3.8 fusion.15
  213.4 0.9 copy-done.14
  214.3 1.2 slice.111
  215.5 0.3 copy.43
  215.8 0.1 copy.79
  216.0 0.1 fusion.39
  216.2 1.3 fusion.62
  217.5 0.6 convolution_convert_fusion.2
  218.1 0.7 copy-done.12
  218.9 3.2 multiply_reduce_fusion.3
  222.1 0.8 copy-done.4
  223.0 0.5 copy-done.28
  223.5 0.9 multiply_convert_fusion.1.n_ref
  224.4 200.0 %feed_forward.1 = (f32[128,1536]{1,0:T(8,128)}, f32[128,1536]{1,0:T(8,128)}, bf16[4,8,48,2304]{3,2,1,0:T(8,128)(2,1)}, bf16[4,1152,384]{2,1,0:T(8,128)(2,1)}) custom-call(bf16[128,1536]{1,0:T(8,128)(2,1)} %multiply_convert_fusion.1.n_ref, bf16[1024,1536]{1,0:T(8,128)(2,1)} %copy-done.1, bf16[1536,2304]{1,0:T(8,128)(2,1)} %copy-done, ...), custom_call_target="tpu_custom_call" | custom-call | tf_op jit(solution)/shard_map/feed_forward/pallas_call | solution.py:446
  424.5 8.3 %copy.57 = bf16[4,48,8,2304]{3,2,1,0:T(8,128)(2,1)} copy(bf16[4,48,8,2304]{3,1,2,0:T(8,128)(2,1)} %bitcast.128) | data formatting | bytes 14155776 | tf_op jit(solution)/shard_map/transpose | solution.py:827
  432.8 0.3 multiply_reduce_fusion
  433.1 0.7 reshape.186
  433.8 2.2 multiply_add_fusion
  436.0 4.1 fusion.18
  440.0 0.2 copy.49
  440.3 1.6 fusion.28
  441.9 1.1 multiply_reduce_fusion.1
  443.1 0.1 multiply_convert_fusion
  443.2 0.3 broadcast_multiply_fusion
  443.5 0.2 fusion.63
  444.0 0.1 fusion.41
  444.2 5.2 fusion.35
  449.3 0.1 reshape.184
  449.4 1.0 fusion.43
  450.4 0.2 fusion.59
  450.7 0.1 maximum_bitcast_fusion
  450.9 1.4 convolution_convert_fusion.1
  452.2 1.9 convolution_convert_fusion
  454.1 5.0 pad_maximum_fusion.w_ref
  459.1 96.6 %attention_gradients.1 = bf16[4,48,3712]{2,1,0:T(8,128)(2,1)S(1)} custom-call(bf16[1536,3712]{1,0:T(8,128)(2,1)} %pad_maximum_fusion.w_ref), custom_call_target="tpu_custom_call" | custom-call | tf_op jit(solution)/shard_map/attention_gradients/pallas_call | solution.py:539
  555.7 0.6 slice_convert_fusion.9
  556.3 0.6 slice_convert_fusion.8
  557.0 1.1 slice_convert_fusion.4
  558.1 1.3 slice_convert_fusion.3
  559.5 3.3 slice_convert_fusion.2
  562.8 7.8 %copy.58 = f32[1120,4,384]{0,2,1:T(8,128)} copy(f32[1120,4,384]{2,0,1:T(8,128)} %slice_convert_fusion.2) | data formatting | bytes 13762560 | tf_op jit(solution)/shard_map/convert_element_type | solution.py:892
  570.6 8.0 %copy.59 = f32[1120,1536]{1,0:T(8,128)} copy(f32[1120,1536]{0,1:T(8,128)} %bitcast.127) | data formatting | bytes 13762560
  578.6 9.1 %slice_convert_fusion = (f32[192,8,1120]{2,1,0:T(8,128)}, f32[192,8,1120]{2,1,0:T(8,128)}) fusion(bf16[192,8,2304]{2,1,0:T(8,128)(2,1)} %bitcast.126), kind=kLoop, calls=%fused_computation.17 | loop fusion | flops 3440640 | bytes 20643840 | tf_op jit(solution)/shard_map/convert_element_type | solution.py:892
  587.7 7.9 %reshape.196 = f32[192,8960]{1,0:T(8,128)} reshape(f32[192,8,1120]{2,1,0:T(8,128)} %get-tuple-element.40) | data formatting | bytes 13762560 | tf_op jit(solution)/shard_map/convert_element_type | solution.py:892
  595.7 7.9 %reshape.195 = f32[192,8960]{1,0:T(8,128)} reshape(f32[192,8,1120]{2,1,0:T(8,128)} %get-tuple-element.41) | data formatting | bytes 13762560 | tf_op jit(solution)/shard_map/convert_element_type | solution.py:892
  (85 shorter events, 0.9 us)
Async XLA Ops:
  2.6 206.3 %copy-start.30 = (f32[128]{0:T(128)}, f32[128]{0:T(128)S(1)}, u32[]{:S(2)}) copy-start(f32[128]{0:T(128)S(1)} %add_rsqrt_fusion.1) | copy-start | bytes 1540
  4.3 213.2 %copy-start.24 = (pred[128,128]{0,1:T(8,128)(4,1)}, pred[128,128]{0,1:T(8,128)(4,1)S(1)}, u32[]{:S(2)}) copy-start(pred[128,128]{0,1:T(8,128)(4,1)S(1)} %convert_compare_fusion) | copy-start | bytes 49156
  28.3 2.0 copy-start.7
  30.2 2.0 copy-start.2
  30.2 179.3 %copy-start.6 = (bf16[1,128,1536]{2,1,0:T(8,128)(2,1)S(1)}, bf16[1,128,1536]{2,1,0:T(8,128)(2,1)}, u32[]{:S(2)}) copy-start(bf16[1,128,1536]{2,1,0:T(8,128)(2,1)} %param.11) | copy-start | bytes 1179652
  199.8 2.9 copy-start
  202.7 1.7 copy-start.1
  204.4 4.2 copy-start.3
  208.8 13.3 %copy-start.21 = (f32[1536]{0:T(1024)}, f32[1536]{0:T(1024)S(1)}, u32[]{:S(2)}) copy-start(f32[1536]{0:T(1024)S(1)} %reshape.194) | copy-start | bytes 18436
  208.9 0.6 copy-start.19
  213.3 1.0 copy-start.14
  213.4 4.7 copy-start.23
  215.9 6.2 %copy-start.17 = (bf16[128,2,128,1]{0,2,3,1:T(8,128)(2,1)}, bf16[128,2,128,1]{0,2,3,1:T(8,128)(2,1)S(1)}, u32[]{:S(2)}) copy-start(bf16[128,2,128,1]{0,2,3,1:T(8,128)(2,1)S(1)} %fusion.53) | copy-start | bytes 196612
  216.2 1.9 copy-start.10
  217.5 4.6 copy-start.26
  218.1 0.8 copy-start.12
  222.1 0.9 copy-start.4
  223.0 0.5 copy-start.28
  424.4 8.4 %copy-start.5 = (f32[128,1536]{1,0:T(8,128)S(1)}, f32[128,1536]{1,0:T(8,128)}, u32[]{:S(2)}) copy-start(f32[128,1536]{1,0:T(8,128)} %copy-done.4) | copy-start | bytes 2359300
  424.4 8.4 %copy-start.9 = (f32[128,1536]{1,0:T(8,128)S(1)}, f32[128,1536]{1,0:T(8,128)}, u32[]{:S(2)}) copy-start(f32[128,1536]{1,0:T(8,128)} %get-tuple-element.23) | copy-start | bytes 2359300
  424.5 8.4 %copy-start.22 = (f32[1536]{0:T(1024)S(1)}, f32[1536]{0:T(1024)}, u32[]{:S(2)}) copy-start(f32[1536]{0:T(1024)} %copy-done.21) | copy-start | bytes 18436
  424.5 8.3 %copy-start.29 = (f32[128]{0:T(128)S(1)}, f32[128]{0:T(128)}, u32[]{:S(2)}) copy-start(f32[128]{0:T(128)} %copy-done.28) | copy-start | bytes 1540
  436.0 6.0 copy-start.15
  436.0 6.0 copy-start.27
  440.0 3.2 copy-start.11
  440.0 3.5 copy-start.18
  440.3 3.5 copy-start.16
  443.0 1.1 copy-start.20
  443.0 1.1 copy-start.31
  444.0 5.4 copy-start.32
  444.1 6.5 %copy-start.25 = (bf16[8,192]{1,0:T(8,128)(2,1)S(1)}, bf16[8,192]{1,0:T(8,128)(2,1)}, u32[]{:S(2)}) copy-start(bf16[8,192]{1,0:T(8,128)(2,1)} %reshape.186) | copy-start | bytes 9220
  444.1 6.7 %copy-start.13 = (bf16[2,128,6,128]{3,1,2,0:T(8,128)(2,1)S(1)}, bf16[2,128,6,128]{3,1,2,0:T(8,128)(2,1)}, u32[]{:S(2)}) copy-start(bf16[2,128,6,128]{3,1,2,0:T(8,128)(2,1)} %copy-done.12) | copy-start | bytes 1179652
  459.1 100.3 %copy-start.8 = (bf16[4,1152,384]{2,1,0:T(8,128)(2,1)S(1)}, bf16[4,1152,384]{2,1,0:T(8,128)(2,1)}, u32[]{:S(2)}) copy-start(bf16[4,1152,384]{2,1,0:T(8,128)(2,1)} %get-tuple-element.25) | copy-start | bytes 10616836

commit v3 on v1

--- a/solution.py
+++ b/solution.py
@@ -3,6 +3,8 @@
 import jax
 import jax.numpy as jnp
 from jax import lax
+from jax.experimental import pallas as pl
+from jax.experimental.pallas import tpu as pltpu
 from jax.sharding import PartitionSpec as P
 
 QUERY_HEADS = 12
@@ -267,6 +269,914 @@
     )
 
 
+MESH = pl.DeviceIdType.MESH
+BF, F32 = jnp.bfloat16, jnp.float32
+HBM = pl.BlockSpec(memory_space=pl.ANY)
+VMEM = pl.BlockSpec(memory_space=pltpu.VMEM)
+DMA = pltpu.SemaphoreType.DMA
+
+
+def shaped(*shape, dtype=BF):
+    return jax.ShapeDtypeStruct(shape, dtype)
+
+
+def low(*shape):
+    return pltpu.VMEM(shape, BF)
+
+
+def full(*shape):
+    return pltpu.VMEM(shape, F32)
+
+
+def dot(a, b):
+    return lax.dot_general(a, b, (((1,), (0,)), ((), ())), preferred_element_type=F32)
+
+
+def dot_nt(a, b):
+    return lax.dot_general(a, b, (((1,), (1,)), ((), ())), preferred_element_type=F32)
+
+
+def rows_of(start, size, unit=16):
+    return pl.ds(pl.multiple_of(start, unit), size)
+
+
+def quarter(t, q):
+    return rows_of(192 * t + 48 * q, 48)
+
+
+def send(src, dst, send_sem, recv_sem, device):
+    copy = pltpu.make_async_remote_copy(
+        src_ref=src, dst_ref=dst, send_sem=send_sem, recv_sem=recv_sem, device_id=device, device_id_type=MESH
+    )
+    copy.start()
+
+
+class Place:
+    def __init__(self):
+        self.r = r = lax.axis_index("replica")
+        self.s = s = lax.axis_index("shard")
+        self.x, self.c, self.z, self.y = r // 2, r % 2, s // 2, s % 2
+        self.rc, self.rx, self.rd = r + 1 - 2 * self.c, (r + 2) % 4, 3 - r
+        self.core, self.across, self.side = (self.rc, s), (self.rx, s), (r, s + 1 - 2 * self.y)
+
+    def peer(self, t):
+        return (self.r, t)
+
+    def line(self, k):
+        return self.z + (1 - 2 * (self.z % 2)) * (k % 2) + (k // 2) * (2 - 4 * (self.z // 2))
+
+    def mine(self, zz):
+        return 2 * zz + self.y
+
+    def theirs(self, zz):
+        return 2 * zz + 1 - self.y
+
+    def greet(self, steps):
+        bar = pltpu.get_barrier_semaphore()
+        devices = [self.core, self.across] + [(self.r, (self.s + k) % 8) for k in steps]
+        for device in devices:
+            pl.semaphore_signal(bar, inc=1, device_id=device, device_id_type=MESH)
+        pl.semaphore_wait(bar, len(devices))
+
+    def arrived(self, ref, sem, spare):
+        pltpu.make_async_remote_copy(
+            src_ref=ref, dst_ref=ref, send_sem=spare, recv_sem=sem, device_id=self.core, device_id_type=MESH
+        ).wait_recv()
+
+    def sent(self, ref, sem, spare):
+        pltpu.make_async_remote_copy(
+            src_ref=ref, dst_ref=ref, send_sem=sem, recv_sem=spare, device_id=self.core, device_id_type=MESH
+        ).wait_send()
+
+
+def inverse_norm(v):
+    return lax.rsqrt(jnp.mean(v * v, axis=-1, keepdims=True) + eps_norm)
+
+
+def gather_body(
+    x_ref, cos_ref, sin_ref, allow_ref, small_ref, wq_ref, wo_ref, wg_ref, wu_ref, c_ref,
+    WQ_out, WO_out, G, C, gains, queries, keys, values, probs, att, a1, mid, a2,
+    WQ, WO, vg, vu, GS, CS, S, bias,
+    rq, ro, rg, rc, rs, szq, syq, sdq, szo, syo, sdo, sg, sdg, scz, scy, ss, loc,
+):
+    p = Place()
+    r, s, z = p.r, p.s, p.z
+    spare = loc.at[0]
+    own = rows_of(192 * s, 192)
+    own_c = rows_of(128 * s, 128, 128)
+    loads = (
+        pltpu.make_async_copy(wq_ref, WQ.at[own], loc.at[1]),
+        pltpu.make_async_copy(wo_ref, WO.at[own], loc.at[2]),
+        pltpu.make_async_copy(wg_ref, vg, loc.at[3]),
+        pltpu.make_async_copy(wu_ref, vu, loc.at[4]),
+        pltpu.make_async_copy(c_ref, CS, loc.at[5]),
+    )
+    for copy in loads:
+        copy.start()
+    p.greet(range(1, 8))
+    S[s] = small_ref[...]
+    for k in range(1, 8):
+        t = (s + k) % 8
+        send(small_ref, S.at[s], ss.at[t], rs.at[s], p.peer(t))
+
+    def in_plane(W, src, sz, sy, rw):
+        for k in (1, 2, 3):
+            zz = p.line(k)
+            send(src, W.at[quarter(s, r)], sz.at[zz], rw.at[s, r], p.peer(p.mine(zz)))
+        send(src, W.at[quarter(s, r)], sy.at[z], rw.at[s, r], p.side)
+
+    in_plane(WQ, wq_ref.at[rows_of(48 * r, 48)], szq, syq, rq)
+    in_plane(WO, wo_ref.at[rows_of(48 * r, 48)], szo, syo, ro)
+
+    def share(view, t, sems, rsems):
+        v = view(t, r)
+        send(v, v, sems.at[t, 0], rsems.at[t, r], p.across)
+        send(v, v, sems.at[t, 1], rsems.at[t, r], p.core)
+
+    def vq(t, q):
+        return WQ.at[quarter(t, q)]
+
+    def vo(t, q):
+        return WO.at[quarter(t, q)]
+
+    def gq(t, q):
+        return G.at[quarter(t, q)]
+
+    def collect(view, sy, sd, rw):
+        @pl.loop(1, 4)
+        def _(k):
+            zz = p.line(k)
+            t = p.mine(zz)
+            v = view(t, r)
+            p.arrived(v, rw.at[t, r], spare)
+            send(v, v, sy.at[zz], rw.at[t, r], p.side)
+            share(view, t, sd, rw)
+
+        @pl.loop(0, 4)
+        def _(k):
+            t = p.theirs(p.line(k))
+            p.arrived(view(t, r), rw.at[t, r], spare)
+            share(view, t, sd, rw)
+
+    def relay(view, sd, rw):
+        @pl.loop(1, 8)
+        def _(k):
+            t = (s + k) % 8
+            v = view(t, p.rx)
+            p.arrived(v, rw.at[t, p.rx], spare)
+            send(v, v, sd.at[t, 2], rw.at[t, p.rx], p.core)
+
+        @pl.loop(1, 8)
+        def _(k):
+            t = (s + k) % 8
+            p.arrived(view(t, p.rc), rw.at[t, p.rc], spare)
+            p.arrived(view(t, p.rd), rw.at[t, p.rd], spare)
+
+    for copy in loads:
+        copy.wait()
+    zeros = jnp.zeros((192, 32), BF)
+    for t in range(8):
+        GS[t, :, 0:1120] = vg[:, 1120 * t : 1120 * t + 1120]
+        GS[t, :, 1120:1152] = zeros
+        GS[t, :, 1152:2272] = vu[:, 1120 * t : 1120 * t + 1120]
+        GS[t, :, 2272:2304] = zeros
+    collect(vq, syq, sdq, rq)
+    for k in range(1, 8):
+        t = (s + k) % 8
+        send(GS.at[t, rows_of(48 * r, 48)], gq(s, r), sg.at[t], rg.at[s, r], p.peer(t))
+    own_out = (
+        pltpu.make_async_copy(GS.at[s], G.at[own], loc.at[1]),
+        pltpu.make_async_copy(CS, C.at[own_c], loc.at[2]),
+    )
+    for copy in own_out:
+        copy.start()
+
+    def cot_block(t):
+        return C.at[rows_of(128 * t, 128, 128)]
+
+    def cot_on(src, t, zz, up, down):
+        if up is not None:
+            pl.when(up)(lambda: send(src, cot_block(t), scz.at[zz, 0], rc.at[t], p.peer(s + 2)))
+        if down is not None:
+            pl.when(down)(lambda: send(src, cot_block(t), scz.at[zz, 1], rc.at[t], p.peer(s - 2)))
+        send(src, cot_block(t), scy.at[zz], rc.at[t], p.side)
+
+    def cot_step(k):
+        def below():
+            t = s - 2 * k
+            p.arrived(cot_block(t), rc.at[t], spare)
+            cot_on(cot_block(t), t, z - k, z < 3, None)
+
+        def above():
+            t = s + 2 * k
+            p.arrived(cot_block(t), rc.at[t], spare)
+            cot_on(cot_block(t), t, z + k, None, z > 0)
+
+        pl.when(z >= k)(below)
+        pl.when(z + k <= 3)(above)
+
+    collect(vo, syo, sdo, ro)
+    cot_on(CS, s, z, z < 3, z > 0)
+    @pl.loop(1, 8)
+    def _(k):
+        t = (s + k) % 8
+        p.arrived(S.at[t], rs.at[t], spare)
+
+    for t in range(8):
+        row = S[t, 0:1, :].astype(F32)
+        gains[0:1, 192 * t : 192 * t + 192] = row[:, 0:192]
+        bias[0:1, 256 * t : 256 * t + 256] = row[:, 256:512]
+        gains[1:2, 192 * t : 192 * t + 192] = row[:, 512:704]
+    x = x_ref[...].astype(F32)
+    a1[...] = (x * inverse_norm(x) * gains[0:1, :]).astype(BF)
+    relay(vq, sdq, rq)
+    cosine, sine = cos_ref[...], sin_ref[...]
+    for j in range(4):
+        co = pl.ds(512 * j, 512)
+        joined = dot(a1[...], WQ[:, co]) + bias[0:1, co]
+        for i in range(4):
+            h = 4 * j + i
+            u = joined[:, 128 * i : 128 * i + 128]
+            if h < 14:
+                u = u * cosine + pltpu.roll(u, 64, 1) * sine
+            if h < 12:
+                queries[h // 6, pl.ds(128 * (h % 6), 128), :] = (u * HEAD_DIMENSION**-0.5).astype(BF)
+            elif h < 14:
+                keys[h - 12] = u.astype(BF)
+            else:
+                values[h - 14] = u.astype(BF)
+    cot_step(1)
+    save = (pltpu.make_async_copy(WQ, WQ_out, loc.at[3]), pltpu.make_async_copy(WO, WO_out, loc.at[4]))
+    save[0].start()
+    open_to = allow_ref[...] != 0
+    for g in range(2):
+        scores = dot_nt(queries[g], keys[g]).reshape(6, 128, 128)
+        scores = jnp.where(open_to[None], scores, -1e30)
+        ex = jnp.exp(scores - jnp.max(scores, axis=-1, keepdims=True))
+        soft = (ex / jnp.sum(ex, axis=-1, keepdims=True)).reshape(768, 128)
+        probs[g] = soft
+        out = dot(soft.astype(BF), values[g]).astype(BF)
+        for i in range(6):
+            att[:, pl.ds(128 * (6 * g + i), 128)] = out[128 * i : 128 * i + 128]
+    relay(vo, sdo, ro)
+    save[1].start()
+    for j in range(3):
+        co = pl.ds(512 * j, 512)
+        mid[:, co] = x[:, 512 * j : 512 * j + 512] + dot(att[...], WO[:, co])
+    hidden = mid[...]
+    a2[...] = (hidden * inverse_norm(hidden) * gains[1:2, :]).astype(BF)
+
+    @pl.loop(1, 8)
+    def _(k):
+        t = (s + k) % 8
+        p.arrived(gq(t, r), rg.at[t, r], spare)
+        share(gq, t, sdg, rg)
+
+    cot_step(2)
+    cot_step(3)
+    relay(gq, sdg, rg)
+
+    @pl.loop(0, 4)
+    def _(zz):
+        t = p.theirs(zz)
+        p.arrived(cot_block(t), rc.at[t], spare)
+
+    @pl.loop(1, 8)
+    def _(k):
+        t = (s + k) % 8
+        p.sent(S.at[t], ss.at[t], spare)
+        p.sent(gq(t, r), sg.at[t], spare)
+        for d in range(3):
+            p.sent(vq(t, r), sdq.at[t, d], spare)
+            p.sent(vo(t, r), sdo.at[t, d], spare)
+            p.sent(gq(t, r), sdg.at[t, d], spare)
+
+    for zz in range(4):
+        p.sent(vq(s, r), syq.at[zz], spare)
+        p.sent(vo(s, r), syo.at[zz], spare)
+        p.sent(CS, scy.at[zz], spare)
+
+        @pl.when(zz != z)
+        def _():
+            p.sent(vq(s, r), szq.at[zz], spare)
+            p.sent(vo(s, r), szo.at[zz], spare)
+
+        pl.when((zz <= z) & (z < 3))(lambda: p.sent(CS, scz.at[zz, 0], spare))
+        pl.when((zz >= z) & (z > 0))(lambda: p.sent(CS, scz.at[zz, 1], spare))
+    for copy in own_out + save:
+        copy.wait()
+
+
+def gather_weights(x, cosine, sine, allowed, small, w_qkv, w_out, w_gate, w_up, cot):
+    return pl.pallas_call(
+        gather_body,
+        out_shape=(
+            shaped(1536, 2048), shaped(1536, 1536), shaped(1536, 2304), shaped(1024, 1536), shaped(8, 1536, dtype=F32),
+            shaped(2, 768, 128), shaped(2, 128, 128), shaped(2, 128, 128), shaped(2, 768, 128, dtype=F32),
+            shaped(128, 1536), shaped(128, 1536), shaped(128, 1536, dtype=F32), shaped(128, 1536),
+        ),
+        in_specs=[VMEM] * 5 + [HBM] * 5,
+        out_specs=(HBM,) * 4 + (VMEM,) * 9,
+        scratch_shapes=[
+            low(1536, 2048), low(1536, 1536), low(192, 8960), low(192, 8960), low(8, 192, 2304), low(128, 1536),
+            low(8, 16, 768), full(8, 2048),
+            DMA((8, 4)), DMA((8, 4)), DMA((8, 4)), DMA((8,)), DMA((8,)),
+            DMA((4,)), DMA((4,)), DMA((8, 3)), DMA((4,)), DMA((4,)), DMA((8, 3)),
+            DMA((8,)), DMA((8, 3)), DMA((4, 2)), DMA((4,)), DMA((8,)), DMA((6,)),
+        ],
+        compiler_params=pltpu.CompilerParams(collective_id=0, has_side_effects=True, vmem_limit_bytes=56 << 20),
+        name="gather_and_attend",
+    )(x, cosine, sine, allowed, small, w_qkv, w_out, w_gate, w_up, cot)
+
+
+def feed_body(
+    n_ref, c_hbm, g_hbm, d_hbm, DS, PO_out, GQ, OD,
+    vG, vD, vC, N, NT, MX, MT, H, PD, PO, YD, ZD, GD, RCd, RXd, RC, RX,
+    rn, syn, szn, ryd, rzd, syd, szd, scd, rcd, sxd, rxd, sfd, rfd, scg, rcg, sxg, rxg, lq, loc,
+):
+    p = Place()
+    r, s, c, y, z = p.r, p.s, p.c, p.y, p.z
+    spare = loc.at[0]
+
+    def block(t):
+        return N.at[rows_of(128 * t, 128, 128)]
+
+    loads = (
+        pltpu.make_async_copy(n_ref, block(s), loc.at[1]),
+        pltpu.make_async_copy(c_hbm, vC, loc.at[2]),
+        pltpu.make_async_copy(g_hbm, vG, loc.at[3]),
+        pltpu.make_async_copy(d_hbm, vD.at[0:1120], loc.at[4]),
+    )
+    for copy in loads:
+        copy.start()
+    p.greet(range(1, 8))
+    send(n_ref, block(s), syn.at[z], rn.at[s], p.side)
+    for k in (1, 2, 3):
+        zz = p.line(k)
+        send(n_ref, block(s), szn.at[zz], rn.at[s], p.peer(p.mine(zz)))
+    vD[1120:1152, :] = jnp.zeros((32, 1536), BF)
+    for copy in loads:
+        copy.wait()
+
+    def add_d(k):
+        zz = p.line(k)
+        t = p.mine(zz)
+        p.arrived(YD.at[zz], ryd.at[zz], spare)
+        PD[t] = (PD[t].astype(F32) + YD[zz].astype(F32)).astype(BF)
+
+    def send_d(k):
+        zz = p.line(k)
+        send(PD.at[p.mine(zz)], ZD.at[z], szd.at[zz], rzd.at[z], p.peer(p.mine(zz)))
+
+    @pl.loop(0, 4)
+    def _(k):
+        zz = p.line(k)
+
+        @pl.when(k < 3)
+        def _():
+            zn = p.line(k + 1)
+            t = p.mine(zn)
+            p.arrived(block(t), rn.at[t], spare)
+            send(block(t), block(t), syn.at[zn], rn.at[t], p.side)
+
+        to = p.theirs(zz)
+        p.arrived(block(to), rn.at[to], spare)
+        rows = rows_of(256 * zz, 256, 256)
+        X = N[rows]
+        NT[:, rows] = X.T
+        cot = vC[rows]
+        for j in range(3):
+            ga, ua = pl.ds(384 * j, 384), pl.ds(1152 + 384 * j, 384)
+            gate = dot(X, vG[:, ga])
+            up = dot(X, vG[:, ua])
+            d_mixed = dot_nt(cot, vD[ga])
+            sg = jax.nn.sigmoid(gate)
+            active = gate * sg
+            d_active = d_mixed * up
+            MX[:, ga] = (active * up).astype(BF)
+            H[rows, ga] = (d_active * sg + d_active * active * (1.0 - sg)).astype(BF)
+            H[rows, ua] = (d_mixed * active).astype(BF)
+        for j in range(3):
+            co = pl.ds(512 * j, 512)
+            part = dot_nt(H[rows], vG[co]).astype(BF)
+            PD[2 * zz, :, co] = part[:128]
+            PD[2 * zz + 1, :, co] = part[128:]
+        send(PD.at[to], YD.at[zz], syd.at[zz], ryd.at[zz], p.side)
+        for j in range(3):
+            co = pl.ds(512 * j, 512)
+            part = dot(MX[...], vD[:, co]).astype(BF)
+            PO[2 * zz, :, co] = part[:128]
+            PO[2 * zz + 1, :, co] = part[128:]
+        MT[:, rows] = MX[...].T
+
+        @pl.when(k >= 1)
+        def _():
+            add_d(k - 1)
+
+        @pl.when(k >= 2)
+        def _():
+            send_d(k - 1)
+
+    save = pltpu.make_async_copy(PO, PO_out, loc.at[1])
+    save.start()
+
+    def chunk(i):
+        return rows_of(288 * i, 288)
+
+    def cols(q):
+        return rows_of(384 * q, 384, 128)
+
+    def down_term(i):
+        for j in range(3):
+            co = pl.ds(512 * j, 512)
+            GD[chunk(i), co] = dot(MT[chunk(i)], vC[:, co]).astype(BF)
+        for xx in range(2):
+            q = 2 * xx + 1 - c
+            send(GD.at[chunk(i), cols(q)], RCd.at[xx, chunk(i)], scd.at[i, xx], rcd.at[i, xx], p.core)
+
+    def down_chip(i):
+        for xx in range(2):
+            p.arrived(RCd.at[xx, chunk(i)], rcd.at[i, xx], spare)
+            q = cols(2 * xx + c)
+            GD[chunk(i), q] = (GD[chunk(i), q].astype(F32) + RCd[xx, chunk(i)].astype(F32)).astype(BF)
+        send(GD.at[chunk(i), cols(p.rx)], RXd.at[chunk(i)], sxd.at[i], rxd.at[i], p.across)
+
+    def down_whole(i):
+        p.arrived(RXd.at[chunk(i)], rxd.at[i], spare)
+        q = cols(r)
+        GD[chunk(i), q] = (GD[chunk(i), q].astype(F32) + RXd[chunk(i)].astype(F32)).astype(BF)
+        src, dst = GD.at[chunk(i), q], OD.at[r, chunk(i)]
+        pltpu.make_async_copy(src, dst, sfd.at[i, 3]).start()
+        send(src, dst, sfd.at[i, 0], rfd.at[i, r], p.across)
+        send(src, dst, sfd.at[i, 1], rfd.at[i, r], p.core)
+
+    def down_relay(i):
+        v = OD.at[p.rx, chunk(i)]
+        p.arrived(v, rfd.at[i, p.rx], spare)
+        send(v, v, sfd.at[i, 2], rfd.at[i, p.rx], p.core)
+
+    @pl.loop(0, 6)
+    def _(i):
+        pl.when(i < 4)(lambda: down_term(i))
+        pl.when((i >= 1) & (i < 5))(lambda: down_chip(i - 1))
+        pl.when(i >= 2)(lambda: down_whole(i - 2))
+
+        @pl.when(i == 1)
+        def _():
+            add_d(3)
+            send_d(3)
+
+    def own(k):
+        return (s + 1 + k) % 8
+
+    def pair_term(k):
+        t = own(k)
+        rows = rows_of(192 * t, 192)
+        for j in range(3):
+            co = pl.ds(768 * j, 768)
+            vG[rows, co] = dot(NT[rows], H[:, co]).astype(BF)
+        for xx in range(2):
+            send(vG.at[quarter(t, 2 * xx + 1 - c)], RC.at[t, xx], scg.at[t, xx], rcg.at[t, xx], p.core)
+
+    def pair_chip(k):
+        t = own(k)
+        for xx in range(2):
+            p.arrived(RC.at[t, xx], rcg.at[t, xx], spare)
+            q = quarter(t, 2 * xx + c)
+            vG[q] = (vG[q].astype(F32) + RC[t, xx].astype(F32)).astype(BF)
+        send(vG.at[quarter(t, p.rx)], RX.at[t], sxg.at[t], rxg.at[t], p.across)
+
+    def pair_whole(k):
+        t = own(k)
+        p.arrived(RX.at[t], rxg.at[t], spare)
+        q = quarter(t, r)
+        vG[q] = (vG[q].astype(F32) + RX[t].astype(F32)).astype(BF)
+        pltpu.make_async_copy(vG.at[q], GQ.at[t], lq.at[t]).start()
+
+    @pl.loop(0, 10)
+    def _(i):
+        pl.when(i < 8)(lambda: pair_term(i))
+        pl.when((i >= 1) & (i < 9))(lambda: pair_chip(i - 1))
+        pl.when(i >= 2)(lambda: pair_whole(i - 2))
+        pl.when(i < 4)(lambda: down_relay(i))
+
+    acc = PD[s].astype(F32)
+    for k in (1, 2, 3):
+        zz = p.line(k)
+        p.arrived(ZD.at[zz], rzd.at[zz], spare)
+        acc = acc + ZD[zz].astype(F32)
+    DS[...] = acc
+
+    @pl.loop(0, 8)
+    def _(t):
+        for xx in range(2):
+            p.sent(RC.at[t, xx], scg.at[t, xx], spare)
+        p.sent(RX.at[t], sxg.at[t], spare)
+        pltpu.make_async_copy(RX.at[t], GQ.at[t], lq.at[t]).wait()
+
+    @pl.loop(0, 4)
+    def _(i):
+        for q in (p.rc, p.rd):
+            p.arrived(OD.at[q, chunk(i)], rfd.at[i, q], spare)
+        for d in range(3):
+            p.sent(OD.at[r, chunk(i)], sfd.at[i, d], spare)
+        pltpu.make_async_copy(OD.at[r, chunk(i)], OD.at[r, chunk(i)], sfd.at[i, 3]).wait()
+        for xx in range(2):
+            p.sent(RCd.at[xx, chunk(i)], scd.at[i, xx], spare)
+        p.sent(RXd.at[chunk(i)], sxd.at[i], spare)
+        p.sent(block(s), syn.at[i], spare)
+        p.sent(YD.at[i], syd.at[i], spare)
+
+        @pl.when(i != z)
+        def _():
+            p.sent(block(s), szn.at[i], spare)
+            p.sent(ZD.at[i], szd.at[i], spare)
+
+    save.wait()
+
+
+def feed_forward(n2, cot, gate_up, w_down):
+    return pl.pallas_call(
+        feed_body,
+        out_shape=(shaped(128, 1536, dtype=F32), shaped(8, 128, 1536), shaped(8, 48, 2304), shaped(4, 1152, 384)),
+        in_specs=[HBM] * 4,
+        out_specs=(VMEM, HBM, HBM, HBM),
+        scratch_shapes=[
+            low(1536, 2304), low(1152, 1536), low(1024, 1536), low(1024, 1536), low(1536, 1024), low(256, 1152),
+            low(1152, 1024), low(1024, 2304), low(8, 128, 1536), low(8, 128, 1536), low(4, 128, 1536), low(4, 128, 1536),
+            low(1152, 1536), low(2, 1152, 384), low(1152, 384), low(8, 2, 48, 2304), low(8, 48, 2304),
+            DMA((8,)), DMA((4,)), DMA((4,)), DMA((4,)), DMA((4,)), DMA((4,)), DMA((4,)),
+            DMA((4, 2)), DMA((4, 2)), DMA((4,)), DMA((4,)), DMA((4, 4)), DMA((4, 4)),
+            DMA((8, 2)), DMA((8, 2)), DMA((8,)), DMA((8,)), DMA((8,)), DMA((5,)),
+        ],
+        compiler_params=pltpu.CompilerParams(collective_id=1, has_side_effects=True, vmem_limit_bytes=62 << 20),
+        name="feed_forward",
+    )(n2, cot, gate_up, w_down)
+
+
+def attend_back_body(
+    ds_ref, mid_ref, x_ref, cot_ref, gains, cos_ref, sin_ref, queries, keys, values, probs, att, a1,
+    wq_ref, wo_ref, po_ref, gq_ref,
+    out_ref, gtok_ref, OG, OWq, OWo,
+    vQ, vO, PO, YO, ZO, own_g, dmid, DB, dA, dj, AT, SM, RCq, RXq, Yq, Zq, RCo, Yo, Zo, RXo,
+    sa, ra, sf, syo, ryo, szo, rzo, scq, rcq, sxq, rxq, syq, ryq, szq, rzq, sfq, rfq,
+    sco, rco, syw, ryw, szw, rzw, sfo, rfo, loc,
+):
+    p = Place()
+    r, s, c, y, z = p.r, p.s, p.c, p.y, p.z
+    spare = loc.at[0]
+    loads = (
+        pltpu.make_async_copy(wo_ref, vO, loc.at[1]),
+        pltpu.make_async_copy(wq_ref, vQ.at[:, 0:2048], loc.at[2]),
+        pltpu.make_async_copy(po_ref, PO, loc.at[3]),
+        pltpu.make_async_copy(gq_ref.at[s], own_g, loc.at[4]),
+    )
+    for copy in loads:
+        copy.start()
+    p.greet(range(1, 8))
+    for k in range(1, 8):
+        t = (s + k) % 8
+        send(gq_ref.at[t], OG.at[r, s], sa.at[t], ra.at[s, r], p.peer(t))
+    for k in range(4):
+        zz = p.line(3 - k)
+        send(po_ref.at[p.theirs(zz)], YO.at[zz], syo.at[zz], ryo.at[zz], p.side)
+
+    def share(t):
+        v = OG.at[r, t]
+        send(v, v, sf.at[t, 0], ra.at[t, r], p.across)
+        send(v, v, sf.at[t, 1], ra.at[t, r], p.core)
+
+    def back(w):
+        return w * cos_ref[...] - pltpu.roll(w, 64, 1) * sin_ref[...]
+
+    dn, hidden = ds_ref[...], mid_ref[...]
+    rstd = inverse_norm(hidden)
+    unit = hidden * rstd
+    gain_ffn_grad = jnp.sum(dn * unit, axis=0, keepdims=True)
+    e = dn * gains[1:2, :]
+    dm = cot_ref[...].astype(F32) + rstd * (e - unit * jnp.mean(e * unit, axis=-1, keepdims=True))
+    dmid[...] = dm
+    DB[...] = dm.astype(BF)
+    AT[...] = att[...].T
+    for copy in loads:
+        copy.wait()
+    keep = pltpu.make_async_copy(own_g, OG.at[r, s], loc.at[4])
+    keep.start()
+    for j in range(3):
+        part = dot_nt(DB[...], vO[pl.ds(512 * j, 512)]).astype(BF)
+        for i in range(4):
+            h = 4 * j + i
+            dA[h // 6, pl.ds(128 * (h % 6), 128), :] = part[:, 128 * i : 128 * i + 128]
+
+    def own(k):
+        return 2 * p.line(3 - k % 4) + (1 - y + (k // 4) * (2 * y - 1))
+
+    for j in range(3):
+        co = pl.ds(512 * j, 512)
+        vO[:, co] = dot(AT[...], DB[:, co]).astype(BF)
+
+    @pl.loop(0, 8)
+    def _(k):
+        t = own(k)
+        for xx in range(2):
+            send(vO.at[quarter(t, 2 * xx + 1 - c)], RCo.at[t, xx], sco.at[t, xx], rco.at[t, xx], p.core)
+
+    def heads(g):
+        grad, soft = dA[g], probs[g]
+        d_probs = dot_nt(grad, values[g])
+        d_scores = (soft * (d_probs - jnp.sum(soft * d_probs, axis=-1, keepdims=True))).astype(BF)
+        d_values = dot(soft.astype(BF).T, grad)
+        d_queries = dot(d_scores, keys[g]) * HEAD_DIMENSION**-0.5
+        d_keys = dot(d_scores.T, queries[g])
+        for i in range(6):
+            dj[:, pl.ds(128 * (6 * g + i), 128)] = back(d_queries[128 * i : 128 * i + 128]).astype(BF)
+        dj[:, pl.ds(128 * (12 + g), 128)] = back(d_keys).astype(BF)
+        dj[:, pl.ds(128 * (14 + g), 128)] = d_values.astype(BF)
+
+    heads(0)
+
+    @pl.loop(0, 8)
+    def _(k):
+        t = own(k)
+        for xx in range(2):
+            p.arrived(RCo.at[t, xx], rco.at[t, xx], spare)
+            q = quarter(t, 2 * xx + c)
+            vO[q] = (vO[q].astype(F32) + RCo[t, xx].astype(F32)).astype(BF)
+
+            @pl.when(k < 4)
+            def _():
+                send(vO.at[q], Yo.at[t // 2, xx], syw.at[t // 2, xx], ryw.at[t // 2, xx], p.side)
+
+    heads(1)
+    joined_grad = dj[...]
+    bias_grad = jnp.sum(joined_grad.astype(F32), axis=0, keepdims=True)
+    x = x_ref[...].astype(F32)
+    rstd = inverse_norm(x)
+    unit = x * rstd
+    dn1 = jnp.concatenate(
+        [dot_nt(joined_grad, vQ[pl.ds(512 * j, 512), 0:2048]) for j in range(3)], axis=1
+    )
+    gain_attn_grad = jnp.sum(dn1 * unit, axis=0, keepdims=True)
+    e = dn1 * gains[0:1, :]
+    gtok_ref[...] = (
+        dmid[...] + rstd * (e - unit * jnp.mean(e * unit, axis=-1, keepdims=True))
+    ).astype(BF)
+    SM[...] = jnp.zeros_like(SM)
+    for t in range(8):
+        SM[t, 0:1, :] = gain_attn_grad[:, 192 * t : 192 * t + 128]
+        SM[t, 1:2, 0:64] = gain_attn_grad[:, 192 * t + 128 : 192 * t + 192]
+        SM[t, 2:3, :] = bias_grad[:, 256 * t : 256 * t + 128]
+        SM[t, 3:4, :] = bias_grad[:, 256 * t + 128 : 256 * t + 256]
+        SM[t, 4:5, :] = gain_ffn_grad[:, 192 * t : 192 * t + 128]
+        SM[t, 5:6, 0:64] = gain_ffn_grad[:, 192 * t + 128 : 192 * t + 192]
+    AT[...] = a1[...].T
+
+    @pl.loop(0, 8)
+    def _(k):
+        t = own(k)
+        rows = rows_of(192 * t, 192)
+        for j in range(2):
+            co = pl.ds(1024 * j, 1024)
+            vQ[rows, co] = dot(AT[rows], dj[:, co]).astype(BF)
+        vQ[rows, 2048:2176] = jnp.zeros((192, 128), BF)
+        vQ[rows_of(192 * t, 16), 2048:2176] = SM[t].astype(BF)
+        for xx in range(2):
+            send(vQ.at[quarter(t, 2 * xx + 1 - c)], RCq.at[t, xx], scq.at[t, xx], rcq.at[t, xx], p.core)
+
+    def q_chip(k):
+        t = own(k)
+        for xx in range(2):
+            p.arrived(RCq.at[t, xx], rcq.at[t, xx], spare)
+            q = quarter(t, 2 * xx + c)
+            vQ[q] = (vQ[q].astype(F32) + RCq[t, xx].astype(F32)).astype(BF)
+        send(vQ.at[quarter(t, p.rx)], RXq.at[t], sxq.at[t], rxq.at[t], p.across)
+
+    def q_whole(k):
+        t = own(k)
+        p.arrived(RXq.at[t], rxq.at[t], spare)
+        q = quarter(t, r)
+        vQ[q] = (vQ[q].astype(F32) + RXq[t].astype(F32)).astype(BF)
+
+        @pl.when(k < 4)
+        def _():
+            send(vQ.at[q], Yq.at[t // 2], syq.at[t // 2], ryq.at[t // 2], p.side)
+
+        @pl.when(k >= 4)
+        def _():
+            p.arrived(Yq.at[t // 2], ryq.at[t // 2], spare)
+            vQ[q] = (vQ[q].astype(F32) + Yq[t // 2].astype(F32)).astype(BF)
+
+        @pl.when((k >= 4) & (k < 7))
+        def _():
+            send(vQ.at[q], Zq.at[z], szq.at[t // 2], rzq.at[z], p.peer(t))
+
+    def out_line(k):
+        zz = p.line(3 - k)
+        t = p.mine(zz)
+        p.arrived(YO.at[zz], ryo.at[zz], spare)
+        PO[t] = (PO[t].astype(F32) + YO[zz].astype(F32)).astype(BF)
+
+        @pl.when(k < 3)
+        def _():
+            send(PO.at[t], ZO.at[z], szo.at[zz], rzo.at[z], p.peer(t))
+
+    def w_line(k):
+        zz = p.line(3 - k)
+        t = p.mine(zz)
+        for xx in range(2):
+            p.arrived(Yo.at[zz, xx], ryw.at[zz, xx], spare)
+            q = quarter(t, 2 * xx + c)
+            vO[q] = (vO[q].astype(F32) + Yo[zz, xx].astype(F32)).astype(BF)
+
+            @pl.when(k < 3)
+            def _():
+                send(vO.at[q], Zo.at[z, xx], szw.at[zz, xx], rzw.at[z, xx], p.peer(t))
+
+    @pl.loop(0, 8)
+    def _(k):
+        q_chip(k)
+    share_own = pltpu.make_async_copy(own_g, OG.at[r, s], loc.at[4])
+    share_own.wait()
+    share(s)
+
+    @pl.loop(1, 8)
+    def _(k):
+        t = (s + 8 - k) % 8
+        p.arrived(OG.at[r, t], ra.at[t, r], spare)
+        share(t)
+
+    @pl.loop(0, 4)
+    def _(k):
+        out_line(k)
+        w_line(k)
+
+    @pl.loop(0, 8)
+    def _(k):
+        q_whole(k)
+    acc = PO[s].astype(F32) + mid_ref[...]
+    for k in (1, 2, 3):
+        zz = p.line(k)
+        p.arrived(ZO.at[zz], rzo.at[zz], spare)
+        acc = acc + ZO[zz].astype(F32)
+    out_ref[...] = acc.astype(BF)
+    for xx in range(2):
+        q = quarter(s, 2 * xx + c)
+        acc = vO[q].astype(F32)
+        for k in (1, 2, 3):
+            zz = p.line(k)
+            p.arrived(Zo.at[zz, xx], rzw.at[zz, xx], spare)
+            acc = acc + Zo[zz, xx].astype(F32)
+        vO[q] = acc.astype(BF)
+    send(vO.at[quarter(s, p.rx)], RXo, sfo.at[3], rfo.at[4], p.across)
+    acc = vQ[quarter(s, r)].astype(F32)
+    for k in (1, 2, 3):
+        zz = p.line(k)
+        p.arrived(Zq.at[zz], rzq.at[zz], spare)
+        acc = acc + Zq[zz].astype(F32)
+    OWq[r] = acc.astype(BF)
+
+    def spread(O, sems, rsems):
+        send(O.at[r], O.at[r], sems.at[0], rsems.at[r], p.across)
+        send(O.at[r], O.at[r], sems.at[1], rsems.at[r], p.core)
+
+    def pass_on(O, sems, rsems):
+        v = O.at[p.rx]
+        p.arrived(v, rsems.at[p.rx], spare)
+        send(v, v, sems.at[2], rsems.at[p.rx], p.core)
+
+    spread(OWq, sfq, rfq)
+    p.arrived(RXo, rfo.at[4], spare)
+    OWo[r] = (vO[quarter(s, r)].astype(F32) + RXo[...].astype(F32)).astype(BF)
+    spread(OWo, sfo, rfo)
+
+    @pl.loop(0, 8)
+    def _(k):
+        t = (s + 8 - k) % 8
+        v = OG.at[p.rx, t]
+        p.arrived(v, ra.at[t, p.rx], spare)
+        send(v, v, sf.at[t, 2], ra.at[t, p.rx], p.core)
+
+    pass_on(OWq, sfq, rfq)
+    pass_on(OWo, sfo, rfo)
+    for q in (p.rc, p.rd):
+        p.arrived(OWq.at[q], rfq.at[q], spare)
+        p.arrived(OWo.at[q], rfo.at[q], spare)
+    for d in range(3):
+        p.sent(OWq.at[r], sfq.at[d], spare)
+        p.sent(OWo.at[r], sfo.at[d], spare)
+    p.sent(RXo, sfo.at[3], spare)
+
+    @pl.loop(0, 8)
+    def _(t):
+        for q in (p.rc, p.rd):
+            p.arrived(OG.at[q, t], ra.at[t, q], spare)
+        for d in range(3):
+            p.sent(OG.at[r, t], sf.at[t, d], spare)
+        for xx in range(2):
+            p.sent(RCq.at[t, xx], scq.at[t, xx], spare)
+            p.sent(RCo.at[t, xx], sco.at[t, xx], spare)
+        p.sent(RXq.at[t], sxq.at[t], spare)
+
+        @pl.when(t != s)
+        def _():
+            p.sent(OG.at[r, s], sa.at[t], spare)
+
+    @pl.loop(0, 4)
+    def _(i):
+        p.sent(YO.at[i], syo.at[i], spare)
+        p.sent(Yq.at[i], syq.at[i], spare)
+        for xx in range(2):
+            p.sent(Yo.at[i, xx], syw.at[i, xx], spare)
+
+        @pl.when(i != z)
+        def _():
+            p.sent(ZO.at[i], szo.at[i], spare)
+            p.sent(Zq.at[i], szq.at[i], spare)
+            for xx in range(2):
+                p.sent(Zo.at[i, xx], szw.at[i, xx], spare)
+
+
+def attend_back(*args):
+    return pl.pallas_call(
+        attend_back_body,
+        out_shape=(
+            shaped(128, 1536), shaped(128, 1536), shaped(4, 8, 48, 2304), shaped(4, 48, 2176), shaped(4, 48, 1536),
+        ),
+        in_specs=[VMEM] * 13 + [HBM] * 4,
+        out_specs=(VMEM, VMEM, HBM, VMEM, VMEM),
+        scratch_shapes=[
+            low(1536, 2176), low(1536, 1536), low(8, 128, 1536), low(4, 128, 1536), low(4, 128, 1536), low(48, 2304),
+            full(128, 1536), low(128, 1536), low(2, 768, 128), low(128, 2048), low(1536, 128), full(8, 16, 128),
+            low(8, 2, 48, 2176), low(8, 48, 2176), low(4, 48, 2176), low(4, 48, 2176),
+            low(8, 2, 48, 1536), low(4, 2, 48, 1536), low(4, 2, 48, 1536), low(48, 1536),
+            DMA((8,)), DMA((8, 4)), DMA((8, 3)), DMA((4,)), DMA((4,)), DMA((4,)), DMA((4,)),
+            DMA((8, 2)), DMA((8, 2)), DMA((8,)), DMA((8,)), DMA((4,)), DMA((4,)), DMA((4,)), DMA((4,)), DMA((3,)), DMA((4,)),
+            DMA((8, 2)), DMA((8, 2)), DMA((4, 2)), DMA((4, 2)), DMA((4, 2)), DMA((4, 2)), DMA((4,)), DMA((5,)), DMA((5,)),
+        ],
+        compiler_params=pltpu.CompilerParams(collective_id=2, has_side_effects=True, vmem_limit_bytes=58 << 20),
+        name="attend_back",
+    )(*args)
+
+
+def widen_body(g_ref, d_ref, q_ref, o_ref, gate, up, down, qkv, out):
+    for t in range(8):
+        gate[:, 1120 * t : 1120 * t + 1120] = g_ref[0, t, :, 0:1120].astype(F32)
+        up[:, 1120 * t : 1120 * t + 1120] = g_ref[0, t, :, 1152:2272].astype(F32)
+    down[...] = d_ref[0, 0:1120, :].astype(F32)
+    qkv[...] = q_ref[0, :, 0:2048].astype(F32)
+    out[...] = o_ref[0].astype(F32)
+
+
+def widen(g, d, q, o):
+    return pl.pallas_call(
+        widen_body,
+        grid=(4,),
+        out_shape=(
+            shaped(192, 8960, dtype=F32), shaped(192, 8960, dtype=F32), shaped(1120, 1536, dtype=F32),
+            shaped(192, 2048, dtype=F32), shaped(192, 1536, dtype=F32),
+        ),
+        in_specs=[
+            pl.BlockSpec((1, 8, 48, 2304), lambda i: (i, 0, 0, 0)),
+            pl.BlockSpec((1, 1152, 384), lambda i: (i, 0, 0)),
+            pl.BlockSpec((1, 48, 2176), lambda i: (i, 0, 0)),
+            pl.BlockSpec((1, 48, 1536), lambda i: (i, 0, 0)),
+        ],
+        out_specs=(
+            pl.BlockSpec((48, 8960), lambda i: (i, 0)),
+            pl.BlockSpec((48, 8960), lambda i: (i, 0)),
+            pl.BlockSpec((1120, 384), lambda i: (0, i)),
+            pl.BlockSpec((48, 2048), lambda i: (i, 0)),
+            pl.BlockSpec((48, 1536), lambda i: (i, 0)),
+        ),
+        compiler_params=pltpu.CompilerParams(vmem_limit_bytes=48 << 20),
+        name="widen",
+    )(g, d, q, o)
+
+
+def shards_eight(
+    tokens, segments, gain_attn, w_qkv, b_qkv, w_out, gain_ffn, w_gate, w_up, w_down, cotangent
+):
+    cosine, sine, allowed = tables(segments[0], HEAD_DIMENSION)
+    half = HEAD_DIMENSION // 2
+    sine = jnp.concatenate([-sine[:, :half], sine[:, half:]], axis=-1)
+    gap = jnp.zeros((64,), BF)
+    small = jnp.concatenate([gain_attn, gap, b_qkv, gain_ffn, gap])[None]
+    small = jnp.pad(small, ((0, 15), (0, 0)))
+    x, cot = tokens[0], cotangent[0]
+    WQ, WO, G, C, gains, queries, keys, values, probs, att, a1, mid, a2 = gather_weights(
+        x, cosine, sine, allowed, small, w_qkv, w_out, w_gate, w_up, cot
+    )
+    ds, parts, gate_up, down = feed_forward(a2, C, G, w_down)
+    out, grad_tokens, gate_up, qkv, o = attend_back(
+        ds, mid, x, cot, gains, cosine, sine, queries, keys, values, probs, att, a1, WQ, WO, parts, gate_up
+    )
+    gate, up, down, qkv_rows, out_rows = widen(gate_up, down, qkv, o)
+    small = qkv[0, 0:6, 2048:].astype(F32).reshape(768)
+    return (
+        out[None], grad_tokens[None], small[0:192], qkv_rows, small[256:512], out_rows, small[512:704], gate, up, down,
+    )
+
+
 def solution(mesh):
     placed = (
         P(("replica", "shard"), None, None),
@@ -282,7 +1192,7 @@
         P(("replica", "shard"), None, None),
     )
     return jax.shard_map(
-        shards,
+        shards_eight if (mesh.shape["replica"], mesh.shape["shard"]) == (4, 8) else shards,
         mesh=mesh,
         in_specs=placed,
         out_specs=(

time: 1200 us -> 454 us (0.38)
  waiting for transfers between devices: 693 us -> 0 us
  Pallas kernels: 0 us -> 442 us
  blocking collectives: 267 us -> 0 us
  matrix products: 107 us -> 0 us
  local copies, waits for them, and re-layouts: 58.6 us -> 6.99 us
  other arithmetic: 36 us -> 4 us
  between operations: 16.5 us -> 0.72 us
  starting transfers between devices: 13.5 us -> 0 us
    pallas_call x0 -> x4, Pallas kernels: none -> 442 us  [the longest x1 164 us: feed_forward(): pl.pallas_call(feed_body, out_shape=(shaped(128, 1536, dtype=F32), shaped...]
    reduce_scatter x4 -> x0, waiting for transfers between devices: 309 us -> none  [the longest x1 122 us: shards(): lax.psum_scatter(qkv_grad_term.astype(jnp.bfloat16), 'shard', scatter_dim...]
    psum x1 -> x0, waiting for transfers between devices: 213 us -> none  [shards(): lax.psum(owned[1].astype(jnp.bfloat16), 'replica').astype(jnp.float32)]
    all_gather x6 -> x0, waiting for transfers between devices: 169 us -> none  [the longest x1 99.8 us: shards(): all_acts = lax.all_gather(acts_second, 'shard', axis=0, tiled=True)]
    unnamed x2 -> x0, blocking collectives: 145 us -> none
    dot_general x20 -> x0, matrix products: 105 us -> none  [the longest x3 24.4 us: column_term(): jnp.einsum('lf,ld->fd', left_side, right_side, preferred_element_type=jnp...]
    all_gather x1 -> x0, blocking collectives: 63.1 us -> none  [shards(): lax.all_gather(b_qkv, 'shard', axis=0, tiled=True)]
    all_to_all x2 -> x0, blocking collectives: 53.5 us -> none  [to_rows(): part = lax.all_to_all(part, 'shard', 0, 0, tiled=True)]
  transfers between devices with their start and end apart: 13 -> 0, of which waited for: 8 -> 0; matrix products, arithmetic and copies ran while one was open for 13% -> 0% of each run, Pallas kernels for 0% -> 0%
where the time goes in v3:
time: 454 us
  Pallas kernels  442 us (97%)
  local copies, waits for them, and re-layouts  6.99 us (2%)
    pallas_call x1, Pallas kernels, feed_forward(): pl.pallas_call(feed_body, out_shape=(shaped(128, 1536, dtype=F32), shaped...  164 us
    pallas_call x1, Pallas kernels, attend_back(): pl.pallas_call(attend_back_body, out_shape=(shaped(128, 1536), shaped(128...  136 us
    pallas_call x1, Pallas kernels, gather_weights(): pl.pallas_call(gather_body, out_shape=(shaped(1536, 2048), shaped(1536, 1...  132 us
    pallas_call x1, Pallas kernels, widen(): pl.pallas_call(widen_body, grid=(4,), out_shape=(shaped(192, 8960, dtype=...  10.5 us

profile of v3, /device:TPU:0, one launch (start us, length us, event | category | flops | bytes accessed | tf_op | source)
XLA Modules:
  0.0 454.1 jit_solution(2358386100650699)
XLA Ops:
  0.6 0.9 convert_reduce_fusion
  1.6 0.3 fusion.2
  1.9 0.8 pad_maximum_fusion
  2.7 1.4 fusion.1.allow_ref
  4.1 2.1 concatenate.11
  6.2 0.6 pad.4.small_ref
  6.8 131.5 %gather_and_attend.1 = (bf16[1536,2048]{1,0:T(8,128)(2,1)}, bf16[1536,1536]{1,0:T(8,128)(2,1)}, bf16[1536,2304]{1,0:T(8,128)(2,1)}, bf16[1024,1536]{1,0:T(8,128)...) custom-call(bf16[128,1536]{1,0:T(8,128)(2,1)} %bitcast.11, ...), custom_call_target="tpu_custom_call" | custom-call | tf_op jit(solution)/shard_map/gather_and_attend/pallas_call | solution.py:571
  138.3 164.5 %feed_forward.1 = (f32[128,1536]{1,0:T(8,128)}, bf16[8,128,1536]{2,1,0:T(8,128)(2,1)}, bf16[8,48,2304]{2,1,0:T(8,128)(2,1)}, bf16[4,1152,384]{2,1,0:T(8,128)(2,1)}) custom-call(bf16[128,1536]{1,0:T(8,128)(2,1)} %get-tuple-element.37.n_ref, bf16[1024,1536]{1,0:T(8,128)(2,1)} %get-tuple-element.38.c_hbm, bf16[1536,2304]{1,0:T(8,128)(2,1)} %get-tuple-element.39.g_hbm, ...), custom_call_target="tpu_custom_call" | custom-call | tf_op jit(solution)/shard_map/feed_forward/pallas_call | solution.py:799
  302.8 0.0 copy-start
  302.8 135.9 %attend_back.1 = (bf16[128,1536]{1,0:T(8,128)(2,1)}, bf16[128,1536]{1,0:T(8,128)(2,1)}, bf16[4,8,48,2304]{3,2,1,0:T(8,128)(2,1)}, bf16[4,48,2176]{2,1,0:T(8,128)(2,1)}, bf16[4,48,1536]{2,1,0:T(8,128)(2,1)}) custom-call(f32[128,1536]{1,0:T(8,128)} %get-tuple-element.40.ds_ref, f32[128,1536]{1,0:T(8,128)} %get-tuple-element.41.mid_ref, ...), custom_call_target="tpu_custom_call" | custom-call | tf_op jit(solution)/shard_map/attend_back/pallas_call | solution.py:1100
  438.7 0.0 copy-done
  438.7 0.0 copy-start.1
  438.7 1.1 copy-done.1
  439.9 0.0 copy-start.2
  439.9 1.1 copy-done.2
  440.9 0.0 copy-start.4
  440.9 0.0 copy-start.3
  440.9 10.5 %widen.1 = (f32[192,8960]{1,0:T(8,128)}, f32[192,8960]{1,0:T(8,128)}, f32[1120,1536]{1,0:T(8,128)}, f32[192,2048]{1,0:T(8,128)}, f32[192,1536]{1,0:T(8,128)}) custom-call(bf16[4,8,48,2304]{3,2,1,0:T(8,128)(2,1)} %get-tuple-element.56.g_ref, bf16[4,1152,384]{2,1,0:T(8,128)(2,1)S(1)} %copy-done, bf16[4,48,2176]{2,1,0:T(8,128)(2,1)S(1)} %copy-done.1, ...), custom_call_target="tpu_custom_call" | custom-call | tf_op jit(solution)/shard_map/widen/pallas_call | solution.py:1131
  451.4 0.6 fusion.3
  452.0 0.6 bitcast_convert_fusion.1
  452.6 0.0 copy-done.4
  452.6 0.7 copy.23
  453.3 0.0 copy-done.3
  453.3 0.7 copy.24
  (5 shorter events, 0.0 us)
Async XLA Ops:
  302.8 135.9 %copy-start = (bf16[4,1152,384]{2,1,0:T(8,128)(2,1)S(1)}, bf16[4,1152,384]{2,1,0:T(8,128)(2,1)}, u32[]{:S(2)}) copy-start(bf16[4,1152,384]{2,1,0:T(8,128)(2,1)} %get-tuple-element.57.d_ref) | copy-start | bytes 10616836
  438.7 1.2 copy-start.1
  439.9 1.1 copy-start.2
  440.9 11.6 %copy-start.4 = (bf16[128,1536]{1,0:T(8,128)(2,1)S(1)}, bf16[128,1536]{1,0:T(8,128)(2,1)}, u32[]{:S(2)}) copy-start(bf16[128,1536]{1,0:T(8,128)(2,1)} %get-tuple-element.53) | copy-start | bytes 1179652
  440.9 12.4 %copy-start.3 = (bf16[128,1536]{1,0:T(8,128)(2,1)S(1)}, bf16[128,1536]{1,0:T(8,128)(2,1)}, u32[]{:S(2)}) copy-start(bf16[128,1536]{1,0:T(8,128)(2,1)} %get-tuple-element.54) | copy-start | bytes 1179652

commit v4 on v3

--- a/solution.py
+++ b/solution.py
@@ -323,7 +323,25 @@
         return (self.r, t)
 
     def line(self, k):
-        return self.z + (1 - 2 * (self.z % 2)) * (k % 2) + (k // 2) * (2 - 4 * (self.z // 2))
+        near = self.z + (1 - 2 * (self.z % 2)) * (k % 2)
+        far = k + (self.z // 2) * (3 - 2 * k)
+        return (1 - k // 2) * near + (k // 2) * far
+
+    def onward(self, zz, copy):
+        pl.when((zz <= self.z) & (self.z < 3))(lambda: copy(0, self.peer(self.s + 2)))
+        pl.when((zz >= self.z) & (self.z > 0))(lambda: copy(1, self.peer(self.s - 2)))
+
+    def went_onward(self, zz, wait):
+        pl.when((zz <= self.z) & (self.z < 3))(lambda: wait(0))
+        pl.when((zz >= self.z) & (self.z > 0))(lambda: wait(1))
+
+    def reduce_step(self, zz, add, hand):
+        pl.when((zz >= self.z) & (self.z > 0))(lambda: add(zz))
+        pl.when((zz < self.z) & (self.z < 3))(lambda: add(zz))
+        pl.when((zz == self.z) & (self.z < 3))(lambda: add(4))
+        pl.when(zz > self.z)(lambda: hand(zz, self.peer(self.s + 2)))
+        pl.when(zz < self.z - 1)(lambda: hand(zz, self.peer(self.s - 2)))
+        pl.when(zz == self.z - 1)(lambda: hand(4, self.peer(self.s - 2)))
 
     def mine(self, zz):
         return 2 * zz + self.y
@@ -351,6 +369,43 @@
 
 def inverse_norm(v):
     return lax.rsqrt(jnp.mean(v * v, axis=-1, keepdims=True) + eps_norm)
+
+
+class Gather:
+    def __init__(self, p, spare, view, arrivals, along, aside):
+        self.p, self.spare, self.view = p, spare, view
+        self.arrivals, self.along, self.aside = arrivals, along, aside
+
+    def move(self, src, t, zz):
+        p, dst, sem = self.p, self.view(t), self.arrivals(t)
+        p.onward(zz, lambda d, device: send(src, dst, self.along.at[zz, d], sem, device))
+        send(src, dst, self.aside.at[zz], sem, p.side)
+
+    def start(self, src):
+        self.move(src, self.p.s, self.p.z)
+
+    def wait(self, t):
+        self.p.arrived(self.view(t), self.arrivals(t), self.spare)
+
+    def step(self, k, then=None):
+        zz = self.p.line(k)
+        t = self.p.mine(zz)
+        self.wait(t)
+        self.move(self.view(t), t, zz)
+        if then is not None:
+            then(t)
+
+    def other(self, k, then=None):
+        t = self.p.theirs(self.p.line(k))
+        self.wait(t)
+        if then is not None:
+            then(t)
+
+    def finish(self):
+        block = self.view(self.p.s)
+        for zz in range(4):
+            self.p.sent(block, self.aside.at[zz], self.spare)
+            self.p.went_onward(zz, lambda d: self.p.sent(block, self.along.at[zz, d], self.spare))
 
 
 def gather_body(
@@ -360,7 +415,7 @@
     rq, ro, rg, rc, rs, szq, syq, sdq, szo, syo, sdo, sg, sdg, scz, scy, ss, loc,
 ):
     p = Place()
-    r, s, z = p.r, p.s, p.z
+    r, s, c, z = p.r, p.s, p.c, p.z
     spare = loc.at[0]
     own = rows_of(192 * s, 192)
     own_c = rows_of(128 * s, 128, 128)
@@ -375,62 +430,51 @@
         copy.start()
     p.greet(range(1, 8))
     S[s] = small_ref[...]
+
+    def vq(t, q):
+        return WQ.at[quarter(t, q)]
+
+    def vo(t, h):
+        return WO.at[rows_of(192 * t + 96 * h, 96)]
+
+    def gq(t, q):
+        return G.at[quarter(t, q)]
+
+    def cot_block(t):
+        return C.at[rows_of(128 * t, 128, 128)]
+
+    g_q = Gather(p, spare, lambda t: vq(t, r), lambda t: rq.at[t, r], szq, syq)
+    g_o = Gather(p, spare, lambda t: vo(t, c), lambda t: ro.at[t, c], szo, syo)
+    g_c = Gather(p, spare, cot_block, lambda t: rc.at[t], scz, scy)
+    g_q.start(wq_ref.at[rows_of(48 * r, 48)])
     for k in range(1, 8):
         t = (s + k) % 8
         send(small_ref, S.at[s], ss.at[t], rs.at[s], p.peer(t))
 
-    def in_plane(W, src, sz, sy, rw):
-        for k in (1, 2, 3):
-            zz = p.line(k)
-            send(src, W.at[quarter(s, r)], sz.at[zz], rw.at[s, r], p.peer(p.mine(zz)))
-        send(src, W.at[quarter(s, r)], sy.at[z], rw.at[s, r], p.side)
-
-    in_plane(WQ, wq_ref.at[rows_of(48 * r, 48)], szq, syq, rq)
-    in_plane(WO, wo_ref.at[rows_of(48 * r, 48)], szo, syo, ro)
-
-    def share(view, t, sems, rsems):
-        v = view(t, r)
-        send(v, v, sems.at[t, 0], rsems.at[t, r], p.across)
-        send(v, v, sems.at[t, 1], rsems.at[t, r], p.core)
-
-    def vq(t, q):
-        return WQ.at[quarter(t, q)]
-
-    def vo(t, q):
-        return WO.at[quarter(t, q)]
-
-    def gq(t, q):
-        return G.at[quarter(t, q)]
-
-    def collect(view, sy, sd, rw):
-        @pl.loop(1, 4)
-        def _(k):
-            zz = p.line(k)
-            t = p.mine(zz)
+    def share(view, sems, rsems):
+        def to_replicas(t):
             v = view(t, r)
-            p.arrived(v, rw.at[t, r], spare)
-            send(v, v, sy.at[zz], rw.at[t, r], p.side)
-            share(view, t, sd, rw)
-
-        @pl.loop(0, 4)
-        def _(k):
-            t = p.theirs(p.line(k))
-            p.arrived(view(t, r), rw.at[t, r], spare)
-            share(view, t, sd, rw)
-
-    def relay(view, sd, rw):
+            send(v, v, sems.at[t, 0], rsems.at[t, r], p.across)
+            send(v, v, sems.at[t, 1], rsems.at[t, r], p.core)
+
+        return to_replicas
+
+    def relay(view, sems, rsems, t):
+        v = view(t, p.rx)
+        p.arrived(v, rsems.at[t, p.rx], spare)
+        send(v, v, sems.at[t, 2], rsems.at[t, p.rx], p.core)
+
+    def from_core(view, rsems):
         @pl.loop(1, 8)
         def _(k):
             t = (s + k) % 8
-            v = view(t, p.rx)
-            p.arrived(v, rw.at[t, p.rx], spare)
-            send(v, v, sd.at[t, 2], rw.at[t, p.rx], p.core)
-
-        @pl.loop(1, 8)
-        def _(k):
-            t = (s + k) % 8
-            p.arrived(view(t, p.rc), rw.at[t, p.rc], spare)
-            p.arrived(view(t, p.rd), rw.at[t, p.rd], spare)
+            p.arrived(view(t, p.rc), rsems.at[t, p.rc], spare)
+            p.arrived(view(t, p.rd), rsems.at[t, p.rd], spare)
+
+    share_q, share_g = share(vq, sdq, rq), share(gq, sdg, rg)
+
+    def share_o(t):
+        send(vo(t, c), vo(t, c), sdo.at[t], ro.at[t, c], p.core)
 
     for copy in loads:
         copy.wait()
@@ -440,43 +484,34 @@
         GS[t, :, 1120:1152] = zeros
         GS[t, :, 1152:2272] = vu[:, 1120 * t : 1120 * t + 1120]
         GS[t, :, 2272:2304] = zeros
-    collect(vq, syq, sdq, rq)
-    for k in range(1, 8):
-        t = (s + k) % 8
+    g_q.step(1, share_q)
+    g_q.other(0, share_q)
+    g_q.step(2, share_q)
+    g_q.other(1, share_q)
+    g_q.step(3, share_q)
+    g_o.start(wo_ref.at[rows_of(96 * c, 96)])
+    turns = (4, 1, 6, 3, 2, 5, 7)
+
+    def give_g(i):
+        t = (s + turns[i]) % 8
         send(GS.at[t, rows_of(48 * r, 48)], gq(s, r), sg.at[t], rg.at[s, r], p.peer(t))
+
+    def take_g(i):
+        t = (s + 8 - turns[i]) % 8
+        p.arrived(gq(t, r), rg.at[t, r], spare)
+        share_g(t)
+
     own_out = (
         pltpu.make_async_copy(GS.at[s], G.at[own], loc.at[1]),
         pltpu.make_async_copy(CS, C.at[own_c], loc.at[2]),
     )
     for copy in own_out:
         copy.start()
-
-    def cot_block(t):
-        return C.at[rows_of(128 * t, 128, 128)]
-
-    def cot_on(src, t, zz, up, down):
-        if up is not None:
-            pl.when(up)(lambda: send(src, cot_block(t), scz.at[zz, 0], rc.at[t], p.peer(s + 2)))
-        if down is not None:
-            pl.when(down)(lambda: send(src, cot_block(t), scz.at[zz, 1], rc.at[t], p.peer(s - 2)))
-        send(src, cot_block(t), scy.at[zz], rc.at[t], p.side)
-
-    def cot_step(k):
-        def below():
-            t = s - 2 * k
-            p.arrived(cot_block(t), rc.at[t], spare)
-            cot_on(cot_block(t), t, z - k, z < 3, None)
-
-        def above():
-            t = s + 2 * k
-            p.arrived(cot_block(t), rc.at[t], spare)
-            cot_on(cot_block(t), t, z + k, None, z > 0)
-
-        pl.when(z >= k)(below)
-        pl.when(z + k <= 3)(above)
-
-    collect(vo, syo, sdo, ro)
-    cot_on(CS, s, z, z < 3, z > 0)
+    g_q.other(2, share_q)
+    give_g(0)
+    g_q.other(3, share_q)
+    give_g(1)
+
     @pl.loop(1, 8)
     def _(k):
         t = (s + k) % 8
@@ -489,7 +524,32 @@
         gains[1:2, 192 * t : 192 * t + 192] = row[:, 512:704]
     x = x_ref[...].astype(F32)
     a1[...] = (x * inverse_norm(x) * gains[0:1, :]).astype(BF)
-    relay(vq, sdq, rq)
+
+    def relay_q(t):
+        relay(vq, sdq, rq, t)
+
+    g_o.step(1, share_o)
+    give_g(2)
+    g_o.other(0, share_o)
+    relay_q(p.mine(p.line(1)))
+    relay_q(p.theirs(p.line(0)))
+    g_o.step(2, share_o)
+    give_g(3)
+    g_o.other(1, share_o)
+    relay_q(p.mine(p.line(2)))
+    relay_q(p.theirs(p.line(1)))
+    g_o.step(3, share_o)
+    give_g(4)
+    g_c.start(CS)
+    take_g(0)
+    take_g(1)
+    relay_q(p.mine(p.line(3)))
+    relay_q(p.theirs(p.line(2)))
+    relay_q(p.theirs(p.line(3)))
+    take_g(2)
+    give_g(5)
+    give_g(6)
+    from_core(vq, rq)
     cosine, sine = cos_ref[...], sin_ref[...]
     for j in range(4):
         co = pl.ds(512 * j, 512)
@@ -505,7 +565,6 @@
                 keys[h - 12] = u.astype(BF)
             else:
                 values[h - 14] = u.astype(BF)
-    cot_step(1)
     save = (pltpu.make_async_copy(WQ, WQ_out, loc.at[3]), pltpu.make_async_copy(WO, WO_out, loc.at[4]))
     save[0].start()
     open_to = allow_ref[...] != 0
@@ -518,51 +577,52 @@
         out = dot(soft.astype(BF), values[g]).astype(BF)
         for i in range(6):
             att[:, pl.ds(128 * (6 * g + i), 128)] = out[128 * i : 128 * i + 128]
-    relay(vo, sdo, ro)
+
+    for i in (3, 4):
+        take_g(i)
+    g_o.other(2, share_o)
+    g_o.other(3, share_o)
+
+    @pl.loop(1, 8)
+    def _(k):
+        t = (s + k) % 8
+        p.arrived(vo(t, 1 - c), ro.at[t, 1 - c], spare)
+
     save[1].start()
     for j in range(3):
         co = pl.ds(512 * j, 512)
         mid[:, co] = x[:, 512 * j : 512 * j + 512] + dot(att[...], WO[:, co])
     hidden = mid[...]
     a2[...] = (hidden * inverse_norm(hidden) * gains[1:2, :]).astype(BF)
-
-    @pl.loop(1, 8)
+    g_c.step(1)
+    take_g(5)
+    g_c.step(2)
+    take_g(6)
+    g_c.step(3)
+
+    for k in turns:
+        relay(gq, sdg, rg, (s + 8 - k) % 8)
+
+    from_core(gq, rg)
+
+    @pl.loop(0, 4)
     def _(k):
-        t = (s + k) % 8
-        p.arrived(gq(t, r), rg.at[t, r], spare)
-        share(gq, t, sdg, rg)
-
-    cot_step(2)
-    cot_step(3)
-    relay(gq, sdg, rg)
-
-    @pl.loop(0, 4)
-    def _(zz):
-        t = p.theirs(zz)
-        p.arrived(cot_block(t), rc.at[t], spare)
+        g_c.other(k)
+
+    g_q.finish()
+    g_o.finish()
+    g_c.finish()
 
     @pl.loop(1, 8)
     def _(k):
         t = (s + k) % 8
         p.sent(S.at[t], ss.at[t], spare)
         p.sent(gq(t, r), sg.at[t], spare)
+        p.sent(vo(t, c), sdo.at[t], spare)
         for d in range(3):
             p.sent(vq(t, r), sdq.at[t, d], spare)
-            p.sent(vo(t, r), sdo.at[t, d], spare)
             p.sent(gq(t, r), sdg.at[t, d], spare)
 
-    for zz in range(4):
-        p.sent(vq(s, r), syq.at[zz], spare)
-        p.sent(vo(s, r), syo.at[zz], spare)
-        p.sent(CS, scy.at[zz], spare)
-
-        @pl.when(zz != z)
-        def _():
-            p.sent(vq(s, r), szq.at[zz], spare)
-            p.sent(vo(s, r), szo.at[zz], spare)
-
-        pl.when((zz <= z) & (z < 3))(lambda: p.sent(CS, scz.at[zz, 0], spare))
-        pl.when((zz >= z) & (z > 0))(lambda: p.sent(CS, scz.at[zz, 1], spare))
     for copy in own_out + save:
         copy.wait()
 
@@ -580,8 +640,8 @@
         scratch_shapes=[
             low(1536, 2048), low(1536, 1536), low(192, 8960), low(192, 8960), low(8, 192, 2304), low(128, 1536),
             low(8, 16, 768), full(8, 2048),
-            DMA((8, 4)), DMA((8, 4)), DMA((8, 4)), DMA((8,)), DMA((8,)),
-            DMA((4,)), DMA((4,)), DMA((8, 3)), DMA((4,)), DMA((4,)), DMA((8, 3)),
+            DMA((8, 4)), DMA((8, 2)), DMA((8, 4)), DMA((8,)), DMA((8,)),
+            DMA((4, 2)), DMA((4,)), DMA((8, 3)), DMA((4, 2)), DMA((4,)), DMA((8,)),
             DMA((8,)), DMA((8, 3)), DMA((4, 2)), DMA((4,)), DMA((8,)), DMA((6,)),
         ],
         compiler_params=pltpu.CompilerParams(collective_id=0, has_side_effects=True, vmem_limit_bytes=56 << 20),
@@ -590,9 +650,9 @@
 
 
 def feed_body(
-    n_ref, c_hbm, g_hbm, d_hbm, DS, PO_out, GQ, OD,
-    vG, vD, vC, N, NT, MX, MT, H, PD, PO, YD, ZD, GD, RCd, RXd, RC, RX,
-    rn, syn, szn, ryd, rzd, syd, szd, scd, rcd, sxd, rxd, sfd, rfd, scg, rcg, sxg, rxg, lq, loc,
+    n_ref, c_hbm, g_hbm, d_hbm, DS, PO_out, GC, OD,
+    vG, vD, vC, N, NT, MX, MT, H, PD, PO, YD, ZD, YO, GD, RCd, RXd, RC, RX,
+    rn, syn, szn, ryd, rzd, syd, szd, syo, ryo, scd, rcd, sxd, rxd, sfd, scg, rcg, sx, rx, lq, lo, loc,
 ):
     p = Place()
     r, s, c, y, z = p.r, p.s, p.c, p.y, p.z
@@ -610,37 +670,43 @@
     for copy in loads:
         copy.start()
     p.greet(range(1, 8))
-    send(n_ref, block(s), syn.at[z], rn.at[s], p.side)
-    for k in (1, 2, 3):
-        zz = p.line(k)
-        send(n_ref, block(s), szn.at[zz], rn.at[s], p.peer(p.mine(zz)))
+    g_n = Gather(p, spare, block, lambda t: rn.at[t], szn, syn)
+    g_n.start(n_ref)
     vD[1120:1152, :] = jnp.zeros((32, 1536), BF)
     for copy in loads:
         copy.wait()
 
-    def add_d(k):
+    def side_d(k):
+        zz = p.line(k)
+        send(PD.at[p.theirs(zz)], YD.at[zz], syd.at[zz], ryd.at[zz], p.side)
+
+    def side_o(k):
+        zz = p.line(k)
+        send(PO.at[p.theirs(zz)], YO.at[zz], syo.at[zz], ryo.at[zz], p.side)
+
+    def step_d(k):
         zz = p.line(k)
         t = p.mine(zz)
-        p.arrived(YD.at[zz], ryd.at[zz], spare)
-        PD[t] = (PD[t].astype(F32) + YD[zz].astype(F32)).astype(BF)
-
-    def send_d(k):
-        zz = p.line(k)
-        send(PD.at[p.mine(zz)], ZD.at[z], szd.at[zz], rzd.at[z], p.peer(p.mine(zz)))
+
+        def add(ref, sem):
+            p.arrived(ref, sem, spare)
+            PD[t] = (PD[t].astype(F32) + ref[...].astype(F32)).astype(BF)
+
+        add(YD.at[zz], ryd.at[zz])
+        p.reduce_step(
+            zz,
+            lambda slot: add(ZD.at[slot], rzd.at[slot]),
+            lambda slot, device: send(PD.at[t], ZD.at[slot], szd.at[zz], rzd.at[slot], device),
+        )
+
+    at_end = (z == 0) | (z == 3)
 
     @pl.loop(0, 4)
     def _(k):
         zz = p.line(k)
 
-        @pl.when(k < 3)
-        def _():
-            zn = p.line(k + 1)
-            t = p.mine(zn)
-            p.arrived(block(t), rn.at[t], spare)
-            send(block(t), block(t), syn.at[zn], rn.at[t], p.side)
-
-        to = p.theirs(zz)
-        p.arrived(block(to), rn.at[to], spare)
+        pl.when(k < 3)(lambda: g_n.step(k + 1))
+        g_n.other(k)
         rows = rows_of(256 * zz, 256, 256)
         X = N[rows]
         NT[:, rows] = X.T
@@ -661,7 +727,7 @@
             part = dot_nt(H[rows], vG[co]).astype(BF)
             PD[2 * zz, :, co] = part[:128]
             PD[2 * zz + 1, :, co] = part[128:]
-        send(PD.at[to], YD.at[zz], syd.at[zz], ryd.at[zz], p.side)
+        pl.when(k == 3)(lambda: side_d(3))
         for j in range(3):
             co = pl.ds(512 * j, 512)
             part = dot(MX[...], vD[:, co]).astype(BF)
@@ -669,16 +735,25 @@
             PO[2 * zz + 1, :, co] = part[128:]
         MT[:, rows] = MX[...].T
 
-        @pl.when(k >= 1)
-        def _():
-            add_d(k - 1)
-
-        @pl.when(k >= 2)
-        def _():
-            send_d(k - 1)
-
-    save = pltpu.make_async_copy(PO, PO_out, loc.at[1])
-    save.start()
+        pl.when(k == 2)(lambda: side_o(2))
+
+    side_d(2)
+    side_d(1)
+    side_d(0)
+
+    def save_o(t, i):
+        pltpu.make_async_copy(PO.at[t], PO_out.at[t], lo.at[i]).start()
+
+    def add_o(k):
+        zz = p.line(k)
+        t = p.mine(zz)
+        p.arrived(YO.at[zz], ryo.at[zz], spare)
+        PO[t] = (PO[t].astype(F32) + YO[zz].astype(F32)).astype(BF)
+        save_o(t, k)
+
+    for k in (0, 1, 3):
+        save_o(p.mine(p.line(k)), k)
+        save_o(p.theirs(p.line(k)), 4 + k)
 
     def chunk(i):
         return rows_of(288 * i, 288)
@@ -705,32 +780,10 @@
         p.arrived(RXd.at[chunk(i)], rxd.at[i], spare)
         q = cols(r)
         GD[chunk(i), q] = (GD[chunk(i), q].astype(F32) + RXd[chunk(i)].astype(F32)).astype(BF)
-        src, dst = GD.at[chunk(i), q], OD.at[r, chunk(i)]
-        pltpu.make_async_copy(src, dst, sfd.at[i, 3]).start()
-        send(src, dst, sfd.at[i, 0], rfd.at[i, r], p.across)
-        send(src, dst, sfd.at[i, 1], rfd.at[i, r], p.core)
-
-    def down_relay(i):
-        v = OD.at[p.rx, chunk(i)]
-        p.arrived(v, rfd.at[i, p.rx], spare)
-        send(v, v, sfd.at[i, 2], rfd.at[i, p.rx], p.core)
-
-    @pl.loop(0, 6)
-    def _(i):
-        pl.when(i < 4)(lambda: down_term(i))
-        pl.when((i >= 1) & (i < 5))(lambda: down_chip(i - 1))
-        pl.when(i >= 2)(lambda: down_whole(i - 2))
-
-        @pl.when(i == 1)
-        def _():
-            add_d(3)
-            send_d(3)
-
-    def own(k):
-        return (s + 1 + k) % 8
+        pltpu.make_async_copy(GD.at[chunk(i), q], OD.at[chunk(i)], sfd.at[i]).start()
 
     def pair_term(k):
-        t = own(k)
+        t = (s + 1 + k) % 8
         rows = rows_of(192 * t, 192)
         for j in range(3):
             co = pl.ds(768 * j, 768)
@@ -739,107 +792,290 @@
             send(vG.at[quarter(t, 2 * xx + 1 - c)], RC.at[t, xx], scg.at[t, xx], rcg.at[t, xx], p.core)
 
     def pair_chip(k):
-        t = own(k)
+        t = (s + 1 + k) % 8
         for xx in range(2):
             p.arrived(RC.at[t, xx], rcg.at[t, xx], spare)
             q = quarter(t, 2 * xx + c)
             vG[q] = (vG[q].astype(F32) + RC[t, xx].astype(F32)).astype(BF)
-        send(vG.at[quarter(t, p.rx)], RX.at[t], sxg.at[t], rxg.at[t], p.across)
+
+            @pl.when(k >= 3)
+            def _():
+                pltpu.make_async_copy(vG.at[q], GC.at[t, xx], lq.at[t, xx]).start()
+
+        @pl.when(k < 3)
+        def _():
+            send(vG.at[quarter(t, p.rx)], RX.at[k], sx.at[k], rx.at[k], p.across)
 
     def pair_whole(k):
-        t = own(k)
-        p.arrived(RX.at[t], rxg.at[t], spare)
+        t = (s + 1 + k) % 8
         q = quarter(t, r)
-        vG[q] = (vG[q].astype(F32) + RX[t].astype(F32)).astype(BF)
-        pltpu.make_async_copy(vG.at[q], GQ.at[t], lq.at[t]).start()
-
-    @pl.loop(0, 10)
+        p.arrived(RX.at[k], rx.at[k], spare)
+        vG[q] = (vG[q].astype(F32) + RX[k].astype(F32)).astype(BF)
+        pltpu.make_async_copy(vG.at[q], GC.at[t, p.x], lq.at[t, 0]).start()
+
+    @pl.loop(0, 5)
+    def _(i):
+        pl.when(i < 4)(lambda: down_term(i))
+        pl.when(i >= 1)(lambda: down_chip(i - 1))
+
+    @pl.loop(0, 9)
     def _(i):
         pl.when(i < 8)(lambda: pair_term(i))
-        pl.when((i >= 1) & (i < 9))(lambda: pair_chip(i - 1))
-        pl.when(i >= 2)(lambda: pair_whole(i - 2))
-        pl.when(i < 4)(lambda: down_relay(i))
-
-    acc = PD[s].astype(F32)
-    for k in (1, 2, 3):
-        zz = p.line(k)
-        p.arrived(ZD.at[zz], rzd.at[zz], spare)
-        acc = acc + ZD[zz].astype(F32)
-    DS[...] = acc
+        pl.when(i >= 1)(lambda: pair_chip(i - 1))
+
+        pl.when((i == 3) & at_end)(lambda: step_d(3))
+
+    pl.when(at_end)(lambda: step_d(2))
+    pl.when(jnp.logical_not(at_end))(lambda: step_d(3))
+
+    @pl.loop(0, 4)
+    def _(i):
+        down_whole(i)
+
+    pl.when(at_end)(lambda: step_d(1))
+    pl.when(jnp.logical_not(at_end))(lambda: step_d(2))
+    zo = p.line(2)
+    to = p.mine(zo)
+    p.arrived(YO.at[zo], ryo.at[zo], spare)
+    PO[to] = (PO[to].astype(F32) + YO[zo].astype(F32)).astype(BF)
+    save_o(to, 2)
+
+    @pl.loop(0, 3)
+    def _(k):
+        pair_whole(k)
+
+    pl.when(jnp.logical_not(at_end))(lambda: step_d(1))
+    step_d(0)
+    DS[...] = PD[s].astype(F32)
 
     @pl.loop(0, 8)
     def _(t):
         for xx in range(2):
             p.sent(RC.at[t, xx], scg.at[t, xx], spare)
-        p.sent(RX.at[t], sxg.at[t], spare)
-        pltpu.make_async_copy(RX.at[t], GQ.at[t], lq.at[t]).wait()
+
+            @pl.when(((t + 7 - s) % 8 >= 3) | (xx == 0))
+            def _():
+                pltpu.make_async_copy(RC.at[t, xx], GC.at[t, xx], lq.at[t, xx]).wait()
 
     @pl.loop(0, 4)
     def _(i):
-        for q in (p.rc, p.rd):
-            p.arrived(OD.at[q, chunk(i)], rfd.at[i, q], spare)
-        for d in range(3):
-            p.sent(OD.at[r, chunk(i)], sfd.at[i, d], spare)
-        pltpu.make_async_copy(OD.at[r, chunk(i)], OD.at[r, chunk(i)], sfd.at[i, 3]).wait()
+        pltpu.make_async_copy(RXd.at[chunk(i)], OD.at[chunk(i)], sfd.at[i]).wait()
         for xx in range(2):
             p.sent(RCd.at[xx, chunk(i)], scd.at[i, xx], spare)
         p.sent(RXd.at[chunk(i)], sxd.at[i], spare)
-        p.sent(block(s), syn.at[i], spare)
         p.sent(YD.at[i], syd.at[i], spare)
 
         @pl.when(i != z)
         def _():
-            p.sent(block(s), szn.at[i], spare)
             p.sent(ZD.at[i], szd.at[i], spare)
 
-    save.wait()
+    g_n.finish()
+    p.sent(YO.at[0], syo.at[p.line(2)], spare)
+    for k in range(3):
+        p.sent(RX.at[k], sx.at[k], spare)
+    for i in range(8):
+        if i == 6:
+            continue
+        pltpu.make_async_copy(PO.at[s], PO_out.at[s], lo.at[i]).wait()
 
 
 def feed_forward(n2, cot, gate_up, w_down):
     return pl.pallas_call(
         feed_body,
-        out_shape=(shaped(128, 1536, dtype=F32), shaped(8, 128, 1536), shaped(8, 48, 2304), shaped(4, 1152, 384)),
+        out_shape=(shaped(128, 1536, dtype=F32), shaped(8, 128, 1536), shaped(8, 2, 48, 2304), shaped(1152, 384)),
         in_specs=[HBM] * 4,
         out_specs=(VMEM, HBM, HBM, HBM),
         scratch_shapes=[
             low(1536, 2304), low(1152, 1536), low(1024, 1536), low(1024, 1536), low(1536, 1024), low(256, 1152),
-            low(1152, 1024), low(1024, 2304), low(8, 128, 1536), low(8, 128, 1536), low(4, 128, 1536), low(4, 128, 1536),
-            low(1152, 1536), low(2, 1152, 384), low(1152, 384), low(8, 2, 48, 2304), low(8, 48, 2304),
-            DMA((8,)), DMA((4,)), DMA((4,)), DMA((4,)), DMA((4,)), DMA((4,)), DMA((4,)),
-            DMA((4, 2)), DMA((4, 2)), DMA((4,)), DMA((4,)), DMA((4, 4)), DMA((4, 4)),
-            DMA((8, 2)), DMA((8, 2)), DMA((8,)), DMA((8,)), DMA((8,)), DMA((5,)),
+            low(1152, 1024), low(1024, 2304), low(8, 128, 1536), low(8, 128, 1536), low(4, 128, 1536), low(5, 128, 1536), low(4, 128, 1536),
+            low(1152, 1536), low(2, 1152, 384), low(1152, 384), low(8, 2, 48, 2304), low(3, 48, 2304),
+            DMA((8,)), DMA((4,)), DMA((4, 2)), DMA((4,)), DMA((5,)), DMA((4,)), DMA((4,)), DMA((4,)), DMA((4,)),
+            DMA((4, 2)), DMA((4, 2)), DMA((4,)), DMA((4,)), DMA((4,)), DMA((8, 2)), DMA((8, 2)), DMA((3,)), DMA((3,)), DMA((8, 2)), DMA((8,)), DMA((5,)),
         ],
         compiler_params=pltpu.CompilerParams(collective_id=1, has_side_effects=True, vmem_limit_bytes=62 << 20),
         name="feed_forward",
     )(n2, cot, gate_up, w_down)
 
 
+class RowSums:
+    def __init__(self, p, spare, total, chip, side, far, across, out, sems):
+        self.p, self.spare, self.total, self.chip, self.side = p, spare, total, chip, side
+        self.far, self.across, self.out, self.sems = far, across, out, sems
+
+    def own(self, k):
+        p = self.p
+        return 2 * p.line(3 - k % 4) + (1 - p.y + (k // 4) * (2 * p.y - 1))
+
+    def to_core(self, t):
+        p = self.p
+        for xx in range(2):
+            send(
+                self.total.at[quarter(t, 2 * xx + 1 - p.c)], self.chip.at[t, xx],
+                self.sems[0].at[t, xx], self.sems[1].at[t, xx], p.core,
+            )
+
+    def add(self, q, ref, sem):
+        self.p.arrived(ref, sem, self.spare)
+        self.total[q] = (self.total[q].astype(F32) + ref[...].astype(F32)).astype(BF)
+
+    def on_chip(self, k):
+        p, t = self.p, self.own(k)
+        for xx in range(2):
+            q = quarter(t, 2 * xx + p.c)
+            self.add(q, self.chip.at[t, xx], self.sems[1].at[t, xx])
+
+    def aside(self, k):
+        p, t = self.p, self.own(k)
+        for xx in range(2):
+            at = t // 2, xx
+            q = quarter(t, 2 * xx + p.c)
+            send(self.total.at[q], self.side.at[at], self.sems[2].at[at], self.sems[3].at[at], p.side)
+
+    def on_line(self, k):
+        p = self.p
+        zz = p.line(3 - k)
+        t = p.mine(zz)
+        for xx in range(2):
+            q = quarter(t, 2 * xx + p.c)
+            self.add(q, self.side.at[zz, xx], self.sems[3].at[zz, xx])
+            p.reduce_step(
+                zz,
+                lambda slot: self.add(q, self.far.at[slot, xx], self.sems[5].at[slot, xx]),
+                lambda slot, device: send(
+                    self.total.at[q], self.far.at[slot, xx], self.sems[4].at[zz, xx], self.sems[5].at[slot, xx], device
+                ),
+            )
+
+    def at_owner(self):
+        p = self.p
+        send(self.total.at[quarter(p.s, p.rx)], self.across, self.sems[6].at[3], self.sems[7].at[4], p.across)
+
+    def spread(self):
+        p = self.p
+        p.arrived(self.across, self.sems[7].at[4], self.spare)
+        q = quarter(p.s, p.r)
+        self.out[p.r] = (self.total[q].astype(F32) + self.across[...].astype(F32)).astype(BF)
+        mine = self.out.at[p.r]
+        send(mine, mine, self.sems[6].at[0], self.sems[7].at[p.r], p.across)
+        send(mine, mine, self.sems[6].at[1], self.sems[7].at[p.r], p.core)
+
+    def pass_on(self):
+        p = self.p
+        v = self.out.at[p.rx]
+        p.arrived(v, self.sems[7].at[p.rx], self.spare)
+        send(v, v, self.sems[6].at[2], self.sems[7].at[p.rx], p.core)
+
+    def finish(self):
+        p = self.p
+        for q in (p.rc, p.rd):
+            p.arrived(self.out.at[q], self.sems[7].at[q], self.spare)
+        for d in range(3):
+            p.sent(self.out.at[p.r], self.sems[6].at[d], self.spare)
+        p.sent(self.across, self.sems[6].at[3], self.spare)
+
+        @pl.loop(0, 8)
+        def _(t):
+            for xx in range(2):
+                p.sent(self.chip.at[t, xx], self.sems[0].at[t, xx], self.spare)
+
+        @pl.loop(0, 4)
+        def _(i):
+            for xx in range(2):
+                p.sent(self.side.at[i, xx], self.sems[2].at[i, xx], self.spare)
+
+                @pl.when(i != p.z)
+                def _():
+                    p.sent(self.far.at[i, xx], self.sems[4].at[i, xx], self.spare)
+
+    @staticmethod
+    def buffers(width):
+        return [low(8, 2, 48, width), low(4, 2, 48, width), low(5, 2, 48, width), low(48, width)]
+
+    @staticmethod
+    def semaphores():
+        return [DMA((8, 2)), DMA((8, 2)), DMA((4, 2)), DMA((4, 2)), DMA((4, 2)), DMA((5, 2)), DMA((4,)), DMA((5,))]
+
+
 def attend_back_body(
     ds_ref, mid_ref, x_ref, cot_ref, gains, cos_ref, sin_ref, queries, keys, values, probs, att, a1,
-    wq_ref, wo_ref, po_ref, gq_ref,
-    out_ref, gtok_ref, OG, OWq, OWo,
-    vQ, vO, PO, YO, ZO, own_g, dmid, DB, dA, dj, AT, SM, RCq, RXq, Yq, Zq, RCo, Yo, Zo, RXo,
-    sa, ra, sf, syo, ryo, szo, rzo, scq, rcq, sxq, rxq, syq, ryq, szq, rzq, sfq, rfq,
-    sco, rco, syw, ryw, szw, rzw, sfo, rfo, loc,
+    wq_ref, wo_ref, po_ref, gc_ref, od_ref,
+    out_ref, gtok_ref, OG, OD, OWq, OWo,
+    vQ, vO, PO, YO, ZO, GX, RX, DQ, dmid, DB, dA, dj, AT, SM, RCq, Yq, Zq, RXq, RCo, Yo, Zo, RXo,
+    sx, rx, sa, ra, sf, sd, rd, syo, ryo, szo, rzo, *sems,
 ):
     p = Place()
     r, s, c, y, z = p.r, p.s, p.c, p.y, p.z
+    loc = sems[-1]
     spare = loc.at[0]
+    q_sums = RowSums(p, spare, vQ, RCq, Yq, Zq, RXq, OWq, sems[0:8])
+    o_sums = RowSums(p, spare, vO, RCo, Yo, Zo, RXo, OWo, sems[8:16])
     loads = (
         pltpu.make_async_copy(wo_ref, vO, loc.at[1]),
         pltpu.make_async_copy(wq_ref, vQ.at[:, 0:2048], loc.at[2]),
         pltpu.make_async_copy(po_ref, PO, loc.at[3]),
-        pltpu.make_async_copy(gq_ref.at[s], own_g, loc.at[4]),
+        pltpu.make_async_copy(gc_ref.at[:, p.x], GX, loc.at[4]),
+        pltpu.make_async_copy(od_ref, DQ, loc.at[5]),
     )
     for copy in loads:
         copy.start()
     p.greet(range(1, 8))
-    for k in range(1, 8):
-        t = (s + k) % 8
-        send(gq_ref.at[t], OG.at[r, s], sa.at[t], ra.at[s, r], p.peer(t))
-    for k in range(4):
-        zz = p.line(3 - k)
+
+    def owner(k):
+        return (s + 1 + k) % 8
+
+    for k in range(3, 8):
+        t = owner(k)
+        send(gc_ref.at[t, 1 - p.x], RX.at[t], sx.at[t], rx.at[t], p.across)
+    for k in range(3):
+        t = owner(k)
+        send(gc_ref.at[t, p.x], OG.at[r, s], sa.at[t], ra.at[s, r], p.peer(t))
+
+    def send_out(k):
+        zz = p.line(k)
         send(po_ref.at[p.theirs(zz)], YO.at[zz], syo.at[zz], ryo.at[zz], p.side)
+
+    send_out(3)
+
+    def step_out(k):
+        zz = p.line(k)
+        t = p.mine(zz)
+
+        def add(ref, sem):
+            p.arrived(ref, sem, spare)
+            PO[t] = (PO[t].astype(F32) + ref[...].astype(F32)).astype(BF)
+
+        if k != 2:
+            add(YO.at[zz], ryo.at[zz])
+        p.reduce_step(
+            zz,
+            lambda slot: add(ZO.at[slot], rzo.at[slot]),
+            lambda slot, device: send(PO.at[t], ZO.at[slot], szo.at[zz], rzo.at[slot], device),
+        )
+
+    def ends(*steps):
+        @pl.when((z == 0) | (z == 3))
+        def _():
+            for f, k in steps:
+                f(k)
+
+    def middles(*steps):
+        @pl.when((z == 1) | (z == 2))
+        def _():
+            for f, k in steps:
+                f(k)
+
+    def pair_whole(k):
+        t = owner(k)
+        p.arrived(RX.at[t], rx.at[t], spare)
+        GX[t] = (GX[t].astype(F32) + RX[t].astype(F32)).astype(BF)
+
+        @pl.when(k < 7)
+        def _():
+            send(GX.at[t], OG.at[r, s], sa.at[t], ra.at[s, r], p.peer(t))
+
+        @pl.when(k == 7)
+        def _():
+            pltpu.make_async_copy(GX.at[t], OG.at[r, s], loc.at[4]).start()
 
     def share(t):
         v = OG.at[r, t]
@@ -860,26 +1096,20 @@
     AT[...] = att[...].T
     for copy in loads:
         copy.wait()
-    keep = pltpu.make_async_copy(own_g, OG.at[r, s], loc.at[4])
+    keep = pltpu.make_async_copy(DQ, OD.at[r], loc.at[5])
     keep.start()
     for j in range(3):
         part = dot_nt(DB[...], vO[pl.ds(512 * j, 512)]).astype(BF)
         for i in range(4):
             h = 4 * j + i
             dA[h // 6, pl.ds(128 * (h % 6), 128), :] = part[:, 128 * i : 128 * i + 128]
-
-    def own(k):
-        return 2 * p.line(3 - k % 4) + (1 - y + (k // 4) * (2 * y - 1))
-
     for j in range(3):
         co = pl.ds(512 * j, 512)
         vO[:, co] = dot(AT[...], DB[:, co]).astype(BF)
 
     @pl.loop(0, 8)
     def _(k):
-        t = own(k)
-        for xx in range(2):
-            send(vO.at[quarter(t, 2 * xx + 1 - c)], RCo.at[t, xx], sco.at[t, xx], rco.at[t, xx], p.core)
+        o_sums.to_core(o_sums.own(k))
 
     def heads(g):
         grad, soft = dA[g], probs[g]
@@ -897,15 +1127,11 @@
 
     @pl.loop(0, 8)
     def _(k):
-        t = own(k)
-        for xx in range(2):
-            p.arrived(RCo.at[t, xx], rco.at[t, xx], spare)
-            q = quarter(t, 2 * xx + c)
-            vO[q] = (vO[q].astype(F32) + RCo[t, xx].astype(F32)).astype(BF)
-
-            @pl.when(k < 4)
-            def _():
-                send(vO.at[q], Yo.at[t // 2, xx], syw.at[t // 2, xx], ryw.at[t // 2, xx], p.side)
+        o_sums.on_chip(k)
+
+    o_sums.aside(0)
+    o_sums.aside(1)
+    ends((step_out, 3))
 
     heads(1)
     joined_grad = dj[...]
@@ -933,138 +1159,91 @@
 
     @pl.loop(0, 8)
     def _(k):
-        t = own(k)
+        t = q_sums.own(k)
         rows = rows_of(192 * t, 192)
         for j in range(2):
             co = pl.ds(1024 * j, 1024)
             vQ[rows, co] = dot(AT[rows], dj[:, co]).astype(BF)
         vQ[rows, 2048:2176] = jnp.zeros((192, 128), BF)
         vQ[rows_of(192 * t, 16), 2048:2176] = SM[t].astype(BF)
-        for xx in range(2):
-            send(vQ.at[quarter(t, 2 * xx + 1 - c)], RCq.at[t, xx], scq.at[t, xx], rcq.at[t, xx], p.core)
-
-    def q_chip(k):
-        t = own(k)
-        for xx in range(2):
-            p.arrived(RCq.at[t, xx], rcq.at[t, xx], spare)
-            q = quarter(t, 2 * xx + c)
-            vQ[q] = (vQ[q].astype(F32) + RCq[t, xx].astype(F32)).astype(BF)
-        send(vQ.at[quarter(t, p.rx)], RXq.at[t], sxq.at[t], rxq.at[t], p.across)
-
-    def q_whole(k):
-        t = own(k)
-        p.arrived(RXq.at[t], rxq.at[t], spare)
-        q = quarter(t, r)
-        vQ[q] = (vQ[q].astype(F32) + RXq[t].astype(F32)).astype(BF)
-
-        @pl.when(k < 4)
-        def _():
-            send(vQ.at[q], Yq.at[t // 2], syq.at[t // 2], ryq.at[t // 2], p.side)
-
-        @pl.when(k >= 4)
-        def _():
-            p.arrived(Yq.at[t // 2], ryq.at[t // 2], spare)
-            vQ[q] = (vQ[q].astype(F32) + Yq[t // 2].astype(F32)).astype(BF)
-
-        @pl.when((k >= 4) & (k < 7))
-        def _():
-            send(vQ.at[q], Zq.at[z], szq.at[t // 2], rzq.at[z], p.peer(t))
-
-    def out_line(k):
-        zz = p.line(3 - k)
-        t = p.mine(zz)
-        p.arrived(YO.at[zz], ryo.at[zz], spare)
-        PO[t] = (PO[t].astype(F32) + YO[zz].astype(F32)).astype(BF)
-
-        @pl.when(k < 3)
-        def _():
-            send(PO.at[t], ZO.at[z], szo.at[zz], rzo.at[z], p.peer(t))
-
-    def w_line(k):
-        zz = p.line(3 - k)
-        t = p.mine(zz)
-        for xx in range(2):
-            p.arrived(Yo.at[zz, xx], ryw.at[zz, xx], spare)
-            q = quarter(t, 2 * xx + c)
-            vO[q] = (vO[q].astype(F32) + Yo[zz, xx].astype(F32)).astype(BF)
-
-            @pl.when(k < 3)
-            def _():
-                send(vO.at[q], Zo.at[z, xx], szw.at[zz, xx], rzw.at[z, xx], p.peer(t))
+        q_sums.to_core(t)
 
     @pl.loop(0, 8)
     def _(k):
-        q_chip(k)
-    share_own = pltpu.make_async_copy(own_g, OG.at[r, s], loc.at[4])
-    share_own.wait()
-    share(s)
-
-    @pl.loop(1, 8)
-    def _(k):
+        q_sums.on_chip(k)
+
+
+    def take(k):
         t = (s + 8 - k) % 8
         p.arrived(OG.at[r, t], ra.at[t, r], spare)
         share(t)
 
-    @pl.loop(0, 4)
-    def _(k):
-        out_line(k)
-        w_line(k)
-
-    @pl.loop(0, 8)
-    def _(k):
-        q_whole(k)
-    acc = PO[s].astype(F32) + mid_ref[...]
-    for k in (1, 2, 3):
-        zz = p.line(k)
-        p.arrived(ZO.at[zz], rzo.at[zz], spare)
-        acc = acc + ZO[zz].astype(F32)
-    out_ref[...] = acc.astype(BF)
-    for xx in range(2):
-        q = quarter(s, 2 * xx + c)
-        acc = vO[q].astype(F32)
-        for k in (1, 2, 3):
-            zz = p.line(k)
-            p.arrived(Zo.at[zz, xx], rzw.at[zz, xx], spare)
-            acc = acc + Zo[zz, xx].astype(F32)
-        vO[q] = acc.astype(BF)
-    send(vO.at[quarter(s, p.rx)], RXo, sfo.at[3], rfo.at[4], p.across)
-    acc = vQ[quarter(s, r)].astype(F32)
-    for k in (1, 2, 3):
-        zz = p.line(k)
-        p.arrived(Zq.at[zz], rzq.at[zz], spare)
-        acc = acc + Zq[zz].astype(F32)
-    OWq[r] = acc.astype(BF)
-
-    def spread(O, sems, rsems):
-        send(O.at[r], O.at[r], sems.at[0], rsems.at[r], p.across)
-        send(O.at[r], O.at[r], sems.at[1], rsems.at[r], p.core)
-
-    def pass_on(O, sems, rsems):
-        v = O.at[p.rx]
-        p.arrived(v, rsems.at[p.rx], spare)
-        send(v, v, sems.at[2], rsems.at[p.rx], p.core)
-
-    spread(OWq, sfq, rfq)
-    p.arrived(RXo, rfo.at[4], spare)
-    OWo[r] = (vO[quarter(s, r)].astype(F32) + RXo[...].astype(F32)).astype(BF)
-    spread(OWo, sfo, rfo)
-
-    @pl.loop(0, 8)
+    o_line, q_line = o_sums.on_line, q_sums.on_line
+    o_sums.aside(2)
+    o_sums.aside(3)
+    ends((step_out, 2), (o_line, 0))
+    pair_whole(3)
+    pair_whole(4)
+    pair_whole(5)
+    middles((step_out, 3), (step_out, 2), (o_line, 0))
+    pair_whole(6)
+    ends((o_line, 1))
+    pair_whole(7)
+    send(od_ref, OD.at[r], sd.at[0], rd.at[r], p.across)
+    send(od_ref, OD.at[r], sd.at[1], rd.at[r], p.core)
+    q_sums.aside(0)
+    q_sums.aside(1)
+    middles((o_line, 1))
+    ends((o_line, 2))
+    take(1)
+    middles((o_line, 2))
+    o_line(3)
+    o_sums.at_owner()
+    q_sums.aside(2)
+    q_sums.aside(3)
+    take(2)
+    take(3)
+    ends((q_line, 0))
+    take(4)
+    middles((q_line, 0))
+    ends((q_line, 1))
+    o_sums.spread()
+    send_out(1)
+    take(5)
+    middles((q_line, 1))
+    ends((q_line, 2))
+    send_out(0)
+    take(6)
+    middles((q_line, 2))
+    take(7)
+    pltpu.make_async_copy(GX.at[s], OG.at[r, s], loc.at[4]).wait()
+    share(s)
+    q_line(3)
+    q_sums.at_owner()
+    step_out(1)
+    q_sums.spread()
+    step_out(0)
+    out_ref[...] = (PO[s].astype(F32) + mid_ref[...]).astype(BF)
+    o_sums.pass_on()
+    v = OD.at[p.rx]
+    p.arrived(v, rd.at[p.rx], spare)
+    send(v, v, sd.at[2], rd.at[p.rx], p.core)
+
+    @pl.loop(1, 9)
     def _(k):
         t = (s + 8 - k) % 8
         v = OG.at[p.rx, t]
         p.arrived(v, ra.at[t, p.rx], spare)
         send(v, v, sf.at[t, 2], ra.at[t, p.rx], p.core)
 
-    pass_on(OWq, sfq, rfq)
-    pass_on(OWo, sfo, rfo)
+    q_sums.pass_on()
+    o_sums.finish()
+    q_sums.finish()
     for q in (p.rc, p.rd):
-        p.arrived(OWq.at[q], rfq.at[q], spare)
-        p.arrived(OWo.at[q], rfo.at[q], spare)
+        p.arrived(OD.at[q], rd.at[q], spare)
     for d in range(3):
-        p.sent(OWq.at[r], sfq.at[d], spare)
-        p.sent(OWo.at[r], sfo.at[d], spare)
-    p.sent(RXo, sfo.at[3], spare)
+        p.sent(OD.at[r], sd.at[d], spare)
+    keep.wait()
 
     @pl.loop(0, 8)
     def _(t):
@@ -1072,10 +1251,7 @@
             p.arrived(OG.at[q, t], ra.at[t, q], spare)
         for d in range(3):
             p.sent(OG.at[r, t], sf.at[t, d], spare)
-        for xx in range(2):
-            p.sent(RCq.at[t, xx], scq.at[t, xx], spare)
-            p.sent(RCo.at[t, xx], sco.at[t, xx], spare)
-        p.sent(RXq.at[t], sxq.at[t], spare)
+        pl.when((t + 7 - s) % 8 >= 3)(lambda: p.sent(RX.at[t], sx.at[t], spare))
 
         @pl.when(t != s)
         def _():
@@ -1083,37 +1259,31 @@
 
     @pl.loop(0, 4)
     def _(i):
-        p.sent(YO.at[i], syo.at[i], spare)
-        p.sent(Yq.at[i], syq.at[i], spare)
-        for xx in range(2):
-            p.sent(Yo.at[i, xx], syw.at[i, xx], spare)
-
         @pl.when(i != z)
         def _():
             p.sent(ZO.at[i], szo.at[i], spare)
-            p.sent(Zq.at[i], szq.at[i], spare)
-            for xx in range(2):
-                p.sent(Zo.at[i, xx], szw.at[i, xx], spare)
+
+    for k in (0, 1, 3):
+        p.sent(YO.at[k], syo.at[p.line(k)], spare)
 
 
 def attend_back(*args):
     return pl.pallas_call(
         attend_back_body,
         out_shape=(
-            shaped(128, 1536), shaped(128, 1536), shaped(4, 8, 48, 2304), shaped(4, 48, 2176), shaped(4, 48, 1536),
+            shaped(128, 1536), shaped(128, 1536), shaped(4, 8, 48, 2304), shaped(4, 1152, 384), shaped(4, 48, 2176),
+            shaped(4, 48, 1536),
         ),
-        in_specs=[VMEM] * 13 + [HBM] * 4,
-        out_specs=(VMEM, VMEM, HBM, VMEM, VMEM),
+        in_specs=[VMEM] * 13 + [HBM] * 5,
+        out_specs=(VMEM, VMEM, HBM, HBM, VMEM, VMEM),
         scratch_shapes=[
-            low(1536, 2176), low(1536, 1536), low(8, 128, 1536), low(4, 128, 1536), low(4, 128, 1536), low(48, 2304),
-            full(128, 1536), low(128, 1536), low(2, 768, 128), low(128, 2048), low(1536, 128), full(8, 16, 128),
-            low(8, 2, 48, 2176), low(8, 48, 2176), low(4, 48, 2176), low(4, 48, 2176),
-            low(8, 2, 48, 1536), low(4, 2, 48, 1536), low(4, 2, 48, 1536), low(48, 1536),
-            DMA((8,)), DMA((8, 4)), DMA((8, 3)), DMA((4,)), DMA((4,)), DMA((4,)), DMA((4,)),
-            DMA((8, 2)), DMA((8, 2)), DMA((8,)), DMA((8,)), DMA((4,)), DMA((4,)), DMA((4,)), DMA((4,)), DMA((3,)), DMA((4,)),
-            DMA((8, 2)), DMA((8, 2)), DMA((4, 2)), DMA((4, 2)), DMA((4, 2)), DMA((4, 2)), DMA((4,)), DMA((5,)), DMA((5,)),
+            low(1536, 2176), low(1536, 1536), low(8, 128, 1536), low(4, 128, 1536), low(5, 128, 1536), low(8, 48, 2304),
+            low(8, 48, 2304), low(1152, 384), full(128, 1536), low(128, 1536), low(2, 768, 128), low(128, 2048),
+            low(1536, 128), full(8, 16, 128), *RowSums.buffers(2176), *RowSums.buffers(1536),
+            DMA((8,)), DMA((8,)), DMA((8,)), DMA((8, 4)), DMA((8, 3)), DMA((3,)), DMA((4,)),
+            DMA((4,)), DMA((4,)), DMA((4,)), DMA((5,)), *RowSums.semaphores(), *RowSums.semaphores(), DMA((6,)),
         ],
-        compiler_params=pltpu.CompilerParams(collective_id=2, has_side_effects=True, vmem_limit_bytes=58 << 20),
+        compiler_params=pltpu.CompilerParams(collective_id=2, has_side_effects=True, vmem_limit_bytes=60 << 20),
         name="attend_back",
     )(*args)
 
@@ -1167,8 +1337,8 @@
         x, cosine, sine, allowed, small, w_qkv, w_out, w_gate, w_up, cot
     )
     ds, parts, gate_up, down = feed_forward(a2, C, G, w_down)
-    out, grad_tokens, gate_up, qkv, o = attend_back(
-        ds, mid, x, cot, gains, cosine, sine, queries, keys, values, probs, att, a1, WQ, WO, parts, gate_up
+    out, grad_tokens, gate_up, down, qkv, o = attend_back(
+        ds, mid, x, cot, gains, cosine, sine, queries, keys, values, probs, att, a1, WQ, WO, parts, gate_up, down
     )
     gate, up, down, qkv_rows, out_rows = widen(gate_up, down, qkv, o)
     small = qkv[0, 0:6, 2048:].astype(F32).reshape(768)

time: 454 us -> 375 us (0.83)
  Pallas kernels: 442 us -> 361 us
    pallas_call x1, Pallas kernels: 164 us -> 94.7 us  [feed_forward(): pl.pallas_call(feed_body, out_shape=(shaped(128, 1536, dtype=F32), shaped...]
    pallas_call x1, Pallas kernels: 132 us -> 118 us  [gather_weights(): pl.pallas_call(gather_body, out_shape=(shaped(1536, 2048), shaped(1536, 1...]
where the time goes in v4:
time: 375 us; the launch traced here: 374 us
  Pallas kernels  361 us (96%)
  local copies, waits for them, and re-layouts  8.98 us (2%)
  other arithmetic  4 us (1%)
    pallas_call x1, Pallas kernels, attend_back(): pl.pallas_call(attend_back_body, out_shape=(shaped(128, 1536), shaped(128...  138 us
    pallas_call x1, Pallas kernels, gather_weights(): pl.pallas_call(gather_body, out_shape=(shaped(1536, 2048), shaped(1536, 1...  118 us
    pallas_call x1, Pallas kernels, feed_forward(): pl.pallas_call(feed_body, out_shape=(shaped(128, 1536, dtype=F32), shaped...  94.7 us
    pallas_call x1, Pallas kernels, widen(): pl.pallas_call(widen_body, grid=(4,), out_shape=(shaped(192, 8960, dtype=...  10.5 us

profile of v4, /device:TPU:0, one launch (start us, length us, event | category | flops | bytes accessed | tf_op | source)
XLA Modules:
  0.0 374.3 jit_solution(7035224672397111156)
XLA Ops:
  0.6 0.9 convert_reduce_fusion
  1.6 0.3 fusion.2
  1.9 0.8 pad_maximum_fusion
  2.7 1.4 fusion.1.allow_ref
  4.1 2.1 concatenate.11
  6.2 0.6 pad.4.small_ref
  6.8 117.9 %gather_and_attend.1 = (bf16[1536,2048]{1,0:T(8,128)(2,1)}, bf16[1536,1536]{1,0:T(8,128)(2,1)}, bf16[1536,2304]{1,0:T(8,128)(2,1)}, bf16[1024,1536]{1,0:T(8,128)...) custom-call(bf16[128,1536]{1,0:T(8,128)(2,1)} %bitcast.11, ...), custom_call_target="tpu_custom_call" | custom-call | tf_op jit(solution)/shard_map/gather_and_attend/pallas_call | solution.py:631
  124.7 94.7 %feed_forward.1 = (f32[128,1536]{1,0:T(8,128)}, bf16[8,128,1536]{2,1,0:T(8,128)(2,1)}, bf16[8,2,48,2304]{3,2,1,0:T(8,128)(2,1)}, bf16[1152,384]{1,0:T(8,128)(2,1)}) custom-call(bf16[128,1536]{1,0:T(8,128)(2,1)} %get-tuple-element.38.n_ref, bf16[1024,1536]{1,0:T(8,128)(2,1)} %get-tuple-element.39.c_hbm, bf16[1536,2304]{1,0:T(8,128)(2,1)} %get-tuple-element.40.g_hbm, ...), custom_call_target="tpu_custom_call" | custom-call | tf_op jit(solution)/shard_map/feed_forward/pallas_call | solution.py:883
  219.4 137.5 %attend_back.1 = (bf16[128,1536]{1,0:T(8,128)(2,1)}, bf16[128,1536]{1,0:T(8,128)(2,1)}, bf16[4,8,48,2304]{3,2,1,0:T(8,128)(2,1)}, bf16[4,1152,384]{2,1,0:T(8,128...) custom-call(f32[128,1536]{1,0:T(8,128)} %get-tuple-element.41.ds_ref, ...), custom_call_target="tpu_custom_call" | custom-call | tf_op jit(solution)/shard_map/attend_back/pallas_call | solution.py:1271
  356.9 0.0 copy-start
  357.0 2.0 copy-done
  358.9 0.0 copy-start.1
  359.0 1.1 copy-done.1
  360.1 0.0 copy-start.2
  360.1 1.1 copy-done.2
  361.2 0.0 copy-start.4
  361.2 0.0 copy-start.3
  361.2 10.5 %widen.1 = (f32[192,8960]{1,0:T(8,128)}, f32[192,8960]{1,0:T(8,128)}, f32[1120,1536]{1,0:T(8,128)}, f32[192,2048]{1,0:T(8,128)}, f32[192,1536]{1,0:T(8,128)}) custom-call(bf16[4,8,48,2304]{3,2,1,0:T(8,128)(2,1)} %get-tuple-element.58.g_ref, bf16[4,1152,384]{2,1,0:T(8,128)(2,1)S(1)} %copy-done, bf16[4,48,2176]{2,1,0:T(8,128)(2,1)S(1)} %copy-done.1, ...), custom_call_target="tpu_custom_call" | custom-call | tf_op jit(solution)/shard_map/widen/pallas_call | solution.py:1301
  371.7 0.6 fusion.3
  372.2 0.6 bitcast_convert_fusion.1
  372.8 0.0 copy-done.4
  372.8 0.7 copy.23
  373.6 0.0 copy-done.3
  373.6 0.7 copy.24
  (5 shorter events, 0.0 us)
Async XLA Ops:
  356.9 2.0 copy-start
  358.9 1.1 copy-start.1
  360.1 1.1 copy-start.2
  361.2 11.6 %copy-start.4 = (bf16[128,1536]{1,0:T(8,128)(2,1)S(1)}, bf16[128,1536]{1,0:T(8,128)(2,1)}, u32[]{:S(2)}) copy-start(bf16[128,1536]{1,0:T(8,128)(2,1)} %get-tuple-element.55) | copy-start | bytes 1179652
  361.2 12.4 %copy-start.3 = (bf16[128,1536]{1,0:T(8,128)(2,1)S(1)}, bf16[128,1536]{1,0:T(8,128)(2,1)}, u32[]{:S(2)}) copy-start(bf16[128,1536]{1,0:T(8,128)(2,1)} %get-tuple-element.56) | copy-start | bytes 1179652

commit v5 on v1

--- a/solution.py
+++ b/solution.py
@@ -3,6 +3,8 @@
 import jax
 import jax.numpy as jnp
 from jax import lax
+from jax.experimental import pallas as pl
+from jax.experimental.pallas import tpu as pltpu
 from jax.sharding import PartitionSpec as P
 
 QUERY_HEADS = 12
@@ -267,6 +269,1128 @@
     )
 
 
+MESH = pl.DeviceIdType.MESH
+BF, F32 = jnp.bfloat16, jnp.float32
+HBM = pl.BlockSpec(memory_space=pl.ANY)
+VMEM = pl.BlockSpec(memory_space=pltpu.VMEM)
+DMA = pltpu.SemaphoreType.DMA
+
+
+def shaped(*shape, dtype=BF):
+    return jax.ShapeDtypeStruct(shape, dtype)
+
+
+def low(*shape):
+    return pltpu.VMEM(shape, BF)
+
+
+def full(*shape):
+    return pltpu.VMEM(shape, F32)
+
+
+def dot(a, b):
+    return lax.dot_general(a, b, (((1,), (0,)), ((), ())), preferred_element_type=F32)
+
+
+def dot_nt(a, b):
+    return lax.dot_general(a, b, (((1,), (1,)), ((), ())), preferred_element_type=F32)
+
+
+def rows_of(start, size, unit=16):
+    return pl.ds(pl.multiple_of(start, unit), size)
+
+
+def quarter(t, q):
+    return rows_of(192 * t + 48 * q, 48)
+
+
+def send(src, dst, send_sem, recv_sem, device):
+    copy = pltpu.make_async_remote_copy(
+        src_ref=src, dst_ref=dst, send_sem=send_sem, recv_sem=recv_sem, device_id=device, device_id_type=MESH
+    )
+    copy.start()
+
+
+class Place:
+    def __init__(self):
+        self.r = r = lax.axis_index("replica")
+        self.s = s = lax.axis_index("shard")
+        self.x, self.c, self.z, self.y = r // 2, r % 2, s // 2, s % 2
+        self.rc, self.rx, self.rd = r + 1 - 2 * self.c, (r + 2) % 4, 3 - r
+        self.core, self.across, self.side = (self.rc, s), (self.rx, s), (r, s + 1 - 2 * self.y)
+
+    def peer(self, t):
+        return (self.r, t)
+
+    def line(self, k):
+        near = self.z + (1 - 2 * (self.z % 2)) * (k % 2)
+        far = k + (self.z // 2) * (3 - 2 * k)
+        return (1 - k // 2) * near + (k // 2) * far
+
+    def onward(self, zz, copy):
+        pl.when((zz <= self.z) & (self.z < 3))(lambda: copy(0, self.peer(self.s + 2)))
+        pl.when((zz >= self.z) & (self.z > 0))(lambda: copy(1, self.peer(self.s - 2)))
+
+    def went_onward(self, zz, wait):
+        pl.when((zz <= self.z) & (self.z < 3))(lambda: wait(0))
+        pl.when((zz >= self.z) & (self.z > 0))(lambda: wait(1))
+
+    def reduce_step(self, zz, add, hand):
+        pl.when((zz >= self.z) & (self.z > 0))(lambda: add(zz))
+        pl.when((zz < self.z) & (self.z < 3))(lambda: add(zz))
+        pl.when((zz == self.z) & (self.z < 3))(lambda: add(4))
+        pl.when(zz > self.z)(lambda: hand(zz, self.peer(self.s + 2)))
+        pl.when(zz < self.z - 1)(lambda: hand(zz, self.peer(self.s - 2)))
+        pl.when(zz == self.z - 1)(lambda: hand(4, self.peer(self.s - 2)))
+
+    def mine(self, zz):
+        return 2 * zz + self.y
+
+    def theirs(self, zz):
+        return 2 * zz + 1 - self.y
+
+    def greet(self, steps):
+        bar = pltpu.get_barrier_semaphore()
+        devices = [self.core, self.across] + [(self.r, (self.s + k) % 8) for k in steps]
+        for device in devices:
+            pl.semaphore_signal(bar, inc=1, device_id=device, device_id_type=MESH)
+        pl.semaphore_wait(bar, len(devices))
+
+    def arrived(self, ref, sem, spare):
+        pltpu.make_async_remote_copy(
+            src_ref=ref, dst_ref=ref, send_sem=spare, recv_sem=sem, device_id=self.core, device_id_type=MESH
+        ).wait_recv()
+
+    def sent(self, ref, sem, spare):
+        pltpu.make_async_remote_copy(
+            src_ref=ref, dst_ref=ref, send_sem=sem, recv_sem=spare, device_id=self.core, device_id_type=MESH
+        ).wait_send()
+
+
+def inverse_norm(v):
+    return lax.rsqrt(jnp.mean(v * v, axis=-1, keepdims=True) + eps_norm)
+
+
+class Gather:
+    def __init__(self, p, spare, view, arrivals, along, aside):
+        self.p, self.spare, self.view = p, spare, view
+        self.arrivals, self.along, self.aside = arrivals, along, aside
+
+    def move(self, src, t, zz):
+        p, dst, sem = self.p, self.view(t), self.arrivals(t)
+        p.onward(zz, lambda d, device: send(src, dst, self.along.at[zz, d], sem, device))
+        send(src, dst, self.aside.at[zz], sem, p.side)
+
+    def start(self, src):
+        self.move(src, self.p.s, self.p.z)
+
+    def wait(self, t):
+        self.p.arrived(self.view(t), self.arrivals(t), self.spare)
+
+    def step(self, k, then=None):
+        zz = self.p.line(k)
+        t = self.p.mine(zz)
+        self.wait(t)
+        self.move(self.view(t), t, zz)
+        if then is not None:
+            then(t)
+
+    def other(self, k, then=None):
+        t = self.p.theirs(self.p.line(k))
+        self.wait(t)
+        if then is not None:
+            then(t)
+
+    def finish(self):
+        block = self.view(self.p.s)
+        for zz in range(4):
+            self.p.sent(block, self.aside.at[zz], self.spare)
+            self.p.went_onward(zz, lambda d: self.p.sent(block, self.along.at[zz, d], self.spare))
+
+
+def gather_body(
+    x_ref, seg_ref, ga_ref, bq_ref, gf_ref, wq_ref, wo_ref, wg_ref, wu_ref, c_ref,
+    WQ_out, WO_out, G, C, cos_ref, sin_ref, gains, queries, keys, values, probs, att, a1, mid, a2,
+    WQ, WO, vg, vu, GS, CS, S, bias,
+    rq, ro, rg, rc, rs, szq, syq, sdq, szo, syo, sdo, sg, sdg, scz, scy, ss, loc,
+):
+    p = Place()
+    r, s, c, z = p.r, p.s, p.c, p.z
+    spare = loc.at[0]
+    own = rows_of(192 * s, 192)
+    own_c = rows_of(128 * s, 128, 128)
+    loads = (
+        pltpu.make_async_copy(wq_ref, WQ.at[own], loc.at[1]),
+        pltpu.make_async_copy(wo_ref, WO.at[own], loc.at[2]),
+        pltpu.make_async_copy(wg_ref, vg, loc.at[3]),
+        pltpu.make_async_copy(wu_ref, vu, loc.at[4]),
+        pltpu.make_async_copy(c_ref, CS, loc.at[5]),
+    )
+    for copy in loads:
+        copy.start()
+    p.greet(range(1, 8))
+    gap = jnp.zeros((1, 64), F32)
+    small = jnp.concatenate(
+        [ga_ref[...].astype(F32), gap, bq_ref[...].astype(F32), gf_ref[...].astype(F32), gap], axis=1
+    )
+    S[s] = jnp.broadcast_to(small, (16, 768)).astype(BF)
+
+    def vq(t, q):
+        return WQ.at[quarter(t, q)]
+
+    def vo(t, h):
+        return WO.at[rows_of(192 * t + 96 * h, 96)]
+
+    def gq(t, q):
+        return G.at[quarter(t, q)]
+
+    def cot_block(t):
+        return C.at[rows_of(128 * t, 128, 128)]
+
+    g_q = Gather(p, spare, lambda t: vq(t, r), lambda t: rq.at[t, r], szq, syq)
+    g_o = Gather(p, spare, lambda t: vo(t, c), lambda t: ro.at[t, c], szo, syo)
+    g_c = Gather(p, spare, cot_block, lambda t: rc.at[t], scz, scy)
+    g_q.start(wq_ref.at[rows_of(48 * r, 48)])
+    for k in range(1, 8):
+        t = (s + k) % 8
+        send(S.at[s], S.at[s], ss.at[t], rs.at[s], p.peer(t))
+
+    def share(view, sems, rsems):
+        def to_replicas(t):
+            v = view(t, r)
+            send(v, v, sems.at[t, 0], rsems.at[t, r], p.across)
+            send(v, v, sems.at[t, 1], rsems.at[t, r], p.core)
+
+        return to_replicas
+
+    def relay(view, sems, rsems, t):
+        v = view(t, p.rx)
+        p.arrived(v, rsems.at[t, p.rx], spare)
+        send(v, v, sems.at[t, 2], rsems.at[t, p.rx], p.core)
+
+    def from_core(view, rsems):
+        @pl.loop(1, 8)
+        def _(k):
+            t = (s + k) % 8
+            p.arrived(view(t, p.rc), rsems.at[t, p.rc], spare)
+            p.arrived(view(t, p.rd), rsems.at[t, p.rd], spare)
+
+    share_q, share_g = share(vq, sdq, rq), share(gq, sdg, rg)
+
+    def share_o(t):
+        send(vo(t, c), vo(t, c), sdo.at[t], ro.at[t, c], p.core)
+
+    for copy in loads:
+        copy.wait()
+    zeros = jnp.zeros((192, 32), BF)
+    for t in range(8):
+        GS[t, :, 0:1120] = vg[:, 1120 * t : 1120 * t + 1120]
+        GS[t, :, 1120:1152] = zeros
+        GS[t, :, 1152:2272] = vu[:, 1120 * t : 1120 * t + 1120]
+        GS[t, :, 2272:2304] = zeros
+    across = jnp.broadcast_to(seg_ref[...].astype(F32), (128, 128))
+    down = across.T
+    row = lax.broadcasted_iota(jnp.int32, (128, 128), 0)
+    column = lax.broadcasted_iota(jnp.int32, (128, 128), 1)
+    earlier = jnp.sum(jnp.where(across < down, 1.0, 0.0), axis=1, keepdims=True)
+    position = row.astype(F32) - earlier
+    half = (column - 64 * (column // 64)).astype(F32)
+    angle = position * jnp.exp(half * (-2.0 * math.log(rope_base) / HEAD_DIMENSION))
+    cos_ref[...] = jnp.cos(angle)
+    sin_ref[...] = jnp.where(column < 64, -1.0, 1.0) * jnp.sin(angle)
+    open_to = (across == down) & (column <= row)
+    g_q.step(1, share_q)
+    g_q.other(0, share_q)
+    g_q.step(2, share_q)
+    g_q.other(1, share_q)
+    g_q.step(3, share_q)
+    g_o.start(wo_ref.at[rows_of(96 * c, 96)])
+    turns = (4, 1, 6, 3, 2, 5, 7)
+
+    def give_g(i):
+        t = (s + turns[i]) % 8
+        send(GS.at[t, rows_of(48 * r, 48)], gq(s, r), sg.at[t], rg.at[s, r], p.peer(t))
+
+    def take_g(i):
+        t = (s + 8 - turns[i]) % 8
+        p.arrived(gq(t, r), rg.at[t, r], spare)
+        share_g(t)
+
+    own_out = (
+        pltpu.make_async_copy(GS.at[s], G.at[own], loc.at[1]),
+        pltpu.make_async_copy(CS, C.at[own_c], loc.at[2]),
+    )
+    for copy in own_out:
+        copy.start()
+    g_q.other(2, share_q)
+    give_g(0)
+    g_q.other(3, share_q)
+    give_g(1)
+
+    @pl.loop(1, 8)
+    def _(k):
+        t = (s + k) % 8
+        p.arrived(S.at[t], rs.at[t], spare)
+
+    for t in range(8):
+        row = S[t, 0:1, :].astype(F32)
+        gains[0:1, 192 * t : 192 * t + 192] = row[:, 0:192]
+        bias[0:1, 256 * t : 256 * t + 256] = row[:, 256:512]
+        gains[1:2, 192 * t : 192 * t + 192] = row[:, 512:704]
+    x = x_ref[...].astype(F32)
+    a1[...] = (x * inverse_norm(x) * gains[0:1, :]).astype(BF)
+
+    def relay_q(t):
+        relay(vq, sdq, rq, t)
+
+    g_o.step(1, share_o)
+    give_g(2)
+    g_o.other(0, share_o)
+    relay_q(p.mine(p.line(1)))
+    relay_q(p.theirs(p.line(0)))
+    g_o.step(2, share_o)
+    give_g(3)
+    g_o.other(1, share_o)
+    relay_q(p.mine(p.line(2)))
+    relay_q(p.theirs(p.line(1)))
+    g_o.step(3, share_o)
+    give_g(4)
+    g_c.start(CS)
+    take_g(0)
+    take_g(1)
+    relay_q(p.mine(p.line(3)))
+    relay_q(p.theirs(p.line(2)))
+    relay_q(p.theirs(p.line(3)))
+    take_g(2)
+    give_g(5)
+    give_g(6)
+    from_core(vq, rq)
+    cosine, sine = cos_ref[...], sin_ref[...]
+    for j in range(4):
+        co = pl.ds(512 * j, 512)
+        joined = dot(a1[...], WQ[:, co]) + bias[0:1, co]
+        for i in range(4):
+            h = 4 * j + i
+            u = joined[:, 128 * i : 128 * i + 128]
+            if h < 14:
+                u = u * cosine + pltpu.roll(u, 64, 1) * sine
+            if h < 12:
+                queries[h // 6, pl.ds(128 * (h % 6), 128), :] = (u * HEAD_DIMENSION**-0.5).astype(BF)
+            elif h < 14:
+                keys[h - 12] = u.astype(BF)
+            else:
+                values[h - 14] = u.astype(BF)
+    save = (pltpu.make_async_copy(WQ, WQ_out, loc.at[3]), pltpu.make_async_copy(WO, WO_out, loc.at[4]))
+    save[0].start()
+    for g in range(2):
+        scores = dot_nt(queries[g], keys[g]).reshape(6, 128, 128)
+        scores = jnp.where(open_to[None], scores, -1e30)
+        ex = jnp.exp(scores - jnp.max(scores, axis=-1, keepdims=True))
+        soft = (ex / jnp.sum(ex, axis=-1, keepdims=True)).reshape(768, 128)
+        probs[g] = soft
+        out = dot(soft.astype(BF), values[g]).astype(BF)
+        for i in range(6):
+            att[:, pl.ds(128 * (6 * g + i), 128)] = out[128 * i : 128 * i + 128]
+
+    for i in (3, 4):
+        take_g(i)
+    g_o.other(2, share_o)
+    g_o.other(3, share_o)
+
+    @pl.loop(1, 8)
+    def _(k):
+        t = (s + k) % 8
+        p.arrived(vo(t, 1 - c), ro.at[t, 1 - c], spare)
+
+    save[1].start()
+    for j in range(3):
+        co = pl.ds(512 * j, 512)
+        mid[:, co] = x[:, 512 * j : 512 * j + 512] + dot(att[...], WO[:, co])
+    hidden = mid[...]
+    a2[...] = (hidden * inverse_norm(hidden) * gains[1:2, :]).astype(BF)
+    g_c.step(1)
+    take_g(5)
+    g_c.step(2)
+    take_g(6)
+    g_c.step(3)
+
+    for k in turns:
+        relay(gq, sdg, rg, (s + 8 - k) % 8)
+
+    from_core(gq, rg)
+
+    @pl.loop(0, 4)
+    def _(k):
+        g_c.other(k)
+
+    g_q.finish()
+    g_o.finish()
+    g_c.finish()
+
+    @pl.loop(1, 8)
+    def _(k):
+        t = (s + k) % 8
+        p.sent(S.at[t], ss.at[t], spare)
+        p.sent(gq(t, r), sg.at[t], spare)
+        p.sent(vo(t, c), sdo.at[t], spare)
+        for d in range(3):
+            p.sent(vq(t, r), sdq.at[t, d], spare)
+            p.sent(gq(t, r), sdg.at[t, d], spare)
+
+    for copy in own_out + save:
+        copy.wait()
+
+
+def gather_weights(x, segments, gain_attn, b_qkv, gain_ffn, w_qkv, w_out, w_gate, w_up, cot):
+    return pl.pallas_call(
+        gather_body,
+        out_shape=(
+            shaped(1536, 2048), shaped(1536, 1536), shaped(1536, 2304), shaped(1024, 1536), shaped(128, 128, dtype=F32),
+            shaped(128, 128, dtype=F32), shaped(8, 1536, dtype=F32), shaped(2, 768, 128), shaped(2, 128, 128), shaped(2, 128, 128), shaped(2, 768, 128, dtype=F32),
+            shaped(128, 1536), shaped(128, 1536), shaped(128, 1536, dtype=F32), shaped(128, 1536),
+        ),
+        in_specs=[VMEM] * 5 + [HBM] * 5,
+        out_specs=(HBM,) * 4 + (VMEM,) * 11,
+        scratch_shapes=[
+            low(1536, 2048), low(1536, 1536), low(192, 8960), low(192, 8960), low(8, 192, 2304), low(128, 1536),
+            low(8, 16, 768), full(8, 2048),
+            DMA((8, 4)), DMA((8, 2)), DMA((8, 4)), DMA((8,)), DMA((8,)),
+            DMA((4, 2)), DMA((4,)), DMA((8, 3)), DMA((4, 2)), DMA((4,)), DMA((8,)),
+            DMA((8,)), DMA((8, 3)), DMA((4, 2)), DMA((4,)), DMA((8,)), DMA((6,)),
+        ],
+        compiler_params=pltpu.CompilerParams(collective_id=0, has_side_effects=True, vmem_limit_bytes=56 << 20),
+        name="gather_and_attend",
+    )(x, segments, gain_attn, b_qkv, gain_ffn, w_qkv, w_out, w_gate, w_up, cot)
+
+
+class RowSums:
+    def __init__(self, p, spare, total, chip, side, far, across, out, sems, width):
+        self.p, self.spare, self.total, self.chip, self.side = p, spare, total, chip, side
+        self.far, self.across, self.out, self.sems = far, across, out, sems
+        self.width = width
+
+    def part(self, t, q):
+        return self.total.at[quarter(t, q), 0 : self.width]
+
+    def slot(self, t, xx):
+        return self.chip.at[t, xx, :, 0 : self.width]
+
+    def own(self, k):
+        p = self.p
+        return 2 * p.line(3 - k % 4) + (1 - p.y + (k // 4) * (2 * p.y - 1))
+
+    def to_core(self, t):
+        p = self.p
+        for xx in range(2):
+            send(
+                self.part(t, 2 * xx + 1 - p.c), self.slot(t, xx),
+                self.sems[0].at[t, xx], self.sems[1].at[t, xx], p.core,
+            )
+
+    def add(self, t, q, ref, sem):
+        self.p.arrived(ref, sem, self.spare)
+        total = self.part(t, q)
+        total[...] = (total[...].astype(F32) + ref[...].astype(F32)).astype(BF)
+
+    def on_chip(self, k):
+        p, t = self.p, self.own(k)
+        for xx in range(2):
+            self.add(t, 2 * xx + p.c, self.slot(t, xx), self.sems[1].at[t, xx])
+
+    def aside(self, k):
+        p, t = self.p, self.own(k)
+        for xx in range(2):
+            at = t // 2, xx
+            send(self.part(t, 2 * xx + p.c), self.side.at[at], self.sems[2].at[at], self.sems[3].at[at], p.side)
+
+    def on_line(self, k):
+        p = self.p
+        zz = p.line(3 - k)
+        t = p.mine(zz)
+        for xx in range(2):
+            q = 2 * xx + p.c
+            self.add(t, q, self.side.at[zz, xx], self.sems[3].at[zz, xx])
+            p.reduce_step(
+                zz,
+                lambda slot: self.add(t, q, self.far.at[slot, xx], self.sems[5].at[slot, xx]),
+                lambda slot, device: send(
+                    self.part(t, q), self.far.at[slot, xx], self.sems[4].at[zz, xx], self.sems[5].at[slot, xx], device
+                ),
+            )
+
+    def at_owner(self):
+        p = self.p
+        for xx in range(2):
+            send(self.part(p.s, 2 * xx + p.c), self.across.at[xx], self.sems[6].at[xx], self.sems[7].at[xx], p.across)
+
+    def spread(self):
+        p = self.p
+        for xx in range(2):
+            q = 2 * xx + p.c
+            p.sent(self.across.at[xx], self.sems[6].at[xx], self.spare)
+            self.add(p.s, q, self.across.at[xx], self.sems[7].at[xx])
+            total = self.part(p.s, q)
+            pltpu.make_async_copy(total, self.out.at[q], self.sems[6].at[4 + xx]).start()
+            send(total, self.out.at[q], self.sems[6].at[2 + xx], self.sems[7].at[2 + xx], p.core)
+
+    def finish(self):
+        p = self.p
+        for xx in range(2):
+            q = 2 * xx + 1 - p.c
+            p.arrived(self.out.at[q], self.sems[7].at[2 + xx], self.spare)
+            p.sent(self.out.at[q], self.sems[6].at[2 + xx], self.spare)
+            pltpu.make_async_copy(self.part(p.s, 0), self.out.at[q], self.sems[6].at[4 + xx]).wait()
+
+        @pl.loop(0, 8)
+        def _(t):
+            for xx in range(2):
+                p.sent(self.slot(t, xx), self.sems[0].at[t, xx], self.spare)
+
+        @pl.loop(0, 4)
+        def _(i):
+            for xx in range(2):
+                p.sent(self.side.at[i, xx], self.sems[2].at[i, xx], self.spare)
+
+                @pl.when(i != p.z)
+                def _():
+                    p.sent(self.far.at[i, xx], self.sems[4].at[i, xx], self.spare)
+
+    @staticmethod
+    def buffers(width):
+        return [low(8, 2, 48, width), low(4, 2, 48, width), low(5, 2, 48, width), low(2, 48, width)]
+
+    @staticmethod
+    def semaphores():
+        return [DMA((8, 2)), DMA((8, 2)), DMA((4, 2)), DMA((4, 2)), DMA((4, 2)), DMA((5, 2)), DMA((6,)), DMA((4,))]
+
+
+def layer_back_body(
+    n_ref, c_hbm, g_hbm, d_hbm, wq_hbm, wo_hbm, att_hbm, a1_hbm, x_hbm, cot_hbm,
+    mid_ref, gains, cos_ref, sin_ref, queries, keys, values, probs,
+    out_ref, gtok_ref, OG, OD, OWq, OWo,
+    NC, H, vG, vD, MX, PD, PO, YD, ZD, YO, ZO, RCd, RXd, RC, RX, dmid, dA, dj, AT, SM,
+    Yq, Zq, RXq, RCo, Yo, Zo, RXo,
+    free, rn, syn, szn, ryd, rzd, syd, szd, syo, ryo, szo, rzo,
+    scd, rcd, sxd, rxd, sfd, rfd, scg, rcg, sx, rx, sa, ra, sf, *sems,
+):
+    p = Place()
+    r, s, c, y, z = p.r, p.s, p.c, p.y, p.z
+    loc = sems[-1]
+    spare = loc.at[0]
+    q_sums = RowSums(p, spare, H, RC, Yq, Zq, RXq, OWq, sems[0:8], 2176)
+    o_sums = RowSums(p, spare, NC, RCo, Yo, Zo, RXo, OWo, sems[8:16], 1536)
+
+    def block(t):
+        return NC.at[rows_of(128 * t, 128, 128)]
+
+    def cot_rows(start, size):
+        return rows_of(1024 + start, size, 128)
+
+    loads = (
+        pltpu.make_async_copy(n_ref, block(s), loc.at[1]),
+        pltpu.make_async_copy(c_hbm, NC.at[1024:2048], loc.at[2]),
+        pltpu.make_async_copy(g_hbm, vG, loc.at[3]),
+        pltpu.make_async_copy(d_hbm, vD.at[0:1120], loc.at[4]),
+    )
+    for copy in loads:
+        copy.start()
+    p.greet(range(1, 8))
+    g_n = Gather(p, spare, block, lambda t: rn.at[t], szn, syn)
+    g_n.start(n_ref)
+    vD[1120:1152, :] = jnp.zeros((32, 1536), BF)
+    for copy in loads:
+        copy.wait()
+
+    def side(P, Y, ssem, rsem, k):
+        zz = p.line(k)
+        send(P.at[p.theirs(zz)], Y.at[zz], ssem.at[zz], rsem.at[zz], p.side)
+
+    def side_d(k):
+        side(PD, YD, syd, ryd, k)
+
+    def line_step(P, Y, Z, ry, sz, rz, k):
+        zz = p.line(k)
+        t = p.mine(zz)
+
+        def add(ref, sem):
+            p.arrived(ref, sem, spare)
+            P[t] = (P[t].astype(F32) + ref[...].astype(F32)).astype(BF)
+
+        add(Y.at[zz], ry.at[zz])
+        p.reduce_step(
+            zz,
+            lambda slot: add(Z.at[slot], rz.at[slot]),
+            lambda slot, device: send(P.at[t], Z.at[slot], sz.at[zz], rz.at[slot], device),
+        )
+
+    def step_d(k):
+        line_step(PD, YD, ZD, ryd, szd, rzd, k)
+
+    def side_o(k):
+        side(PO, YO, syo, ryo, k)
+
+    def step_o(k):
+        line_step(PO, YO, ZO, ryo, szo, rzo, k)
+
+    at_end = (z == 0) | (z == 3)
+    in_middle = (z == 1) | (z == 2)
+    g_n.step(1)
+
+    @pl.loop(0, 4)
+    def _(k):
+        zz = p.line(k)
+        pl.when(at_end & (k > 0) & (k < 3))(lambda: g_n.step(k + 1))
+        pl.when(in_middle & (k < 2))(lambda: g_n.step(k + 2))
+        g_n.other(k)
+        rows = rows_of(256 * zz, 256, 256)
+        X = NC[rows]
+        cot = NC[cot_rows(256 * zz, 256)]
+        for j in range(3):
+            ga, ua = pl.ds(384 * j, 384), pl.ds(1152 + 384 * j, 384)
+            gate = dot(X, vG[:, ga])
+            up = dot(X, vG[:, ua])
+            d_mixed = dot_nt(cot, vD[ga])
+            sg = jax.nn.sigmoid(gate)
+            active = gate * sg
+            d_active = d_mixed * up
+            MX[rows, ga] = (active * up).astype(BF)
+            H[rows, ga] = (d_active * sg + d_active * active * (1.0 - sg)).astype(BF)
+            H[rows, ua] = (d_mixed * active).astype(BF)
+        for j in range(3):
+            co = pl.ds(512 * j, 512)
+            part = dot_nt(H[rows], vG[co]).astype(BF)
+            PD[2 * zz, :, co] = part[:128]
+            PD[2 * zz + 1, :, co] = part[128:]
+        pl.when(k == 2)(lambda: side_d(1))
+        pl.when(k == 3)(lambda: side_d(3))
+        for j in range(3):
+            co = pl.ds(512 * j, 512)
+            part = dot(MX[rows], vD[:, co]).astype(BF)
+            PO[2 * zz, :, co] = part[:128]
+            PO[2 * zz + 1, :, co] = part[128:]
+
+    side_d(2)
+    side_d(0)
+
+    def owner(k):
+        return 2 * ((z + 1 + k // 2) % 4) + (k % 2) * (2 * y - 1) + 1 - y
+
+    def pair_chip(k):
+        t = owner(k)
+        for xx in range(2):
+            p.arrived(RC.at[t, xx], rcg.at[t, xx], spare)
+            q = quarter(t, 2 * xx + c)
+            vG[q] = (vG[q].astype(F32) + RC[t, xx].astype(F32)).astype(BF)
+        send(vG.at[quarter(t, p.rx)], RX.at[t], sx.at[t], rx.at[t], p.across)
+
+    @pl.loop(0, 5)
+    def _(j):
+        @pl.when(j < 4)
+        def _():
+            pair = (z + 1 + j) % 4
+            rows = rows_of(384 * pair, 384, 128)
+            X = NC[0:1024, rows].T
+            for i in range(3):
+                co = pl.ds(768 * i, 768)
+                vG[rows, co] = dot(X, H[0:1024, co]).astype(BF)
+            for i in range(2):
+                t = owner(2 * j + i)
+                for xx in range(2):
+                    send(vG.at[quarter(t, 2 * xx + 1 - c)], RC.at[t, xx], scg.at[t, xx], rcg.at[t, xx], p.core)
+
+        @pl.when(j > 0)
+        def _():
+            pair_chip(2 * j - 2)
+            pair_chip(2 * j - 1)
+
+    pl.semaphore_signal(free, inc=1, device_id=p.core, device_id_type=MESH)
+
+    def chunk(i):
+        return rows_of(384 * i, 384, 128)
+
+    def cols(q):
+        return rows_of(384 * q, 384, 128)
+
+    held = (
+        pltpu.make_async_copy(wo_hbm, NC.at[0:1536], loc.at[1]),
+        pltpu.make_async_copy(wq_hbm, H.at[:, 0:2048], loc.at[2]),
+        pltpu.make_async_copy(att_hbm, NC.at[1536:1664], loc.at[3]),
+        pltpu.make_async_copy(a1_hbm, NC.at[1664:1792], loc.at[4]),
+        pltpu.make_async_copy(x_hbm, NC.at[1792:1920], loc.at[5]),
+        pltpu.make_async_copy(cot_hbm, NC.at[1920:2048], loc.at[6]),
+    )
+
+    def down_terms():
+        @pl.loop(0, 3)
+        def _(i):
+            X = MX[:, chunk(i)].T
+            for j in range(3):
+                co = pl.ds(512 * j, 512)
+                vD[chunk(i), co] = dot(X, NC[1024:2048, co]).astype(BF)
+            for xx in range(2):
+                q = 2 * xx + 1 - c
+                send(vD.at[chunk(i), cols(q)], RCd.at[xx, chunk(i)], scd.at[i, xx], rcd.at[i, xx], p.core)
+
+        g_n.finish()
+        for copy in held:
+            copy.start()
+
+        @pl.loop(0, 3)
+        def _(i):
+            for xx in range(2):
+                p.arrived(RCd.at[xx, chunk(i)], rcd.at[i, xx], spare)
+                q = cols(2 * xx + c)
+                vD[chunk(i), q] = (vD[chunk(i), q].astype(F32) + RCd[xx, chunk(i)].astype(F32)).astype(BF)
+
+    def pair_whole(k):
+        t = owner(k)
+        q = quarter(t, r)
+        p.arrived(RX.at[t], rx.at[t], spare)
+        vG[q] = (vG[q].astype(F32) + RX[t].astype(F32)).astype(BF)
+
+        if k < 7:
+            send(vG.at[q], OG.at[r, s], sa.at[t], ra.at[s, r], p.peer(t))
+        else:
+            pltpu.make_async_copy(vG.at[q], OG.at[r, s], loc.at[7]).start()
+
+    def share(t):
+        v = OG.at[r, t]
+        send(v, v, sf.at[t, 0], ra.at[t, r], p.across)
+        send(v, v, sf.at[t, 1], ra.at[t, r], p.core)
+
+    def source(k):
+        return 2 * ((z + 3 - k // 2) % 4) + (1 - y if k % 2 == 0 else y)
+
+    def take(k):
+        t = source(k)
+        if k < 7:
+            p.arrived(OG.at[r, t], ra.at[t, r], spare)
+        else:
+            pltpu.make_async_copy(vG.at[quarter(s, r)], OG.at[r, s], loc.at[7]).wait()
+        share(t)
+
+    def relay(k):
+        t = source(k)
+        v = OG.at[p.rx, t]
+        p.arrived(v, ra.at[t, p.rx], spare)
+        send(v, v, sf.at[t, 2], ra.at[t, p.rx], p.core)
+
+    def down_across(i):
+        send(vD.at[chunk(i), cols(p.rx)], RXd.at[chunk(i)], sxd.at[i], rxd.at[i], p.across)
+
+    def down_whole(i):
+        p.arrived(RXd.at[chunk(i)], rxd.at[i], spare)
+        q = cols(r)
+        vD[chunk(i), q] = (vD[chunk(i), q].astype(F32) + RXd[chunk(i)].astype(F32)).astype(BF)
+        src, dst = vD.at[chunk(i), q], OD.at[r, chunk(i)]
+        pltpu.make_async_copy(src, dst, sfd.at[i, 3]).start()
+        send(src, dst, sfd.at[i, 0], rfd.at[i, r], p.across)
+        send(src, dst, sfd.at[i, 1], rfd.at[i, r], p.core)
+
+    def down_relay(i):
+        v = OD.at[p.rx, chunk(i)]
+        p.arrived(v, rfd.at[i, p.rx], spare)
+        send(v, v, sfd.at[i, 2], rfd.at[i, p.rx], p.core)
+
+    def back(w):
+        return w * cos_ref[...] - pltpu.roll(w, 64, 1) * sin_ref[...]
+
+    kept = {}
+
+    def attention_out():
+        for copy in held:
+            copy.wait()
+        dn, hidden = PD[s].astype(F32), mid_ref[...]
+        rstd = inverse_norm(hidden)
+        unit = hidden * rstd
+        kept["ffn"] = jnp.sum(dn * unit, axis=0, keepdims=True)
+        e = dn * gains[1:2, :]
+        dm = NC[1920:2048].astype(F32) + rstd * (e - unit * jnp.mean(e * unit, axis=-1, keepdims=True))
+        dmid[...] = dm
+        NC[1920:2048] = dm.astype(BF)
+        AT[...] = NC[1536:1664].T
+        for j in range(3):
+            part = dot_nt(NC[1920:2048], NC[pl.ds(512 * j, 512)]).astype(BF)
+            for i in range(4):
+                h = 4 * j + i
+                dA[h // 6, pl.ds(128 * (h % 6), 128), :] = part[:, 128 * i : 128 * i + 128]
+        for j in range(3):
+            co = pl.ds(512 * j, 512)
+            NC[0:1536, co] = dot(AT[...], NC[1920:2048, co]).astype(BF)
+
+        @pl.loop(0, 8)
+        def _(k):
+            o_sums.to_core(o_sums.own(k))
+
+    def heads(g):
+        grad, soft = dA[g], probs[g]
+        d_probs = dot_nt(grad, values[g])
+        d_scores = (soft * (d_probs - jnp.sum(soft * d_probs, axis=-1, keepdims=True))).astype(BF)
+        d_values = dot(soft.astype(BF).T, grad)
+        d_queries = dot(d_scores, keys[g]) * HEAD_DIMENSION**-0.5
+        d_keys = dot(d_scores.T, queries[g])
+        for i in range(6):
+            dj[:, pl.ds(128 * (6 * g + i), 128)] = back(d_queries[128 * i : 128 * i + 128]).astype(BF)
+        dj[:, pl.ds(128 * (12 + g), 128)] = back(d_keys).astype(BF)
+        dj[:, pl.ds(128 * (14 + g), 128)] = d_values.astype(BF)
+
+    def attention_in():
+        heads(1)
+        joined_grad = dj[...]
+        bias_grad = jnp.sum(joined_grad.astype(F32), axis=0, keepdims=True)
+        x = NC[1792:1920].astype(F32)
+        rstd = inverse_norm(x)
+        unit = x * rstd
+        dn1 = jnp.concatenate(
+            [dot_nt(joined_grad, H[pl.ds(512 * j, 512), 0:2048]) for j in range(3)], axis=1
+        )
+        gain_attn_grad = jnp.sum(dn1 * unit, axis=0, keepdims=True)
+        e = dn1 * gains[0:1, :]
+        NC[1792:1920] = (
+            dmid[...] + rstd * (e - unit * jnp.mean(e * unit, axis=-1, keepdims=True))
+        ).astype(BF)
+        pltpu.make_async_copy(NC.at[1792:1920], gtok_ref, loc.at[5]).start()
+        SM[...] = jnp.zeros_like(SM)
+        ffn = kept["ffn"]
+        for t in range(8):
+            SM[t, 0:1, :] = gain_attn_grad[:, 192 * t : 192 * t + 128]
+            SM[t, 1:2, 0:64] = gain_attn_grad[:, 192 * t + 128 : 192 * t + 192]
+            SM[t, 2:3, :] = bias_grad[:, 256 * t : 256 * t + 128]
+            SM[t, 3:4, :] = bias_grad[:, 256 * t + 128 : 256 * t + 256]
+            SM[t, 4:5, :] = ffn[:, 192 * t : 192 * t + 128]
+            SM[t, 5:6, 0:64] = ffn[:, 192 * t + 128 : 192 * t + 192]
+        AT[...] = NC[1664:1792].T
+
+    def joined_terms():
+        pl.semaphore_wait(free, 1)
+
+        @pl.loop(0, 8)
+        def _(k):
+            t = q_sums.own(k)
+            rows = rows_of(192 * t, 192)
+            for j in range(2):
+                co = pl.ds(1024 * j, 1024)
+                H[rows, co] = dot(AT[rows], dj[:, co]).astype(BF)
+            H[rows, 2048:2176] = jnp.zeros((192, 128), BF)
+            H[rows_of(192 * t, 16), 2048:2176] = SM[t].astype(BF)
+            q_sums.to_core(t)
+
+    def on_chip(sums):
+        @pl.loop(0, 8)
+        def _(k):
+            sums.on_chip(k)
+
+    def finish_out():
+        PO[s] = (PO[s].astype(F32) + mid_ref[...]).astype(BF)
+        pltpu.make_async_copy(PO.at[s], out_ref, loc.at[6]).start()
+
+    def first_heads():
+        heads(0)
+
+    def o_on_chip():
+        on_chip(o_sums)
+
+    def q_on_chip():
+        on_chip(q_sums)
+
+
+    @pl.when(in_middle)
+    def _():
+        side_o(3)
+        side_o(1)
+
+    step_d(3)
+    down_terms()
+
+    @pl.when(at_end)
+    def _():
+        side_o(3)
+        side_o(1)
+        step_d(2)
+        step_d(1)
+        pair_whole(6)
+        step_o(3)
+        pair_whole(7)
+        pair_whole(5)
+
+
+    @pl.when(in_middle)
+    def _():
+        step_d(2)
+        step_d(1)
+        pair_whole(6)
+        pair_whole(7)
+        pair_whole(5)
+        down_across(0)
+
+    pair_whole(1)
+    down_across(1)
+    step_d(0)
+    attention_out()
+    down_across(2)
+
+    @pl.when(at_end)
+    def _():
+        pair_whole(4)
+        pair_whole(3)
+
+    o_on_chip()
+
+    @pl.when(at_end)
+    def _():
+        down_across(0)
+        o_sums.aside(1)
+        take(1)
+        o_sums.aside(0)
+        o_sums.aside(2)
+
+
+    @pl.when(in_middle)
+    def _():
+        o_sums.aside(1)
+        take(1)
+        o_sums.aside(0)
+        o_sums.aside(2)
+        pair_whole(0)
+        take(7)
+        take(6)
+
+    first_heads()
+    take(5)
+    pair_whole(2)
+
+    @pl.when(at_end)
+    def _():
+        pair_whole(0)
+        take(6)
+
+
+    @pl.when(in_middle)
+    def _():
+        down_whole(1)
+
+    attention_in()
+    joined_terms()
+
+    @pl.when(at_end)
+    def _():
+        o_sums.aside(3)
+
+
+    @pl.when(in_middle)
+    def _():
+        pair_whole(4)
+        o_sums.aside(3)
+        pair_whole(3)
+
+    down_whole(0)
+    relay(5)
+    q_on_chip()
+
+    @pl.when(at_end)
+    def _():
+        q_sums.aside(0)
+        o_sums.on_line(0)
+        take(4)
+        q_sums.aside(1)
+        o_sums.on_line(1)
+        take(0)
+        take(7)
+        o_sums.on_line(2)
+        q_sums.on_line(0)
+        q_sums.aside(2)
+        side_o(2)
+        down_whole(1)
+        take(3)
+        down_whole(2)
+        q_sums.aside(3)
+        relay(4)
+        take(2)
+        q_sums.on_line(1)
+        relay(6)
+        down_relay(0)
+        q_sums.on_line(2)
+        o_sums.on_line(3)
+        relay(0)
+        side_o(0)
+        relay(2)
+        down_relay(1)
+        relay(3)
+        o_sums.at_owner()
+        step_o(2)
+        relay(7)
+        relay(1)
+        step_o(1)
+        q_sums.on_line(3)
+        q_sums.at_owner()
+        step_o(0)
+        finish_out()
+        down_relay(2)
+        o_sums.spread()
+        q_sums.spread()
+
+
+    @pl.when(in_middle)
+    def _():
+        take(4)
+        q_sums.aside(1)
+        step_o(3)
+        o_sums.on_line(0)
+        take(0)
+        o_sums.on_line(1)
+        q_sums.aside(0)
+        o_sums.on_line(2)
+        q_sums.aside(2)
+        down_whole(2)
+        q_sums.aside(3)
+        q_sums.on_line(0)
+        take(2)
+        q_sums.on_line(1)
+        relay(6)
+        relay(2)
+        side_o(2)
+        down_relay(0)
+        o_sums.on_line(3)
+        down_relay(1)
+        o_sums.at_owner()
+        take(3)
+        relay(4)
+        q_sums.on_line(2)
+        down_relay(2)
+        o_sums.spread()
+        q_sums.on_line(3)
+        relay(1)
+        step_o(1)
+        relay(0)
+        relay(3)
+        side_o(0)
+        q_sums.at_owner()
+        step_o(2)
+        q_sums.spread()
+        relay(7)
+        step_o(0)
+        finish_out()
+
+
+    o_sums.finish()
+    q_sums.finish()
+    pltpu.make_async_copy(NC.at[1792:1920], gtok_ref, loc.at[5]).wait()
+    pltpu.make_async_copy(PO.at[s], out_ref, loc.at[6]).wait()
+
+    @pl.loop(0, 3)
+    def _(i):
+        for q in (p.rc, p.rd):
+            p.arrived(OD.at[q, chunk(i)], rfd.at[i, q], spare)
+        for d in range(3):
+            p.sent(OD.at[r, chunk(i)], sfd.at[i, d], spare)
+        pltpu.make_async_copy(OD.at[r, chunk(i)], OD.at[r, chunk(i)], sfd.at[i, 3]).wait()
+        for xx in range(2):
+            p.sent(RCd.at[xx, chunk(i)], scd.at[i, xx], spare)
+        p.sent(RXd.at[chunk(i)], sxd.at[i], spare)
+
+    @pl.loop(0, 8)
+    def _(t):
+        for q in (p.rc, p.rd):
+            p.arrived(OG.at[q, t], ra.at[t, q], spare)
+        for d in range(3):
+            p.sent(OG.at[r, t], sf.at[t, d], spare)
+        for xx in range(2):
+            p.sent(RC.at[t, xx], scg.at[t, xx], spare)
+        p.sent(RX.at[t], sx.at[t], spare)
+
+        @pl.when(t != s)
+        def _():
+            p.sent(OG.at[r, s], sa.at[t], spare)
+
+    @pl.loop(0, 4)
+    def _(i):
+        p.sent(YD.at[i], syd.at[i], spare)
+        p.sent(YO.at[i], syo.at[i], spare)
+
+        @pl.when(i != z)
+        def _():
+            p.sent(ZD.at[i], szd.at[i], spare)
+            p.sent(ZO.at[i], szo.at[i], spare)
+
+
+def layer_back(*args):
+    return pl.pallas_call(
+        layer_back_body,
+        out_shape=(
+            shaped(128, 1536), shaped(128, 1536), shaped(4, 8, 48, 2304), shaped(4, 1152, 384), shaped(4, 48, 2176),
+            shaped(4, 48, 1536),
+        ),
+        in_specs=[HBM] * 10 + [VMEM] * 8,
+        out_specs=(HBM,) * 6,
+        scratch_shapes=[
+            low(2048, 1536), low(1536, 2304), low(1536, 2304), low(1152, 1536), low(1024, 1152),
+            low(8, 128, 1536), low(8, 128, 1536), low(4, 128, 1536), low(5, 128, 1536), low(4, 128, 1536), low(5, 128, 1536),
+            low(2, 1152, 384), low(1152, 384), low(8, 2, 48, 2304), low(8, 48, 2304),
+            full(128, 1536), low(2, 768, 128), low(128, 2048), low(1536, 128), full(8, 16, 128),
+            *RowSums.buffers(2176)[1:], *RowSums.buffers(1536),
+            pltpu.SemaphoreType.REGULAR, DMA((8,)), DMA((4,)), DMA((4, 2)),
+            DMA((4,)), DMA((5,)), DMA((4,)), DMA((4,)), DMA((4,)), DMA((4,)), DMA((4,)), DMA((5,)),
+            DMA((3, 2)), DMA((3, 2)), DMA((3,)), DMA((3,)), DMA((3, 4)), DMA((3, 4)),
+            DMA((8, 2)), DMA((8, 2)), DMA((8,)), DMA((8,)), DMA((8,)), DMA((8, 4)), DMA((8, 3)),
+            *RowSums.semaphores(), *RowSums.semaphores(), DMA((8,)),
+        ],
+        compiler_params=pltpu.CompilerParams(collective_id=1, has_side_effects=True, vmem_limit_bytes=64 << 20),
+        name="layer_back",
+    )(*args)
+
+
+def widen_body(g_ref, d_ref, q_ref, o_ref, gate, up, down, qkv, out):
+    for t in range(8):
+        gate[:, 1120 * t : 1120 * t + 1120] = g_ref[0, t, :, 0:1120].astype(F32)
+        up[:, 1120 * t : 1120 * t + 1120] = g_ref[0, t, :, 1152:2272].astype(F32)
+    down[...] = d_ref[0, 0:1120, :].astype(F32)
+    qkv[...] = q_ref[0, :, 0:2048].astype(F32)
+    out[...] = o_ref[0].astype(F32)
+
+
+def widen(g, d, q, o):
+    return pl.pallas_call(
+        widen_body,
+        grid=(4,),
+        out_shape=(
+            shaped(192, 8960, dtype=F32), shaped(192, 8960, dtype=F32), shaped(1120, 1536, dtype=F32),
+            shaped(192, 2048, dtype=F32), shaped(192, 1536, dtype=F32),
+        ),
+        in_specs=[
+            pl.BlockSpec((1, 8, 48, 2304), lambda i: (i, 0, 0, 0)),
+            pl.BlockSpec((1, 1152, 384), lambda i: (i, 0, 0)),
+            pl.BlockSpec((1, 48, 2176), lambda i: (i, 0, 0)),
+            pl.BlockSpec((1, 48, 1536), lambda i: (i, 0, 0)),
+        ],
+        out_specs=(
+            pl.BlockSpec((48, 8960), lambda i: (i, 0)),
+            pl.BlockSpec((48, 8960), lambda i: (i, 0)),
+            pl.BlockSpec((1120, 384), lambda i: (0, i)),
+            pl.BlockSpec((48, 2048), lambda i: (i, 0)),
+            pl.BlockSpec((48, 1536), lambda i: (i, 0)),
+        ),
+        compiler_params=pltpu.CompilerParams(vmem_limit_bytes=62 << 20),
+        name="widen",
+    )(g, d, q, o)
+
+
+def shards_eight(
+    tokens, segments, gain_attn, w_qkv, b_qkv, w_out, gain_ffn, w_gate, w_up, w_down, cotangent
+):
+    x, cot = tokens[0], cotangent[0]
+    WQ, WO, G, C, cosine, sine, gains, queries, keys, values, probs, att, a1, mid, a2 = gather_weights(
+        x, segments, gain_attn[None], b_qkv[None], gain_ffn[None], w_qkv, w_out, w_gate, w_up, cot
+    )
+    out, grad_tokens, gate_up, down, qkv, o = layer_back(
+        a2, C, G, w_down, WQ, WO, att, a1, x, cot, mid, gains, cosine, sine, queries, keys, values, probs
+    )
+    gate, up, down, qkv_rows, out_rows = widen(gate_up, down, qkv, o)
+    small = qkv[0, 0:6, 2048:].astype(F32).reshape(768)
+    return (
+        out[None], grad_tokens[None], small[0:192], qkv_rows, small[256:512], out_rows, small[512:704], gate, up, down,
+    )
+
+
 def solution(mesh):
     placed = (
         P(("replica", "shard"), None, None),
@@ -282,7 +1406,7 @@
         P(("replica", "shard"), None, None),
     )
     return jax.shard_map(
-        shards,
+        shards_eight if (mesh.shape["replica"], mesh.shape["shard"]) == (4, 8) else shards,
         mesh=mesh,
         in_specs=placed,
         out_specs=(

time: 1200 us -> 342 us (0.28)
  waiting for transfers between devices: 693 us -> 0 us
  Pallas kernels: 0 us -> 331 us
  blocking collectives: 267 us -> 0 us
  matrix products: 107 us -> 0 us
  local copies, waits for them, and re-layouts: 58.6 us -> 5.73 us
  other arithmetic: 36 us -> 1.92 us
  between operations: 16.5 us -> 0.93 us
  starting transfers between devices: 13.5 us -> 0 us
    pallas_call x0 -> x3, Pallas kernels: none -> 331 us  [the longest x1 200 us: layer_back(): pl.pallas_call(layer_back_body, out_shape=(shaped(128, 1536), shaped(128,...]
    reduce_scatter x4 -> x0, waiting for transfers between devices: 309 us -> none  [the longest x1 122 us: shards(): lax.psum_scatter(qkv_grad_term.astype(jnp.bfloat16), 'shard', scatter_dim...]
    psum x1 -> x0, waiting for transfers between devices: 213 us -> none  [shards(): lax.psum(owned[1].astype(jnp.bfloat16), 'replica').astype(jnp.float32)]
    all_gather x6 -> x0, waiting for transfers between devices: 169 us -> none  [the longest x1 99.8 us: shards(): all_acts = lax.all_gather(acts_second, 'shard', axis=0, tiled=True)]
    unnamed x2 -> x0, blocking collectives: 145 us -> none
    dot_general x20 -> x0, matrix products: 105 us -> none  [the longest x3 24.4 us: column_term(): jnp.einsum('lf,ld->fd', left_side, right_side, preferred_element_type=jnp...]
    all_gather x1 -> x0, blocking collectives: 63.1 us -> none  [shards(): lax.all_gather(b_qkv, 'shard', axis=0, tiled=True)]
    all_to_all x2 -> x0, blocking collectives: 53.5 us -> none  [to_rows(): part = lax.all_to_all(part, 'shard', 0, 0, tiled=True)]
  transfers between devices with their start and end apart: 13 -> 0, of which waited for: 8 -> 0; matrix products, arithmetic and copies ran while one was open for 13% -> 0% of each run, Pallas kernels for 0% -> 0%
where the time goes in v5:
time: 342 us; the launch traced here: 339 us
  Pallas kernels  331 us (97%)
  local copies, waits for them, and re-layouts  5.73 us (2%)
    pallas_call x1, Pallas kernels, layer_back(): pl.pallas_call(layer_back_body, out_shape=(shaped(128, 1536), shaped(128,...  200 us
    pallas_call x1, Pallas kernels, gather_weights(): pl.pallas_call(gather_body, out_shape=(shaped(1536, 2048), shaped(1536, 1...  118 us
    pallas_call x1, Pallas kernels, widen(): pl.pallas_call(widen_body, grid=(4,), out_shape=(shaped(192, 8960, dtype=...  12.5 us

profile of v5, /device:TPU:0, one launch (start us, length us, event | category | flops | bytes accessed | tf_op | source)
XLA Modules:
  0.0 339.4 jit_solution(9276182866711238871)
XLA Ops:
  0.6 1.2 broadcast_in_dim.15.ga_ref
  1.9 1.2 broadcast_in_dim.16.bq_ref
  3.1 1.2 broadcast_in_dim.17.gf_ref
  4.3 118.0 %gather_and_attend.1 = (bf16[1536,2048]{1,0:T(8,128)(2,1)}, bf16[1536,1536]{1,0:T(8,128)(2,1)}, bf16[1536,2304]{1,0:T(8,128)(2,1)}, bf16[1024,1536]{1,0:T(8,128)...) custom-call(bf16[128,1536]{1,0:T(8,128)(2,1)} %bitcast.10, ...), custom_call_target="tpu_custom_call" | custom-call | tf_op jit(solution)/shard_map/gather_and_attend/pallas_call | solution.py:645
  122.3 200.3 %layer_back.1 = (bf16[128,1536]{1,0:T(8,128)(2,1)}, bf16[128,1536]{1,0:T(8,128)(2,1)}, bf16[4,8,48,2304]{3,2,1,0:T(8,128)(2,1)}, bf16[4,1152,384]{2,1,0:T(8,128)...) custom-call(bf16[128,1536]{1,0:T(8,128)(2,1)} %get-tuple-element.36.n_ref, ...), custom_call_target="tpu_custom_call" | custom-call | tf_op jit(solution)/shard_map/layer_back/pallas_call | solution.py:1317
  322.6 1.2 bitcast_convert_fusion.1
  323.9 0.7 bitcast_convert_fusion
  324.5 0.6 fusion
  325.1 0.0 copy-start.1
  325.1 0.0 copy-start
  325.1 12.5 %widen.1 = (f32[192,8960]{1,0:T(8,128)}, f32[192,8960]{1,0:T(8,128)}, f32[1120,1536]{1,0:T(8,128)}, f32[192,2048]{1,0:T(8,128)}, f32[192,1536]{1,0:T(8,128)}) custom-call(bf16[4,8,48,2304]{3,2,1,0:T(8,128)(2,1)} %get-tuple-element.54.g_ref, bf16[4,1152,384]{2,1,0:T(8,128)(2,1)} %get-tuple-element.55.d_ref, bf16[4,48,2176]{2,1,0:T(8,128)(2,1)} %get-tuple-element.53.q_ref, ...), custom_call_target="tpu_custom_call" | custom-call | tf_op jit(solution)/shard_map/widen/pallas_call | solution.py:1352
  337.6 0.0 copy-done.1
  337.6 0.7 copy.23
  338.4 0.0 copy-done
  338.4 0.7 copy.24
Async XLA Ops:
  325.1 12.5 %copy-start.1 = (bf16[128,1536]{1,0:T(8,128)(2,1)S(1)}, bf16[128,1536]{1,0:T(8,128)(2,1)}, u32[]{:S(2)}) copy-start(bf16[128,1536]{1,0:T(8,128)(2,1)} %get-tuple-element.51) | copy-start | bytes 1179652
  325.1 13.2 %copy-start = (bf16[128,1536]{1,0:T(8,128)(2,1)S(1)}, bf16[128,1536]{1,0:T(8,128)(2,1)}, u32[]{:S(2)}) copy-start(bf16[128,1536]{1,0:T(8,128)(2,1)} %get-tuple-element.52) | copy-start | bytes 1179652

commit v6 on v5

--- a/solution.py
+++ b/solution.py
@@ -431,7 +431,8 @@
     p.greet(range(1, 8))
     gap = jnp.zeros((1, 64), F32)
     small = jnp.concatenate(
-        [ga_ref[...].astype(F32), gap, bq_ref[...].astype(F32), gf_ref[...].astype(F32), gap], axis=1
+        [ga_ref[...].astype(F32)[None], gap, bq_ref[...].astype(F32)[None], gf_ref[...].astype(F32)[None], gap],
+        axis=1,
     )
     S[s] = jnp.broadcast_to(small, (16, 768)).astype(BF)
 
@@ -587,8 +588,8 @@
         scores = jnp.where(open_to[None], scores, -1e30)
         ex = jnp.exp(scores - jnp.max(scores, axis=-1, keepdims=True))
         soft = (ex / jnp.sum(ex, axis=-1, keepdims=True)).reshape(768, 128)
-        probs[g] = soft
-        out = dot(soft.astype(BF), values[g]).astype(BF)
+        probs[g] = soft.astype(BF)
+        out = dot(probs[g], values[g]).astype(BF)
         for i in range(6):
             att[:, pl.ds(128 * (6 * g + i), 128)] = out[128 * i : 128 * i + 128]
 
@@ -646,7 +647,7 @@
         gather_body,
         out_shape=(
             shaped(1536, 2048), shaped(1536, 1536), shaped(1536, 2304), shaped(1024, 1536), shaped(128, 128, dtype=F32),
-            shaped(128, 128, dtype=F32), shaped(8, 1536, dtype=F32), shaped(2, 768, 128), shaped(2, 128, 128), shaped(2, 128, 128), shaped(2, 768, 128, dtype=F32),
+            shaped(128, 128, dtype=F32), shaped(8, 1536, dtype=F32), shaped(2, 768, 128), shaped(2, 128, 128), shaped(2, 128, 128), shaped(2, 768, 128),
             shaped(128, 1536), shaped(128, 1536), shaped(128, 1536, dtype=F32), shaped(128, 1536),
         ),
         in_specs=[VMEM] * 5 + [HBM] * 5,
@@ -765,12 +766,12 @@
 
 
 def layer_back_body(
-    n_ref, c_hbm, g_hbm, d_hbm, wq_hbm, wo_hbm, att_hbm, a1_hbm, x_hbm, cot_hbm,
-    mid_ref, gains, cos_ref, sin_ref, queries, keys, values, probs,
+    n_ref, c_hbm, g_hbm, d_hbm, wq_hbm, wo_hbm, att_hbm, a1_hbm, x_hbm, cot_hbm, q_hbm,
+    mid_ref, gains, cos_ref, sin_ref, keys, values, probs,
     out_ref, gtok_ref, OG, OD, OWq, OWo,
-    NC, H, vG, vD, MX, PD, PO, YD, ZD, YO, ZO, RCd, RXd, RC, RX, dmid, dA, dj, AT, SM,
+    NC, H, vG, vD, MX, PD, PO, YD, ZD, YO, ZO, YB, ZB, RCd, RXd, RC, RX, dj, AT, SM,
     Yq, Zq, RXq, RCo, Yo, Zo, RXo,
-    free, rn, syn, szn, ryd, rzd, syd, szd, syo, ryo, szo, rzo,
+    free, rn, syn, szn, ryd, rzd, syd, szd, syo, ryo, szo, rzo, syb, ryb, szb, rzb,
     scd, rcd, sxd, rxd, sfd, rfd, scg, rcg, sx, rx, sa, ra, sf, *sems,
 ):
     p = Place()
@@ -826,11 +827,39 @@
     def step_d(k):
         line_step(PD, YD, ZD, ryd, szd, rzd, k)
 
-    def side_o(k):
-        side(PO, YO, syo, ryo, k)
-
-    def step_o(k):
-        line_step(PO, YO, ZO, ryo, szo, rzo, k)
+    def side_oa(k):
+        zz = p.line(k)
+        send(PO.at[p.theirs(zz), :, 0:768], YO.at[zz], syo.at[zz], ryo.at[zz], p.side)
+
+    def step_oa(k):
+        zz = p.line(k)
+        half = PO.at[p.mine(zz), :, 0:768]
+
+        def add(ref, sem):
+            p.arrived(ref, sem, spare)
+            half[...] = (half[...].astype(F32) + ref[...].astype(F32)).astype(BF)
+
+        add(YO.at[zz], ryo.at[zz])
+        p.reduce_step(
+            zz,
+            lambda slot: add(ZO.at[slot], rzo.at[slot]),
+            lambda slot, device: send(half, ZO.at[slot], szo.at[zz], rzo.at[slot], device),
+        )
+
+    def step_ob(k):
+        zz = p.line(k)
+        both = PO.at[pl.ds(2 * zz, 2), :, 768:1536]
+
+        def add(slot):
+            p.arrived(ZB.at[slot], rzb.at[slot], spare)
+            both[...] = (both[...].astype(F32) + ZB[slot].astype(F32)).astype(BF)
+
+        p.reduce_step(
+            zz, add, lambda slot, device: send(both, ZB.at[slot], szb.at[zz], rzb.at[slot], device)
+        )
+
+    def side_ob():
+        send(PO.at[p.theirs(z), :, 768:1536], YB, syb, ryb, p.side)
 
     at_end = (z == 0) | (z == 3)
     in_middle = (z == 1) | (z == 2)
@@ -868,6 +897,8 @@
             part = dot(MX[rows], vD[:, co]).astype(BF)
             PO[2 * zz, :, co] = part[:128]
             PO[2 * zz + 1, :, co] = part[128:]
+        pl.when(at_end & (k == 1))(lambda: step_ob(1))
+        pl.when(at_end & (k == 2))(lambda: step_ob(2))
 
     side_d(2)
     side_d(0)
@@ -918,6 +949,8 @@
         pltpu.make_async_copy(a1_hbm, NC.at[1664:1792], loc.at[4]),
         pltpu.make_async_copy(x_hbm, NC.at[1792:1920], loc.at[5]),
         pltpu.make_async_copy(cot_hbm, NC.at[1920:2048], loc.at[6]),
+        pltpu.make_async_copy(q_hbm.at[0], MX.at[0:768, 256:384], loc.at[8]),
+        pltpu.make_async_copy(q_hbm.at[1], MX.at[0:768, 384:512], loc.at[9]),
     )
 
     def down_terms():
@@ -1006,14 +1039,13 @@
         kept["ffn"] = jnp.sum(dn * unit, axis=0, keepdims=True)
         e = dn * gains[1:2, :]
         dm = NC[1920:2048].astype(F32) + rstd * (e - unit * jnp.mean(e * unit, axis=-1, keepdims=True))
-        dmid[...] = dm
         NC[1920:2048] = dm.astype(BF)
         AT[...] = NC[1536:1664].T
         for j in range(3):
             part = dot_nt(NC[1920:2048], NC[pl.ds(512 * j, 512)]).astype(BF)
             for i in range(4):
                 h = 4 * j + i
-                dA[h // 6, pl.ds(128 * (h % 6), 128), :] = part[:, 128 * i : 128 * i + 128]
+                MX[pl.ds(128 * (h % 6), 128), pl.ds(128 * (h // 6), 128)] = part[:, 128 * i : 128 * i + 128]
         for j in range(3):
             co = pl.ds(512 * j, 512)
             NC[0:1536, co] = dot(AT[...], NC[1920:2048, co]).astype(BF)
@@ -1023,12 +1055,14 @@
             o_sums.to_core(o_sums.own(k))
 
     def heads(g):
-        grad, soft = dA[g], probs[g]
+        grad = MX[0:768, 128 * g : 128 * g + 128]
+        query = MX[0:768, 256 + 128 * g : 384 + 128 * g]
+        soft = probs[g].astype(F32)
         d_probs = dot_nt(grad, values[g])
         d_scores = (soft * (d_probs - jnp.sum(soft * d_probs, axis=-1, keepdims=True))).astype(BF)
-        d_values = dot(soft.astype(BF).T, grad)
+        d_values = dot(probs[g].T, grad)
         d_queries = dot(d_scores, keys[g]) * HEAD_DIMENSION**-0.5
-        d_keys = dot(d_scores.T, queries[g])
+        d_keys = dot(d_scores.T, query)
         for i in range(6):
             dj[:, pl.ds(128 * (6 * g + i), 128)] = back(d_queries[128 * i : 128 * i + 128]).astype(BF)
         dj[:, pl.ds(128 * (12 + g), 128)] = back(d_keys).astype(BF)
@@ -1047,7 +1081,7 @@
         gain_attn_grad = jnp.sum(dn1 * unit, axis=0, keepdims=True)
         e = dn1 * gains[0:1, :]
         NC[1792:1920] = (
-            dmid[...] + rstd * (e - unit * jnp.mean(e * unit, axis=-1, keepdims=True))
+            NC[1920:2048].astype(F32) + rstd * (e - unit * jnp.mean(e * unit, axis=-1, keepdims=True))
         ).astype(BF)
         pltpu.make_async_copy(NC.at[1792:1920], gtok_ref, loc.at[5]).start()
         SM[...] = jnp.zeros_like(SM)
@@ -1081,6 +1115,8 @@
             sums.on_chip(k)
 
     def finish_out():
+        p.arrived(YB, ryb, spare)
+        PO[s, :, 768:1536] = (PO[s, :, 768:1536].astype(F32) + YB[...].astype(F32)).astype(BF)
         PO[s] = (PO[s].astype(F32) + mid_ref[...]).astype(BF)
         pltpu.make_async_copy(PO.at[s], out_ref, loc.at[6]).start()
 
@@ -1094,183 +1130,194 @@
         on_chip(q_sums)
 
 
+    @pl.when(at_end)
+    def _():
+        step_d(3)
+        side_oa(3)
+        step_d(2)
+        side_oa(2)
+        side_oa(0)
+        step_d(1)
+        pair_whole(3)
+
+
     @pl.when(in_middle)
     def _():
-        side_o(3)
-        side_o(1)
-
-    step_d(3)
-    down_terms()
-
-    @pl.when(at_end)
-    def _():
-        side_o(3)
-        side_o(1)
+        side_oa(2)
+        side_oa(0)
+        step_ob(2)
+        step_d(3)
         step_d(2)
         step_d(1)
         pair_whole(6)
-        step_o(3)
-        pair_whole(7)
+
+    down_terms()
+
+    @pl.when(at_end)
+    def _():
+        step_ob(3)
+        pair_whole(6)
+        down_across(1)
         pair_whole(5)
+        step_oa(3)
+        pair_whole(0)
+        down_across(0)
+        side_oa(1)
 
 
     @pl.when(in_middle)
     def _():
-        step_d(2)
-        step_d(1)
-        pair_whole(6)
-        pair_whole(7)
+        side_oa(3)
         pair_whole(5)
         down_across(0)
-
-    pair_whole(1)
-    down_across(1)
+        side_oa(1)
+        pair_whole(3)
+        take(3)
+        pair_whole(1)
+        down_across(1)
+        pair_whole(2)
+
     step_d(0)
     attention_out()
-    down_across(2)
+
+    @pl.when(at_end)
+    def _():
+        down_across(2)
+
+    first_heads()
+    attention_in()
 
     @pl.when(at_end)
     def _():
         pair_whole(4)
-        pair_whole(3)
-
-    o_on_chip()
-
-    @pl.when(at_end)
-    def _():
-        down_across(0)
-        o_sums.aside(1)
-        take(1)
-        o_sums.aside(0)
-        o_sums.aside(2)
-
-
-    @pl.when(in_middle)
-    def _():
-        o_sums.aside(1)
-        take(1)
-        o_sums.aside(0)
-        o_sums.aside(2)
-        pair_whole(0)
-        take(7)
-        take(6)
-
-    first_heads()
-    take(5)
-    pair_whole(2)
-
-    @pl.when(at_end)
-    def _():
-        pair_whole(0)
-        take(6)
-
-
-    @pl.when(in_middle)
-    def _():
-        down_whole(1)
-
-    attention_in()
+        pair_whole(2)
+
     joined_terms()
-
-    @pl.when(at_end)
-    def _():
-        o_sums.aside(3)
-
 
     @pl.when(in_middle)
     def _():
         pair_whole(4)
-        o_sums.aside(3)
-        pair_whole(3)
-
-    down_whole(0)
-    relay(5)
+
+    o_on_chip()
+
+    @pl.when(at_end)
+    def _():
+        o_sums.aside(2)
+        take(3)
+        o_sums.aside(0)
+        pair_whole(1)
+        take(6)
+
+
+    @pl.when(in_middle)
+    def _():
+        down_across(2)
+        o_sums.aside(2)
+        pair_whole(7)
+        down_whole(0)
+        o_sums.aside(0)
+        step_oa(3)
+        pair_whole(0)
+        take(7)
+
     q_on_chip()
 
     @pl.when(at_end)
     def _():
         q_sums.aside(0)
+        take(2)
+        q_sums.aside(1)
+        down_whole(1)
+        take(5)
+        down_whole(0)
+        pair_whole(7)
         o_sums.on_line(0)
+        down_whole(2)
+        take(1)
+        q_sums.aside(2)
+        take(7)
+        q_sums.on_line(0)
+        o_sums.aside(1)
         take(4)
-        q_sums.aside(1)
+        relay(5)
+        q_sums.aside(3)
+        q_sums.on_line(1)
+        q_sums.on_line(2)
+        step_ob(0)
+        take(0)
         o_sums.on_line(1)
-        take(0)
-        take(7)
-        o_sums.on_line(2)
-        q_sums.on_line(0)
-        q_sums.aside(2)
-        side_o(2)
-        down_whole(1)
-        take(3)
-        down_whole(2)
-        q_sums.aside(3)
-        relay(4)
-        take(2)
-        q_sums.on_line(1)
-        relay(6)
-        down_relay(0)
-        q_sums.on_line(2)
-        o_sums.on_line(3)
-        relay(0)
-        side_o(0)
-        relay(2)
-        down_relay(1)
-        relay(3)
-        o_sums.at_owner()
-        step_o(2)
-        relay(7)
-        relay(1)
-        step_o(1)
+        o_sums.aside(3)
         q_sums.on_line(3)
         q_sums.at_owner()
-        step_o(0)
+        o_sums.on_line(2)
+        relay(2)
+        relay(3)
+        step_oa(2)
+        relay(4)
+        o_sums.on_line(3)
+        o_sums.at_owner()
+        q_sums.spread()
+        step_oa(1)
+        down_relay(2)
+        down_relay(0)
+        relay(1)
+        relay(6)
+        relay(7)
+        relay(0)
+        side_ob()
+        down_relay(1)
+        step_oa(0)
         finish_out()
-        down_relay(2)
         o_sums.spread()
-        q_sums.spread()
 
 
     @pl.when(in_middle)
     def _():
+        q_sums.aside(1)
+        q_sums.aside(0)
         take(4)
-        q_sums.aside(1)
-        step_o(3)
+        take(6)
+        down_whole(1)
+        take(5)
+        relay(3)
+        step_ob(3)
+        take(2)
+        take(1)
+        q_sums.aside(2)
         o_sums.on_line(0)
+        q_sums.aside(3)
+        o_sums.aside(1)
+        down_whole(2)
+        step_ob(1)
+        q_sums.on_line(0)
+        relay(5)
+        o_sums.aside(3)
+        q_sums.on_line(1)
+        q_sums.on_line(2)
+        step_ob(0)
         take(0)
+        q_sums.on_line(3)
+        q_sums.at_owner()
+        relay(4)
+        o_sums.on_line(2)
+        side_ob()
+        relay(2)
         o_sums.on_line(1)
-        q_sums.aside(0)
-        o_sums.on_line(2)
-        q_sums.aside(2)
-        down_whole(2)
-        q_sums.aside(3)
-        q_sums.on_line(0)
-        take(2)
-        q_sums.on_line(1)
         relay(6)
-        relay(2)
-        side_o(2)
+        o_sums.on_line(3)
+        o_sums.at_owner()
+        relay(0)
+        step_oa(1)
+        down_relay(1)
+        down_relay(2)
+        relay(7)
         down_relay(0)
-        o_sums.on_line(3)
-        down_relay(1)
-        o_sums.at_owner()
-        take(3)
-        relay(4)
-        q_sums.on_line(2)
-        down_relay(2)
+        q_sums.spread()
+        relay(1)
+        step_oa(2)
         o_sums.spread()
-        q_sums.on_line(3)
-        relay(1)
-        step_o(1)
-        relay(0)
-        relay(3)
-        side_o(0)
-        q_sums.at_owner()
-        step_o(2)
-        q_sums.spread()
-        relay(7)
-        step_o(0)
+        step_oa(0)
         finish_out()
-
 
     o_sums.finish()
     q_sums.finish()
@@ -1311,6 +1358,9 @@
         def _():
             p.sent(ZD.at[i], szd.at[i], spare)
             p.sent(ZO.at[i], szo.at[i], spare)
+            p.sent(ZB.at[i], szb.at[i], spare)
+
+    p.sent(YB, syb, spare)
 
 
 def layer_back(*args):
@@ -1320,58 +1370,78 @@
             shaped(128, 1536), shaped(128, 1536), shaped(4, 8, 48, 2304), shaped(4, 1152, 384), shaped(4, 48, 2176),
             shaped(4, 48, 1536),
         ),
-        in_specs=[HBM] * 10 + [VMEM] * 8,
+        in_specs=[HBM] * 11 + [VMEM] * 7,
         out_specs=(HBM,) * 6,
         scratch_shapes=[
             low(2048, 1536), low(1536, 2304), low(1536, 2304), low(1152, 1536), low(1024, 1152),
-            low(8, 128, 1536), low(8, 128, 1536), low(4, 128, 1536), low(5, 128, 1536), low(4, 128, 1536), low(5, 128, 1536),
+            low(8, 128, 1536), low(8, 128, 1536), low(4, 128, 1536), low(5, 128, 1536), low(4, 128, 768), low(5, 128, 768),
+            low(128, 768), low(5, 2, 128, 768),
             low(2, 1152, 384), low(1152, 384), low(8, 2, 48, 2304), low(8, 48, 2304),
-            full(128, 1536), low(2, 768, 128), low(128, 2048), low(1536, 128), full(8, 16, 128),
+            low(128, 2048), low(1536, 128), full(8, 16, 128),
             *RowSums.buffers(2176)[1:], *RowSums.buffers(1536),
             pltpu.SemaphoreType.REGULAR, DMA((8,)), DMA((4,)), DMA((4, 2)),
-            DMA((4,)), DMA((5,)), DMA((4,)), DMA((4,)), DMA((4,)), DMA((4,)), DMA((4,)), DMA((5,)),
+            DMA((4,)), DMA((5,)), DMA((4,)), DMA((4,)), DMA((4,)), DMA((4,)), DMA((4,)), DMA((5,)), DMA, DMA, DMA((4,)), DMA((5,)),
             DMA((3, 2)), DMA((3, 2)), DMA((3,)), DMA((3,)), DMA((3, 4)), DMA((3, 4)),
             DMA((8, 2)), DMA((8, 2)), DMA((8,)), DMA((8,)), DMA((8,)), DMA((8, 4)), DMA((8, 3)),
-            *RowSums.semaphores(), *RowSums.semaphores(), DMA((8,)),
+            *RowSums.semaphores(), *RowSums.semaphores(), DMA((10,)),
         ],
         compiler_params=pltpu.CompilerParams(collective_id=1, has_side_effects=True, vmem_limit_bytes=64 << 20),
         name="layer_back",
     )(*args)
 
 
-def widen_body(g_ref, d_ref, q_ref, o_ref, gate, up, down, qkv, out):
-    for t in range(8):
-        gate[:, 1120 * t : 1120 * t + 1120] = g_ref[0, t, :, 0:1120].astype(F32)
-        up[:, 1120 * t : 1120 * t + 1120] = g_ref[0, t, :, 1152:2272].astype(F32)
+def widen_body(
+    g_ref, d_ref, q_ref, o_ref, x_ref, y_ref, gate, up, down, qkv, out, x_out, y_out, ga, bq, gf, narrow
+):
+    for first, wide in ((0, gate), (1152, up)):
+        for t in range(8):
+            narrow[:, 1120 * t : 1120 * t + 1120] = g_ref[0, t, :, first : first + 1120]
+        wide[...] = narrow[...].astype(F32)
     down[...] = d_ref[0, 0:1120, :].astype(F32)
     qkv[...] = q_ref[0, :, 0:2048].astype(F32)
     out[...] = o_ref[0].astype(F32)
-
-
-def widen(g, d, q, o):
+    x_out[...] = x_ref[...]
+    y_out[...] = y_ref[...]
+
+    @pl.when(pl.program_id(0) == 0)
+    def _():
+        small = q_ref[0, 0:16, 2048:2176].astype(F32)
+        ga[...] = jnp.concatenate([small[0:1], small[1:2, 0:64]], axis=1)[0]
+        bq[...] = jnp.concatenate([small[2:3], small[3:4]], axis=1)[0]
+        gf[...] = jnp.concatenate([small[4:5], small[5:6, 0:64]], axis=1)[0]
+
+
+def widen(g, d, q, o, x, y):
+    def rows(size, width):
+        return pl.BlockSpec((size, width), lambda i: (i, 0))
+
+    def whole(size):
+        return pl.BlockSpec((size,), lambda i: (0,))
+
     return pl.pallas_call(
         widen_body,
         grid=(4,),
         out_shape=(
             shaped(192, 8960, dtype=F32), shaped(192, 8960, dtype=F32), shaped(1120, 1536, dtype=F32),
-            shaped(192, 2048, dtype=F32), shaped(192, 1536, dtype=F32),
+            shaped(192, 2048, dtype=F32), shaped(192, 1536, dtype=F32), shaped(128, 1536), shaped(128, 1536),
+            shaped(192, dtype=F32), shaped(256, dtype=F32), shaped(192, dtype=F32),
         ),
         in_specs=[
             pl.BlockSpec((1, 8, 48, 2304), lambda i: (i, 0, 0, 0)),
             pl.BlockSpec((1, 1152, 384), lambda i: (i, 0, 0)),
             pl.BlockSpec((1, 48, 2176), lambda i: (i, 0, 0)),
             pl.BlockSpec((1, 48, 1536), lambda i: (i, 0, 0)),
+            rows(32, 1536),
+            rows(32, 1536),
         ],
         out_specs=(
-            pl.BlockSpec((48, 8960), lambda i: (i, 0)),
-            pl.BlockSpec((48, 8960), lambda i: (i, 0)),
-            pl.BlockSpec((1120, 384), lambda i: (0, i)),
-            pl.BlockSpec((48, 2048), lambda i: (i, 0)),
-            pl.BlockSpec((48, 1536), lambda i: (i, 0)),
+            rows(48, 8960), rows(48, 8960), pl.BlockSpec((1120, 384), lambda i: (0, i)), rows(48, 2048), rows(48, 1536),
+            rows(32, 1536), rows(32, 1536), whole(192), whole(256), whole(192),
         ),
+        scratch_shapes=[low(48, 8960)],
         compiler_params=pltpu.CompilerParams(vmem_limit_bytes=62 << 20),
         name="widen",
-    )(g, d, q, o)
+    )(g, d, q, o, x, y)
 
 
 def shards_eight(
@@ -1379,16 +1449,13 @@
 ):
     x, cot = tokens[0], cotangent[0]
     WQ, WO, G, C, cosine, sine, gains, queries, keys, values, probs, att, a1, mid, a2 = gather_weights(
-        x, segments, gain_attn[None], b_qkv[None], gain_ffn[None], w_qkv, w_out, w_gate, w_up, cot
+        x, segments, gain_attn, b_qkv, gain_ffn, w_qkv, w_out, w_gate, w_up, cot
     )
     out, grad_tokens, gate_up, down, qkv, o = layer_back(
-        a2, C, G, w_down, WQ, WO, att, a1, x, cot, mid, gains, cosine, sine, queries, keys, values, probs
-    )
-    gate, up, down, qkv_rows, out_rows = widen(gate_up, down, qkv, o)
-    small = qkv[0, 0:6, 2048:].astype(F32).reshape(768)
-    return (
-        out[None], grad_tokens[None], small[0:192], qkv_rows, small[256:512], out_rows, small[512:704], gate, up, down,
-    )
+        a2, C, G, w_down, WQ, WO, att, a1, x, cot, queries, mid, gains, cosine, sine, keys, values, probs
+    )
+    gate, up, down, qkv_rows, out_rows, out, grad_tokens, ga, bq, gf = widen(gate_up, down, qkv, o, out, grad_tokens)
+    return out[None], grad_tokens[None], ga, qkv_rows, bq, out_rows, gf, gate, up, down
 
 
 def solution(mesh):

time: 342 us -> 329 us (0.962)
  local copies, waits for them, and re-layouts: 5.73 us -> 0 us
  Pallas kernels: 331 us -> 326 us
    pallas_call x1, Pallas kernels: 200 us -> 195 us  [layer_back(): pl.pallas_call(layer_back_body, out_shape=(shaped(128, 1536), shaped(128,...]
    broadcast_in_dim x3 -> x0, local copies, waits for them, and re-layouts: 3.66 us -> none  [the longest x1 1.22 us: shards_eight(): gain_attn[None]]
where the time goes in v6:
time: 329 us; the launch traced here: 327 us
  Pallas kernels  326 us (99%)
    pallas_call x1, Pallas kernels, layer_back(): pl.pallas_call(layer_back_body, out_shape=(shaped(128, 1536), shaped(128,...  195 us
    pallas_call x1, Pallas kernels, gather_weights(): pl.pallas_call(gather_body, out_shape=(shaped(1536, 2048), shaped(1536, 1...  118 us
    pallas_call x1, Pallas kernels, widen(): pl.pallas_call(widen_body, grid=(4,), out_shape=(shaped(192, 8960, dtype=...  13.5 us

profile of v6, /device:TPU:0, one launch (start us, length us, event | category | flops | bytes accessed | tf_op | source)
XLA Modules:
  0.0 326.8 jit_solution(14867395939659838310)
XLA Ops:
  0.6 117.9 %gather_and_attend.1 = (bf16[1536,2048]{1,0:T(8,128)(2,1)}, bf16[1536,1536]{1,0:T(8,128)(2,1)}, bf16[1536,2304]{1,0:T(8,128)(2,1)}, bf16[1024,1536]{1,0:T(8,128)...) custom-call(bf16[128,1536]{1,0:T(8,128)(2,1)} %bitcast.4, ...), custom_call_target="tpu_custom_call" | custom-call | tf_op jit(solution)/shard_map/gather_and_attend/pallas_call | solution.py:646
  118.5 194.5 %layer_back.1 = (bf16[128,1536]{1,0:T(8,128)(2,1)}, bf16[128,1536]{1,0:T(8,128)(2,1)}, bf16[4,8,48,2304]{3,2,1,0:T(8,128)(2,1)}, bf16[4,1152,384]{2,1,0:T(8,128)...) custom-call(bf16[128,1536]{1,0:T(8,128)(2,1)} %get-tuple-element.41.n_ref, ...), custom_call_target="tpu_custom_call" | custom-call | tf_op jit(solution)/shard_map/layer_back/pallas_call | solution.py:1367
  313.1 13.5 %widen.1 = (f32[192,8960]{1,0:T(8,128)}, f32[192,8960]{1,0:T(8,128)}, f32[1120,1536]{1,0:T(8,128)}, f32[192,2048]{1,0:T(8,128)}, f32[192,1536]{1,0:T(8,128)}, /*...) custom-call(bf16[4,8,48,2304]{3,2,1,0:T(8,128)(2,1)} %get-tuple-element.56.g_r, ...), custom_call_target="tpu_custom_call" | custom-call | tf_op jit(solution)/shard_map/widen/pallas_call | solution.py:1421
